TPU v7x, 32 devices: a whole 2x2x4 slice. The times are simulated.
32 devices in a mesh: dp: 8 (over y, x, core), et: 4 (over z).
Axes of the slice: x: 2, y: 2, z: 4, core: 2. Of those that a mesh axis runs over, the one named last changes fastest.
Arguments:
- out_grad: bfloat16 [4096, 4096], P(('dp', 'et')), may hold values from -6 to 6
- routes: int32 [4096, 2], P(('dp', 'et')), may hold values from 0 to 7, as said below
- gates: float32 [4096, 2], P(('dp', 'et')), may hold values from 0.05 to 1
- lengths: int32 [32, 8], P(('dp', 'et')), may hold values from 1 to 48, 128 in all within a row
- saved_gate: bfloat16 [8, 128, 16384], P('dp', None, 'et'), may hold values from -6 to 6
- saved_up: bfloat16 [8, 128, 16384], P('dp', None, 'et'), may hold values from -6 to 6
- w_gate: bfloat16 [4096, 16384], P('dp', 'et'), may hold values from -0.09375 to 0.09375
- w_up: bfloat16 [4096, 16384], P('dp', 'et'), may hold values from -0.09375 to 0.09375
- w_down: bfloat16 [16384, 4096], P('et', 'dp'), may hold values from -0.046875 to 0.046875
Outputs:
- input_grad: bfloat16 [4096, 4096], P(('dp', 'et'))
Inputs may be any that keep to these rules, and one draw needn't show every extreme that they name: `routes`: the two ids of a row differ. In each block of 128 rows (one device's tokens) at most 32 rows name expert 0, and in every draw some block has exactly 32 of them.
All inputs are finite; a program needn't handle non-finite values.
Results may differ from a plain program's by a relative error of at most 0.0095.
Values may be sent and summed in bfloat16 or wider, within the bound.
No kernel may reach another device: no remote copies, remote signals or barrier semaphores. Data moves between devices by JAX's collectives and lax.ppermute only.
A program may use at most 256 MiB of HBM per device.

v0:
```python
import jax
import jax.numpy as jnp
from jax import lax
from jax.sharding import PartitionSpec as P


def swiglu_grads(upstream, gate_pre, up_pre):
    gate_value = gate_pre.astype(jnp.float32)
    up_value = up_pre.astype(jnp.float32)
    sigmoid_gate = jax.nn.sigmoid(gate_value)
    slope = sigmoid_gate * (1.0 + gate_value * (1.0 - sigmoid_gate))
    grad_gate = (upstream * up_value * slope).astype(jnp.bfloat16)
    grad_up = (upstream * gate_value * sigmoid_gate).astype(jnp.bfloat16)
    return (grad_gate, grad_up)


def contract_last(left, right):
    return lax.dot_general(
        left, right, (((1,), (1,)), ((), ())), preferred_element_type=jnp.float32
    )


def round_trip(values):
    return lax.optimization_barrier(values.astype(jnp.bfloat16)).astype(jnp.float32)


def per_device(out_grad, routes, gates, lengths, saved_gate, saved_up, w_gate, w_up, w_down):
    tok_rows = out_grad.shape[0]
    group_size = lax.axis_size("et")
    slots = saved_gate.shape[1] // group_size
    hit_zero = routes == 0
    weight_zero = jnp.sum(jnp.where(hit_zero, gates, 0.0), axis=1)
    chosen = jnp.any(hit_zero, axis=1)
    doc_len = lengths[0]
    ends = jnp.cumsum(doc_len)
    starts = ends - doc_len
    position = jnp.arange(tok_rows, dtype=jnp.int32)
    inside = (position[:, None] >= starts[None, :]) & (position[:, None] < ends[None, :])
    mean_len = tok_rows / doc_len.shape[0]
    factor = jnp.sum(
        jnp.where(inside, mean_len / doc_len.astype(jnp.float32)[None, :], 0.0), axis=1
    )
    scaled = (out_grad.astype(jnp.float32) * (weight_zero * factor)[:, None]).astype(jnp.bfloat16)
    slot_of = jnp.cumsum(chosen.astype(jnp.int32)) - 1
    placing = (
        (slot_of[None, :] == jnp.arange(slots, dtype=jnp.int32)[:, None]) & chosen[None, :]
    ).astype(jnp.bfloat16)
    packed = jnp.dot(placing, scaled, preferred_element_type=jnp.float32).astype(jnp.bfloat16)
    gate_saved = saved_gate[0]
    up_saved = saved_up[0]
    gathered = lax.all_gather(packed, "et", axis=0, tiled=True)
    upstream = contract_last(gathered, lax.all_gather(w_down, "dp", axis=1, tiled=True))
    grad_gate, grad_up = swiglu_grads(upstream, gate_saved, up_saved)
    stacked = jnp.stack((w_gate, w_up))
    piece = lax.all_gather(stacked, "dp", axis=1, tiled=True)
    terms = round_trip(contract_last(grad_gate, piece[0]) + contract_last(grad_up, piece[1]))
    summed = lax.psum_scatter(terms.astype(jnp.bfloat16), "et", scatter_dimension=0, tiled=True)
    input_grad = lax.dot_general(
        placing, summed, (((0,), (0,)), ((), ())), preferred_element_type=jnp.float32
    )
    return input_grad.astype(jnp.bfloat16)


def solution(mesh):
    in_specs = (
        P(("dp", "et"), None),
        P(("dp", "et"), None),
        P(("dp", "et"), None),
        P(("dp", "et"), None),
        P("dp", None, "et"),
        P("dp", None, "et"),
        P("dp", "et"),
        P("dp", "et"),
        P("et", "dp"),
    )
    out_specs = P(("dp", "et"), None)
    return jax.shard_map(
        per_device, mesh=mesh, in_specs=in_specs, out_specs=out_specs, check_vma=False
    )
```

profile of v0, /device:TPU:0, one launch (start us, length us, event | category | flops | bytes accessed | tf_op | source)
XLA Modules:
  0.0 587.5 jit_solution(6419602870144856387)
XLA Ops:
  6.5 0.0 all-gather.4.cloned.1.call-start
  6.5 0.7 fusion.30
  7.2 0.7 divide_bitcast_fusion
  7.9 0.8 reduce-window.14
  8.7 0.7 fusion.29
  9.4 0.7 select_reduce_fusion.1
  10.1 0.1 copy.12
  10.2 0.2 reduce-window.13
  10.4 0.1 add_reduce_fusion
  10.5 0.1 select_reduce_fusion
  10.6 2.3 convolution_convert_fusion.1
  12.9 0.0 all-gather.4.cloned.1.call-update
  12.9 0.0 all-gather.6.cloned.1.call-start
  13.0 0.7 all-gather.6.cloned.1.call-update
  13.7 0.0 all-gather.8.cloned.1.call-start
  13.7 7.5 %pad_maximum_fusion = bf16[2,512,4096]{2,1,0:T(8,128)(2,1)} fusion(bf16[1,512,4096]{2,1,0:T(8,128)(2,1)} %bitcast.43, bf16[1,512,4096]{2,1,0:T(8,128)(2,1)} %bitcast.44), kind=kLoop, calls=%fused_computation.4 | loop fusion | flops 4194304 | bytes 16777216 | tf_op jit(solution)/shard_map/stack | solution.py:54
  21.3 0.0 all-gather.8.cloned.1.call-update
  21.3 0.0 copy-start
  21.3 0.0 reduce-scatter.2.cloned.1.call-start
  21.3 22.4 %all-gather.4.cloned.1.call-done = bf16[128,4096]{1,0:T(8,128)(2,1)} async-done(((bf16[32,4096]{1,0:T(8,128)(2,1)}), bf16[128,4096]{1,0:T(8,128)(2,1)}) %all-gather.4.cloned.1.call-update) | async-done | bytes 1048592 | tf_op jit(solution)/shard_map/all_gather | solution.py:51
  43.7 168.8 %all-gather.6.cloned.1.call-done = bf16[4096,4096]{1,0:T(8,128)(2,1)} async-done(((bf16[4096,512]{1,0:T(8,128)(2,1)}), bf16[4096,4096]{1,0:T(8,128)(2,1)}) %all-gather.6.cloned.1.call-update) | async-done | bytes 33554448 | tf_op jit(solution)/shard_map/all_gather | solution.py:52
  212.5 19.7 %fusion.33 = f32[128,4096]{1,0:T(8,128)S(1)} fusion(bf16[128,4096]{1,0:T(8,128)(2,1)} %all-gather.4.cloned.1.call-done, bf16[4096,4096]{1,0:T(8,128)(2,1)} %all-gather.6.cloned.1.call-done), kind=kOutput, calls=%fused_computation.49 | convolution fusion | flops 4294967296 | bytes 36700160 | tf_op jit(solution)/shard_map/dot_general | solution.py:18
  232.3 285.0 %all-gather.8.cloned.1.call-done = bf16[2,4096,4096]{2,1,0:T(8,128)(2,1)} async-done(((bf16[2,512,4096]{2,1,0:T(8,128)(2,1)}), bf16[2,4096,4096]{2,1,0:T(8,128)(2,1)}) %all-gather.8.cloned.1.call-update) | async-done | bytes 67108880 | tf_op jit(solution)/shard_map/all_gather | solution.py:55
  517.3 0.0 copy-done
  517.3 16.9 %fusion = f32[128,4096]{1,0:T(8,128)} fusion(bf16[2,4096,4096]{2,1,0:T(8,128)(2,1)} %all-gather.8.cloned.1.call-done, f32[128,4096]{1,0:T(8,128)S(1)} %fusion.33, bf16[1,128,4096]{2,1,0:T(8,128)(2,1)S(1)} %copy-done), kind=kOutput, calls=%fused_computation.1 | convolution fusion | flops 4298637312 | bytes 38797312 | tf_op jit(solution)/shard_map/dot_general | solution.py:18
  534.3 17.0 %fusion.3 = bf16[128,4096]{1,0:T(8,128)(2,1)} fusion(f32[128,4096]{1,0:T(8,128)} %fusion, bf16[2,4096,4096]{2,1,0:T(8,128)(2,1)} %all-gather.8.cloned.1.call-done, f32[128,4096]{1,0:T(8,128)S(1)} %fusion.33, bf16[1,128,4096]{2,1,0:T(8,128)(2,1)} %param.14, bf16[1,128,4096]{2,1,0:T(8,128)(2,1)S(1)} %copy-done), kind=kOutput, calls=%fused_computation.6 | convolution fusion | flops 4302307328 | bytes 40894464 | tf_op jit(solution)/shard_map/dot_general | solution.py:18
  551.3 0.0 reduce-scatter.2.cloned.1.call-update
  551.3 27.3 %reduce-scatter.2.cloned.1.call-done = bf16[32,4096]{1,0:T(8,128)(2,1)} async-done(((bf16[128,4096]{1,0:T(8,128)(2,1)}), bf16[32,4096]{1,0:T(8,128)(2,1)}) %reduce-scatter.2.cloned.1.call-update) | async-done | bytes 262160 | tf_op jit(solution)/shard_map/reduce_scatter | solution.py:57
  578.6 2.4 convolution_convert_fusion
  (2 shorter events, 0.0 us)
Async XLA Ops:
  6.5 37.2 %all-gather.4.cloned.1.call-start = ((), (), s32[]{:S(2)}) async-start(), calls=%async_computation.1 | async-start | bytes 1310720 | tf_op jit(solution)/shard_map/all_gather | solution.py:51
  12.9 199.6 %all-gather.6.cloned.1.call-start = ((), (), s32[]{:S(2)}) async-start(), calls=%async_computation.2 | async-start | bytes 37748736 | tf_op jit(solution)/shard_map/all_gather | solution.py:52
  13.7 503.6 %all-gather.8.cloned.1.call-start = ((), (), s32[]{:S(2)}) async-start(), calls=%async_computation.3 | async-start | bytes 75497472 | tf_op jit(solution)/shard_map/all_gather | solution.py:55
  21.3 496.0 %copy-start = (bf16[1,128,4096]{2,1,0:T(8,128)(2,1)S(1)}, bf16[1,128,4096]{2,1,0:T(8,128)(2,1)}, u32[]{:S(2)}) copy-start(bf16[1,128,4096]{2,1,0:T(8,128)(2,1)} %param.13) | copy-start | bytes 3145732
  21.3 557.3 %reduce-scatter.2.cloned.1.call-start = ((), (), s32[]{:S(2)}) async-start(), calls=%async_computation.4 | async-start | bytes 1310720 | tf_op jit(solution)/shard_map/reduce_scatter | solution.py:57
Sparse Core Ops, SparseCore 0:
  13.0 30.6 all-gather.3
  45.6 166.9 all-gather.5
  214.4 302.8 all-gather.7
  551.4 27.1 reduce-scatter.1
where the time goes:
time: 588 us
  waiting for transfers between devices  504 us (86%)
  matrix products  58.4 us (10%)
  between operations  13.2 us (2%)
  other arithmetic  11.5 us (2%)
    all_gather x1, waiting for transfers between devices, per_device(): piece = lax.all_gather(stacked, 'dp', axis=1, tiled=True)  285 us
    all_gather x1, waiting for transfers between devices, per_device(): lax.all_gather(w_down, 'dp', axis=1, tiled=True)  169 us
    dot_general x3, matrix products, contract_last(): lax.dot_general(left, right, (((1,), (1,)), ((), ())), preferred_element_...  53.7 us
    reduce_scatter x1, waiting for transfers between devices, per_device(): lax.psum_scatter(terms.astype(jnp.bfloat16), 'et', scatter_dimension=0, t...  27.3 us
    all_gather x1, waiting for transfers between devices, per_device(): gathered = lax.all_gather(packed, 'et', axis=0, tiled=True)  22.4 us
  transfers between devices with their start and end apart: 4, of which 4 were waited for; matrix products, arithmetic and copies ran while one was open for 5% of the time, Pallas kernels for 0%

commit v1 on v0

--- a/solution.py
+++ b/solution.py
@@ -15,19 +15,14 @@
 
 
 def contract_last(left, right):
+    axis = left.ndim - 1
     return lax.dot_general(
-        left, right, (((1,), (1,)), ((), ())), preferred_element_type=jnp.float32
+        left, right, (((axis,), (1,)), ((), ())), preferred_element_type=jnp.float32
     )
 
 
-def round_trip(values):
-    return lax.optimization_barrier(values.astype(jnp.bfloat16)).astype(jnp.float32)
-
-
-def per_device(out_grad, routes, gates, lengths, saved_gate, saved_up, w_gate, w_up, w_down):
-    tok_rows = out_grad.shape[0]
-    group_size = lax.axis_size("et")
-    slots = saved_gate.shape[1] // group_size
+def place_rows(routes, gates, lengths, slots):
+    tok_rows = routes.shape[0]
     hit_zero = routes == 0
     weight_zero = jnp.sum(jnp.where(hit_zero, gates, 0.0), axis=1)
     chosen = jnp.any(hit_zero, axis=1)
@@ -40,21 +35,34 @@
     factor = jnp.sum(
         jnp.where(inside, mean_len / doc_len.astype(jnp.float32)[None, :], 0.0), axis=1
     )
-    scaled = (out_grad.astype(jnp.float32) * (weight_zero * factor)[:, None]).astype(jnp.bfloat16)
     slot_of = jnp.cumsum(chosen.astype(jnp.int32)) - 1
     placing = (
         (slot_of[None, :] == jnp.arange(slots, dtype=jnp.int32)[:, None]) & chosen[None, :]
     ).astype(jnp.bfloat16)
+    return placing, weight_zero * factor
+
+
+def per_device(out_grad, routes, gates, lengths, saved_gate, saved_up, w_gate, w_up, w_down):
+    group_size = lax.axis_size("et")
+    groups = lax.axis_size("dp")
+    group_rows = saved_gate.shape[1]
+    slots = group_rows // group_size
+    width = w_gate.shape[0]
+    placing, coef = place_rows(routes, gates, lengths, slots)
+    scaled = (out_grad.astype(jnp.float32) * coef[:, None]).astype(jnp.bfloat16)
     packed = jnp.dot(placing, scaled, preferred_element_type=jnp.float32).astype(jnp.bfloat16)
-    gate_saved = saved_gate[0]
-    up_saved = saved_up[0]
-    gathered = lax.all_gather(packed, "et", axis=0, tiled=True)
-    upstream = contract_last(gathered, lax.all_gather(w_down, "dp", axis=1, tiled=True))
-    grad_gate, grad_up = swiglu_grads(upstream, gate_saved, up_saved)
-    stacked = jnp.stack((w_gate, w_up))
-    piece = lax.all_gather(stacked, "dp", axis=1, tiled=True)
-    terms = round_trip(contract_last(grad_gate, piece[0]) + contract_last(grad_up, piece[1]))
-    summed = lax.psum_scatter(terms.astype(jnp.bfloat16), "et", scatter_dimension=0, tiled=True)
+    rows = lax.all_to_all(packed.reshape(slots, groups, width), "dp", split_axis=1, concat_axis=0)
+    rows = rows.reshape(groups, slots, width)
+    rows = lax.all_gather(rows, "et", axis=1)
+    partial_up = contract_last(rows.reshape(groups * group_rows, width), w_down).astype(jnp.bfloat16)
+    upstream = lax.psum_scatter(partial_up, "dp", scatter_dimension=0, tiled=True).astype(jnp.float32)
+    grads = jnp.stack(swiglu_grads(upstream, saved_gate[0], saved_up[0]))
+    grads = lax.all_gather(grads, "dp", axis=0)
+    terms = contract_last(grads[:, 0], w_gate) + contract_last(grads[:, 1], w_up)
+    terms = terms.astype(jnp.bfloat16).reshape(groups, group_size, slots, width)
+    summed = lax.psum_scatter(terms, "et", scatter_dimension=1, tiled=False)
+    summed = lax.all_to_all(summed, "dp", split_axis=0, concat_axis=1)
+    summed = summed.reshape(slots, groups * width)
     input_grad = lax.dot_general(
         placing, summed, (((0,), (0,)), ((), ())), preferred_element_type=jnp.float32
     )

time: 588 us -> 292 us (0.50)
  waiting for transfers between devices: 504 us -> 215 us
  matrix products: 58.4 us -> 29.9 us
  blocking collectives: 0 us -> 22.6 us
    all_gather x3 -> x2, waiting for transfers between devices: 476 us -> 117 us  [the longest x1 89.8 us: per_device(): grads = lax.all_gather(grads, 'dp', axis=0)]
    reduce_scatter x1 -> x2, waiting for transfers between devices: 27.3 us -> 98.1 us  [the longest x1 70.9 us: per_device(): lax.psum_scatter(partial_up, 'dp', scatter_dimension=0, tiled=True)]
    dot_general x3, matrix products: 53.7 us -> 26.9 us  [contract_last(): lax.dot_general(left, right, (((axis,), (1,)), ((), ())), preferred_eleme...]
    all_to_all x0 -> x2, blocking collectives: none -> 22.6 us  [the longest x1 12 us: per_device(): lax.all_to_all(packed.reshape(slots, groups, width), 'dp', split_axis=1,...]
  transfers between devices with their start and end apart: 4 -> 4, of which waited for: 4 -> 4; matrix products, arithmetic and copies ran while one was open for 5% -> 0% of each run, Pallas kernels for 0% -> 0%
where the time goes in v1:
time: 292 us; the launch traced here: 291 us
  waiting for transfers between devices  215 us (74%)
  matrix products  29.9 us (10%)
  blocking collectives  22.6 us (8%)
  between operations  13.2 us (5%)
  other arithmetic  7.84 us (3%)
    all_gather x1, waiting for transfers between devices, per_device(): grads = lax.all_gather(grads, 'dp', axis=0)  89.8 us
    reduce_scatter x1, waiting for transfers between devices, per_device(): lax.psum_scatter(partial_up, 'dp', scatter_dimension=0, tiled=True)  70.9 us
    all_gather x1, waiting for transfers between devices, per_device(): rows = lax.all_gather(rows, 'et', axis=1)  27.4 us
    reduce_scatter x1, waiting for transfers between devices, per_device(): summed = lax.psum_scatter(terms, 'et', scatter_dimension=1, tiled=False)  27.3 us
    dot_general x3, matrix products, contract_last(): lax.dot_general(left, right, (((axis,), (1,)), ((), ())), preferred_eleme...  26.9 us
    all_to_all x1, blocking collectives, per_device(): lax.all_to_all(packed.reshape(slots, groups, width), 'dp', split_axis=1,...  12 us
    all_to_all x1, blocking collectives, per_device(): summed = lax.all_to_all(summed, 'dp', split_axis=0, concat_axis=1)  10.6 us
  transfers between devices with their start and end apart: 4, of which 4 were waited for; matrix products, arithmetic and copies ran while one was open for 0% of the time, Pallas kernels for 0%

profile of v1, /device:TPU:0, one launch (start us, length us, event | category | flops | bytes accessed | tf_op | source)
XLA Modules:
  0.0 291.2 jit_solution(6110540363830168574)
XLA Ops:
  6.5 0.0 all-gather.5.cloned.1.call-start
  6.5 0.7 fusion.27
  7.2 0.7 divide_bitcast_fusion
  7.9 0.8 reduce-window.14
  8.7 0.7 fusion.26
  9.4 0.7 select_reduce_fusion.1
  10.1 0.1 copy.28
  10.2 0.2 reduce-window.13
  10.4 0.1 add_reduce_fusion
  10.5 0.1 select_reduce_fusion
  10.6 1.6 convolution_convert_fusion.2
  12.2 0.1 copy.36
  12.3 0.1 copy.29
  12.4 12.0 %all_to_all.30 = bf16[1,32,8,512]{3,1,0,2:T(8,128)(2,1)} all-to-all(bf16[1,32,8,512]{3,1,0,2:T(8,128)(2,1)S(1)} %copy.29), channel_id=1, replica_groups=mesh['dp'=8,'et'=4] {'dp'}, dimensions={2} | all-to-all | bytes 524288 | tf_op jit(solution)/shard_map/all_to_all | solution.py:54
  24.4 0.0 all-gather.5.cloned.1.call-update
  24.4 0.0 reduce-scatter.3.cloned.1.call-start
  24.5 27.4 %all-gather.5.cloned.1.call-done = bf16[8,4,32,1,512]{4,2,1,0,3:T(8,128)(2,1)} async-done(((bf16[8,1,32,1,512]{4,2,1,0,3:T(8,128)(2,1)}), bf16[8,4,32,1,512]{4,2,1,0,3:T(8,128)(2,1)}) %all-gather.5.cloned.1.call-update) | async-done | bytes 1048592 | tf_op jit(solution)/shard_map/all_gather | solution.py:56
  51.9 10.3 %convolution_convert_fusion = bf16[1024,4096]{1,0:T(8,128)(2,1)} fusion(bf16[1024,512]{1,0:T(8,128)(2,1)} %bitcast.81, bf16[4096,512]{1,0:T(8,128)(2,1)} %param.17), kind=kOutput, calls=%fused_computation.4 | convolution fusion | flops 4299161600 | bytes 13631488 | tf_op jit(solution)/shard_map/dot_general | solution.py:19
  62.1 0.0 copy-start
  62.1 0.0 copy-start.1
  62.2 0.0 reduce-scatter.3.cloned.1.call-update
  62.2 0.0 all-gather.7.cloned.1.call-start
  62.2 70.9 %reduce-scatter.3.cloned.1.call-done = bf16[128,4096]{1,0:T(8,128)(2,1)} async-done(((bf16[1024,4096]{1,0:T(8,128)(2,1)}), bf16[128,4096]{1,0:T(8,128)(2,1)}) %reduce-scatter.3.cloned.1.call-update) | async-done | bytes 1048592 | tf_op jit(solution)/shard_map/reduce_scatter | solution.py:58
  133.1 0.0 copy-done
  133.1 0.0 copy-done.1
  133.1 2.4 fusion.17
  135.5 1.5 pad_maximum_fusion
  137.0 0.0 all-gather.7.cloned.1.call-update
  137.0 0.2 reduce-scatter.5.cloned.1.call-start
  137.3 89.8 %all-gather.7.cloned.1.call-done = bf16[16,128,4096]{2,1,0:T(8,128)(2,1)} async-done(((bf16[2,128,4096]{2,1,0:T(8,128)(2,1)}), bf16[16,128,4096]{2,1,0:T(8,128)(2,1)}) %all-gather.7.cloned.1.call-update) | async-done | bytes 16777232 | tf_op jit(solution)/shard_map/all_gather | solution.py:60
  227.0 0.0 copy-start.2
  227.0 0.0 copy-start.3
  227.0 10.6 %fusion = f32[8,128,512]{2,1,0:T(8,128)} fusion(bf16[8,2,128,4096]{3,2,1,0:T(8,128)(2,1)} %bitcast.79, bf16[512,4096]{1,0:T(8,128)(2,1)} %param.16), kind=kOutput, calls=%fused_computation.1 | convolution fusion | flops 4294967296 | bytes 14680064 | tf_op jit(solution)/shard_map/dot_general | solution.py:19
  237.6 0.0 copy-done.2
  237.6 0.7 copy-done.3
  238.3 6.0 %add_convert_fusion = bf16[8,128,512]{2,1,0:T(8,128)(2,1)S(1)} fusion(f32[8,128,512]{2,1,0:T(8,128)} %fusion, bf16[512,4096]{1,0:T(8,128)(2,1)S(1)} %copy-done.3, bf16[8,2,128,4096]{3,2,1,0:T(8,128)(2,1)S(1)} %bitcast.80), kind=kOutput, calls=%fused_computation.23 | convolution fusion | flops 4296015872 | bytes 15728640 | tf_op jit(solution)/shard_map/dot_general | solution.py:19
  244.3 1.0 copy.32
  245.3 0.0 reduce-scatter.5.cloned.1.call-update
  245.3 27.3 %reduce-scatter.5.cloned.1.call-done = bf16[8,1,32,512]{3,2,0,1:T(8,128)(2,1)} async-done(((bf16[8,4,32,512]{3,2,0,1:T(8,128)(2,1)}), bf16[8,1,32,512]{3,2,0,1:T(8,128)(2,1)}) %reduce-scatter.5.cloned.1.call-update) | async-done | bytes 262160 | tf_op jit(solution)/shard_map/reduce_scatter | solution.py:63
  272.6 10.6 %all_to_all.31 = bf16[8,32,1,512]{3,1,2,0:T(8,128)(2,1)S(1)} all-to-all(bf16[8,32,1,512]{3,1,2,0:T(8,128)(2,1)} %bitcast.77), channel_id=1, replica_groups=mesh['dp'=8,'et'=4] {'dp'}, dimensions={0} | all-to-all | bytes 524288 | tf_op jit(solution)/shard_map/all_to_all | solution.py:64
  283.2 1.5 convolution_convert_fusion.1
  (3 shorter events, 0.0 us)
Async XLA Ops:
  6.5 45.3 %all-gather.5.cloned.1.call-start = ((), (), s32[]{:S(2)}) async-start(), calls=%async_computation.6 | async-start | bytes 1310720 | tf_op jit(solution)/shard_map/all_gather | solution.py:56
  24.4 108.7 %reduce-scatter.3.cloned.1.call-start = ((), (), s32[]{:S(2)}) async-start(), calls=%async_computation.4 | async-start | bytes 9437184 | tf_op jit(solution)/shard_map/reduce_scatter | solution.py:58
  62.1 70.9 %copy-start = (bf16[1,128,4096]{2,1,0:T(8,128)(2,1)S(1)}, bf16[1,128,4096]{2,1,0:T(8,128)(2,1)}, u32[]{:S(2)}) copy-start(bf16[1,128,4096]{2,1,0:T(8,128)(2,1)} %param.13) | copy-start | bytes 3145732
  62.1 70.9 %copy-start.1 = (bf16[1,128,4096]{2,1,0:T(8,128)(2,1)S(1)}, bf16[1,128,4096]{2,1,0:T(8,128)(2,1)}, u32[]{:S(2)}) copy-start(bf16[1,128,4096]{2,1,0:T(8,128)(2,1)} %param.14) | copy-start | bytes 3145732
  62.2 164.8 %all-gather.7.cloned.1.call-start = ((), (), s32[]{:S(2)}) async-start(), calls=%async_computation.7 | async-start | bytes 18874368 | tf_op jit(solution)/shard_map/all_gather | solution.py:60
  137.0 135.6 %reduce-scatter.5.cloned.1.call-start = ((), (), s32[]{:S(2)}) async-start(), calls=%async_computation.5 | async-start | bytes 1310720 | tf_op jit(solution)/shard_map/reduce_scatter | solution.py:63
  227.0 10.6 %copy-start.2 = (bf16[16,128,4096]{2,1,0:T(8,128)(2,1)S(1)}, bf16[16,128,4096]{2,1,0:T(8,128)(2,1)}, u32[]{:S(2)}) copy-start(bf16[16,128,4096]{2,1,0:T(8,128)(2,1)} %all-gather.7.cloned.1.call-done) | copy-start | bytes 50331652
  227.0 11.2 %copy-start.3 = (bf16[512,4096]{1,0:T(8,128)(2,1)S(1)}, bf16[512,4096]{1,0:T(8,128)(2,1)}, u32[]{:S(2)}) copy-start(bf16[512,4096]{1,0:T(8,128)(2,1)} %param.15) | copy-start | bytes 12582916
Sparse Core Ops, SparseCore 0:
  24.5 27.2 all-gather.4
  62.3 70.7 reduce-scatter.2
  137.1 89.8 all-gather.6
  245.5 27.1 reduce-scatter.4

commit v2 on v1

--- a/solution.py
+++ b/solution.py
@@ -42,7 +42,7 @@
     return placing, weight_zero * factor
 
 
-def per_device(out_grad, routes, gates, lengths, saved_gate, saved_up, w_gate, w_up, w_down):
+def plain_exchange(out_grad, routes, gates, lengths, saved_gate, saved_up, w_gate, w_up, w_down):
     group_size = lax.axis_size("et")
     groups = lax.axis_size("dp")
     group_rows = saved_gate.shape[1]
@@ -69,6 +69,123 @@
     return input_grad.astype(jnp.bfloat16)
 
 
+def swap(values, axis, offset):
+    size = lax.axis_size(axis)
+    return lax.ppermute(values, axis, [(i, i ^ offset) for i in range(size)])
+
+
+def scatter_sum(values, bits):
+    for bit in bits:
+        keep = [m for m in sorted(values) if not m & bit]
+        sent = jnp.concatenate([values[m | bit] for m in keep], axis=0).astype(jnp.bfloat16)
+        got = swap(sent, "dp", bit)
+        rows = got.shape[0] // len(keep)
+        values = {
+            m: values[m].astype(jnp.float32) + got[i * rows : (i + 1) * rows].astype(jnp.float32)
+            for i, m in enumerate(keep)
+        }
+    return values[0]
+
+
+def gather_blocks(block, bits):
+    order = [0]
+    for bit in bits:
+        block = jnp.concatenate([block, swap(block, "dp", bit)], axis=0)
+        order = order + [m | bit for m in order]
+    return block, order
+
+
+def per_device(out_grad, routes, gates, lengths, saved_gate, saved_up, w_gate, w_up, w_down):
+    planes = lax.axis_size("et")
+    groups = lax.axis_size("dp")
+    group_rows = saved_gate.shape[1]
+    slots = group_rows // planes
+    width, hidden = w_gate.shape
+    half = hidden // 2
+    quarter = half // 2
+    me = lax.axis_index("dp")
+    plane = lax.axis_index("et")
+    core = me % 2
+    mine, other = core * half, (1 - core) * half
+    chip_bits = [1 << b for b in range(1, groups.bit_length() - 1)]
+    orders = (chip_bits, chip_bits[::-1])
+    chips = [2 * m for m in range(groups // 2)]
+
+    placing, coef = place_rows(routes, gates, lengths, slots)
+    scaled = (out_grad.astype(jnp.float32) * coef[:, None]).astype(jnp.bfloat16)
+    packed = jnp.dot(placing, scaled, preferred_element_type=jnp.float32).astype(jnp.bfloat16)
+    rows = lax.all_to_all(packed.reshape(slots, groups, width), "dp", split_axis=1, concat_axis=0)
+    rows = rows.reshape(groups, slots, width)
+    rows = jnp.take(rows, me ^ jnp.arange(groups), axis=0).reshape(groups * slots, width)
+
+    down = jnp.concatenate(
+        [
+            lax.dynamic_slice_in_dim(w_down, mine, half, 0),
+            swap(lax.dynamic_slice_in_dim(w_down, other, half, 0), "dp", 1),
+        ],
+        axis=1,
+    )
+    saved = jnp.stack([saved_gate[0], saved_up[0]])
+    saved = jnp.stack(
+        [
+            lax.dynamic_slice_in_dim(saved, mine, half, 2),
+            swap(lax.dynamic_slice_in_dim(saved, other, half, 2), "dp", 1),
+        ],
+        axis=1,
+    ).reshape(2, 2, planes, slots, half)
+
+    def hidden_part(weight, start):
+        return lax.dynamic_slice_in_dim(weight, start, half, 1)
+
+    ups = jnp.concatenate([hidden_part(w_gate, mine), hidden_part(w_up, mine)], axis=1)
+    ups_sent = jnp.concatenate([hidden_part(w_gate, other), hidden_part(w_up, other)], axis=1)
+    ups = jnp.concatenate([ups, swap(ups_sent, "dp", 1)], axis=0).reshape(2 * width, 2, 2, quarter)
+
+    offsets = [0] + [s for s in range(2, planes)] + [1]
+    total = None
+    for offset in offsets:
+        here = rows if offset == 0 else swap(rows, "et", offset)
+        flipped = here.reshape(groups // 2, 2, slots, width)[:, ::-1].reshape(here.shape)
+        here = jnp.concatenate([here, swap(flipped, "dp", 1)], axis=1)
+        there = jnp.arange(2)
+        saved_here = lax.dynamic_index_in_dim(saved, plane ^ offset, 2, keepdims=False)
+        terms = None
+        for part, bits in enumerate(orders):
+            columns = slice(part * quarter, (part + 1) * quarter)
+            partial_up = contract_last(here, down[columns]).astype(jnp.bfloat16)
+            partial_up = partial_up.reshape(groups // 2, 2 * slots, quarter)
+            upstream = scatter_sum({m: partial_up[m // 2] for m in chips}, bits)
+            grads = jnp.concatenate(
+                swiglu_grads(
+                    upstream,
+                    saved_here[0, :, :, columns].reshape(2 * slots, quarter),
+                    saved_here[1, :, :, columns].reshape(2 * slots, quarter),
+                ),
+                axis=1,
+            )
+            grads, order = gather_blocks(grads, bits[::-1])
+            grads = grads.reshape(groups // 2, 2 * slots, 2 * quarter)
+            grads = jnp.stack([grads[order.index(m)] for m in chips])
+            part_terms = contract_last(grads, ups[:, :, part].reshape(2 * width, 2 * quarter))
+            terms = part_terms if terms is None else terms + part_terms
+        terms = terms.reshape(groups // 2, 2, slots, 2, width)
+        sent = terms[:, ::-1, :, 1].astype(jnp.bfloat16)
+        terms = terms[:, :, :, 0] + swap(sent, "dp", 1).astype(jnp.float32)
+        terms = terms.astype(jnp.bfloat16)
+        if offset:
+            terms = swap(terms, "et", offset)
+        terms = terms.astype(jnp.float32)
+        total = terms if total is None else total + terms
+    summed = total.astype(jnp.bfloat16).reshape(groups, slots, width)
+    summed = jnp.take(summed, me ^ jnp.arange(groups), axis=0)
+    summed = lax.all_to_all(summed, "dp", split_axis=0, concat_axis=1)
+    summed = summed.reshape(slots, groups * width)
+    input_grad = lax.dot_general(
+        placing, summed, (((0,), (0,)), ((), ())), preferred_element_type=jnp.float32
+    )
+    return input_grad.astype(jnp.bfloat16)
+
+
 def solution(mesh):
     in_specs = (
         P(("dp", "et"), None),
@@ -82,6 +199,7 @@
         P("et", "dp"),
     )
     out_specs = P(("dp", "et"), None)
+    body = per_device if mesh.shape["dp"] == 8 else plain_exchange
     return jax.shard_map(
-        per_device, mesh=mesh, in_specs=in_specs, out_specs=out_specs, check_vma=False
-    )
+        body, mesh=mesh, in_specs=in_specs, out_specs=out_specs, check_vma=False
+    )

time: 292 us -> 362 us (1.24); the launches traced: 291 us -> 357 us
  local copies, waits for them, and re-layouts: 2 us -> 135 us
  waiting for transfers between devices: 215 us -> 100 us
  starting transfers between devices: 0.31 us -> 51.6 us
  other arithmetic: 7.84 us -> 32.5 us
  blocking collectives: 22.6 us -> 9.78 us
  between operations: 13.2 us -> 1.5 us
  matrix products: 29.9 us -> 26.2 us
    all_gather x2 -> x0, waiting for transfers between devices: 117 us -> none  [the longest x1 89.8 us: per_device(): grads = lax.all_gather(grads, 'dp', axis=0)]
    reduce_scatter x2 -> x0, waiting for transfers between devices: 98.1 us -> none  [the longest x1 70.9 us: per_device(): lax.psum_scatter(partial_up, 'dp', scatter_dimension=0, tiled=True)]
    ppermute x0 -> x49, waiting for transfers between devices: none -> 95.2 us  [swap(): return lax.ppermute(values, axis, [(i, i ^ offset) for i in range(size)])]
    slice x0 -> x29, local copies, waits for them, and re-layouts: none -> 71.1 us  [the longest x2 62.1 us: per_device(): ups[:, :, part].reshape(2 * width, 2 * quarter)]
    ppermute x0 -> x49, starting transfers between devices: none -> 46.8 us  [swap(): return lax.ppermute(values, axis, [(i, i ^ offset) for i in range(size)])]
    concatenate x0 -> x15, other arithmetic: none -> 22.7 us  [the longest x1 19.1 us: per_device(): jnp.concatenate([ups, swap(ups_sent, 'dp', 1)], axis=0)]
    reshape x1 -> x5, local copies, waits for them, and re-layouts: 1.04 us -> 19.3 us  [the longest x1 14.5 us: per_device(): jnp.concatenate([ups, swap(ups_sent, 'dp', 1)], axis=0)]
    another operation x0 -> x3, local copies, waits for them, and re-layouts: none -> 15.9 us  [the longest x2 15.8 us: per_device(): ups[:, :, part].reshape(2 * width, 2 * quarter)]
  transfers between devices with their start and end apart: 4 -> 50, of which waited for: 4 -> 27; matrix products, arithmetic and copies ran while one was open for 0% -> 13% of each run, Pallas kernels for 0% -> 0%
where the time goes in v2:
time: 362 us; the launch traced here: 357 us
  local copies, waits for them, and re-layouts  135 us (37%)
  waiting for transfers between devices  100 us (28%)
  starting transfers between devices  51.6 us (14%)
  other arithmetic  32.5 us (9%)
  matrix products  26.2 us (7%)
  blocking collectives  9.78 us (3%)
    ppermute x49, waiting for transfers between devices, swap(): return lax.ppermute(values, axis, [(i, i ^ offset) for i in range(size)])  95.2 us
    slice x2, local copies, waits for them, and re-layouts, per_device(): ups[:, :, part].reshape(2 * width, 2 * quarter)  62.1 us
    ppermute x49, starting transfers between devices, swap(): return lax.ppermute(values, axis, [(i, i ^ offset) for i in range(size)])  46.8 us
    dot_general x16, matrix products, contract_last(): lax.dot_general(left, right, (((axis,), (1,)), ((), ())), preferred_eleme...  24.3 us
    concatenate x1, other arithmetic, per_device(): jnp.concatenate([ups, swap(ups_sent, 'dp', 1)], axis=0)  19.1 us
    another operation x2, local copies, waits for them, and re-layouts, per_device(): ups[:, :, part].reshape(2 * width, 2 * quarter)  15.8 us
    reshape x1, local copies, waits for them, and re-layouts, per_device(): jnp.concatenate([ups, swap(ups_sent, 'dp', 1)], axis=0)  14.5 us
    all_to_all x1, blocking collectives, per_device(): summed = lax.all_to_all(summed, 'dp', split_axis=0, concat_axis=1)  9.78 us
  transfers between devices with their start and end apart: 50, of which 27 were waited for; matrix products, arithmetic and copies ran while one was open for 13% of the time, Pallas kernels for 0%

profile of v2, /device:TPU:0, one launch (start us, length us, event | category | flops | bytes accessed | tf_op | source)
XLA Modules:
  0.0 357.0 jit_solution(17944540354168231203)
XLA Ops:
  0.0 6.7 %constant_dynamic-slice_fusion.2 = (bf16[512,2048]{1,0:T(8,128)(2,1)}, bf16[512,2048]{1,0:T(8,128)(2,1)S(1)}, bf16[512,2048]{1,0:T(8,128)(2,1)S(1)}, bf16[512,2048]{1,0:T(8,128)(2,1)}) fusion(bf16[512,4096]{1,0:T(8,128)(2,1)} %param.18, s32[]{:T(128)S(6)} %select_n.50, s32[]{:T(128)S(6)} %select_n.51, bf16[512,4096]{1,0:T(8,128)(2,1)} %param.17), kind=kLoop, calls=%fused_computation.303 | loop fusion | bytes 16777224 | tf_op jit(solution)/shard_map/dynamic_slice | solution.py:138
  6.8 2.3 pad_maximum_fusion.1
  11.5 4.8 %all-to-all-start = ((bf16[1,32,8,512]{3,1,0,2:T(8,128)(2,1)}), bf16[1,32,8,512]{3,1,0,2:T(8,128)(2,1)S(1)}, u32[]{:S(2)}, u32[]{:S(2)}) async-start(bf16[1,32,8,512]{3,1,0,2:T(8,128)(2,1)} %copy.76), calls=%async_computation | async-start | bytes 524288 | tf_op jit(solution)/shard_map/all_to_all | solution.py:117
  18.2 5.1 %all-to-all-done = bf16[1,32,8,512]{3,1,0,2:T(8,128)(2,1)S(1)} async-done(((bf16[1,32,8,512]{3,1,0,2:T(8,128)(2,1)}), bf16[1,32,8,512]{3,1,0,2:T(8,128)(2,1)S(1)}, u32[]{:S(2)}, u32[]{:S(2)}) %all-to-all-start) | async-done | bytes 262176 | tf_op jit(solution)/shard_map/all_to_all | solution.py:117
  23.9 1.6 collective-permute-start.37
  25.6 2.5 collective-permute-start.25
  28.2 3.8 %constant_dynamic-slice_fusion.7 = (bf16[2048,512]{1,0:T(8,128)(2,1)S(1)}, bf16[2048,512]{1,0:T(8,128)(2,1)}) fusion(bf16[4096,512]{1,0:T(8,128)(2,1)} %param.19, s32[]{:T(128)S(6)} %select_n.50, s32[]{:T(128)S(6)} %select_n.51), kind=kLoop, calls=%fused_computation.308 | loop fusion | bytes 8388616 | tf_op jit(solution)/shard_map/dynamic_slice | solution.py:123
  32.7 1.7 rev.30
  34.4 6.7 %collective-permute-done.25 = bf16[256,512]{1,0:T(8,128)(2,1)} collective-permute-done((bf16[256,512]{1,0:T(8,128)(2,1)S(1)}, bf16[256,512]{1,0:T(8,128)(2,1)}, u32[]{:S(2)}, u32[]{:S(2)}) %collective-permute-start.25) | collective-permute-done | bytes 262176 | tf_op jit(solution)/shard_map/ppermute | solution.py:74
  41.1 1.7 rev.28
  42.8 7.7 %collective-permute-done.13 = bf16[256,512]{1,0:T(8,128)(2,1)} collective-permute-done((bf16[256,512]{1,0:T(8,128)(2,1)S(1)}, bf16[256,512]{1,0:T(8,128)(2,1)}, u32[]{:S(2)}, u32[]{:S(2)}) %collective-permute-start.13) | collective-permute-done | bytes 262176 | tf_op jit(solution)/shard_map/ppermute | solution.py:74
  50.5 1.7 rev.26
  57.9 1.4 fusion.63
  65.9 1.2 collective-permute-start.39
  67.1 1.7 collective-permute-start.31
  71.3 3.1 collective-permute-done.43
  76.3 3.7 %collective-permute-done.31 = bf16[128,1024]{1,0:T(8,128)(2,1)S(1)} collective-permute-done((bf16[128,1024]{1,0:T(8,128)(2,1)S(1)}, bf16[128,1024]{1,0:T(8,128)(2,1)S(1)}, u32[]{:S(2)}, u32[]{:S(2)}) %collective-permute-start.31) | collective-permute-done | bytes 262176 | tf_op jit(solution)/shard_map/ppermute | solution.py:74
  80.7 1.2 collective-permute-start.2
  81.9 3.7 %collective-permute-done.19 = bf16[128,1024]{1,0:T(8,128)(2,1)S(1)} collective-permute-done((bf16[128,1024]{1,0:T(8,128)(2,1)S(1)}, bf16[128,1024]{1,0:T(8,128)(2,1)S(1)}, u32[]{:S(2)}, u32[]{:S(2)}) %collective-permute-start.19) | collective-permute-done | bytes 262176 | tf_op jit(solution)/shard_map/ppermute | solution.py:74
  85.6 1.3 collective-permute-start.44
  87.8 3.4 collective-permute-done.8
  91.2 1.3 collective-permute-start.32
  93.5 1.3 collective-permute-done.44
  94.8 1.2 collective-permute-start.20
  96.1 1.7 collective-permute-start.16
  99.1 1.5 collective-permute-start.3
  100.9 1.2 collective-permute-start.45
  102.6 1.4 collective-permute-start.41
  108.7 1.5 collective-permute-done.45
  111.8 1.4 collective-permute-start.17
  113.3 2.6 collective-permute-done.33
  117.4 1.4 collective-permute-start.5
  118.9 2.5 collective-permute-done.21
  121.5 1.3 collective-permute-start.46
  124.3 2.8 collective-permute-done.10
  127.1 1.3 collective-permute-start.34
  128.7 1.2 collective-permute-start.30
  129.9 10.0 %collective-permute-done.46 = bf16[128,2048]{1,0:T(8,128)(2,1)S(1)} collective-permute-done((bf16[128,2048]{1,0:T(8,128)(2,1)S(1)}, bf16[128,2048]{1,0:T(8,128)(2,1)S(1)}, u32[]{:S(2)}, u32[]{:S(2)}) %collective-permute-start.46) | collective-permute-done | bytes 524320 | tf_op jit(solution)/shard_map/ppermute | solution.py:74
  139.9 1.4 collective-permute-start.22
  143.0 8.1 %collective-permute-done.34 = bf16[128,2048]{1,0:T(8,128)(2,1)S(1)} collective-permute-done((bf16[128,2048]{1,0:T(8,128)(2,1)S(1)}, bf16[128,2048]{1,0:T(8,128)(2,1)S(1)}, u32[]{:S(2)}, u32[]{:S(2)}) %collective-permute-start.34) | collective-permute-done | bytes 524320 | tf_op jit(solution)/shard_map/ppermute | solution.py:74
  151.1 1.4 collective-permute-start.11
  155.0 7.3 %collective-permute-done.22 = bf16[128,2048]{1,0:T(8,128)(2,1)S(1)} collective-permute-done((bf16[128,2048]{1,0:T(8,128)(2,1)S(1)}, bf16[128,2048]{1,0:T(8,128)(2,1)S(1)}, u32[]{:S(2)}, u32[]{:S(2)}) %collective-permute-start.22) | collective-permute-done | bytes 524320 | tf_op jit(solution)/shard_map/ppermute | solution.py:74
  164.1 7.3 %collective-permute-done.11 = bf16[128,2048]{1,0:T(8,128)(2,1)S(1)} collective-permute-done((bf16[128,2048]{1,0:T(8,128)(2,1)S(1)}, bf16[128,2048]{1,0:T(8,128)(2,1)S(1)}, u32[]{:S(2)}, u32[]{:S(2)}) %collective-permute-start.11) | collective-permute-done | bytes 524320 | tf_op jit(solution)/shard_map/ppermute | solution.py:74
  173.1 19.1 %pad_maximum_fusion = bf16[1024,4096]{1,0:T(8,128)(2,1)} fusion(bf16[512,4096]{1,0:T(8,128)(2,1)} %collective-permute-done.7, bf16[512,2048]{1,0:T(8,128)(2,1)S(1)} %copy-done.1, bf16[512,2048]{1,0:T(8,128)(2,1)S(1)} %copy-done.2), kind=kLoop, calls=%fused_computation.4 | loop fusion | flops 25165824 | bytes 16777216 | tf_op jit(solution)/shard_map/concatenate | solution.py:142
  192.1 14.5 %reshape.255 = bf16[1024,2,2,1024]{3,2,1,0:T(2,128)(2,1)} reshape(bf16[1024,4096]{1,0:T(8,128)(2,1)} %pad_maximum_fusion) | data formatting | bytes 16777216 | tf_op jit(solution)/shard_map/reshape | solution.py:142
  206.6 32.8 %slice_reduce_fusion = bf16[1024,2,1024]{2,1,0:T(2,128)(2,1)} fusion(bf16[1024,2,2,1024]{3,2,1,0:T(2,128)(2,1)} %reshape.255), kind=kLoop, calls=%fused_computation.2 | loop fusion | bytes 8388608 | tf_op jit(solution)/shard_map/slice | solution.py:169
  239.5 29.3 %slice_reduce_fusion.1 = bf16[1024,2,1024]{2,1,0:T(2,128)(2,1)} fusion(bf16[1024,2,2,1024]{3,2,1,0:T(2,128)(2,1)S(1)} %copy-done), kind=kLoop, calls=%fused_computation.3 | loop fusion | bytes 8388608 | tf_op jit(solution)/shard_map/slice | solution.py:169
  268.7 7.8 %reshape.307 = bf16[1024,2048,1]{1,0,2:T(8,128)(2,1)} reshape(bf16[1024,2,1024]{2,1,0:T(2,128)(2,1)} %slice_reduce_fusion) | data formatting | bytes 8388608 | tf_op jit(solution)/shard_map/reshape;squeeze | solution.py:169
  276.5 8.0 %reshape.306 = bf16[1024,2048,1]{1,0,2:T(8,128)(2,1)} reshape(bf16[1024,2,1024]{2,1,0:T(2,128)(2,1)} %slice_reduce_fusion.1) | data formatting | bytes 8388608 | tf_op jit(solution)/shard_map/reshape;squeeze | solution.py:169
  284.6 3.6 %fusion.53 = f32[4,64,1024]{2,1,0:T(8,128)S(1)} fusion(bf16[1024,2048,1]{1,0,2:T(8,128)(2,1)} %reshape.307, bf16[1,64,2048]{2,1,0:T(8,128)(2,1)S(1)} %get-tuple-element.75, bf16[1,64,2048]{2,1,0:T(8,128)(2,1)S(1)} %get-tuple-element.74, bf16[1,64,2048]{2,1,0:T(8,128)(2,1)S(1)} %bitcast.239, bf16[1,64,2048]{2,1,0:T(8,128)(2,1)S(1)} %get-tuple-element.90), kind=kOutput, calls=%fused_computation.85 | convolution fusion | flops 1075314688 | bytes 6291456 | tf_op jit(solution)/shard_map/dot_general | solution.py:19
  288.2 1.3 convolution_add_fusion
  291.9 3.6 %fusion.38 = f32[4,64,1024]{2,1,0:T(8,128)S(1)} fusion(bf16[1024,2048,1]{1,0,2:T(8,128)(2,1)} %reshape.307, bf16[1,64,2048]{2,1,0:T(8,128)(2,1)S(1)} %copy-done.33, bf16[1,64,2048]{2,1,0:T(8,128)(2,1)S(1)} %copy-done.32, bf16[1,64,2048]{2,1,0:T(8,128)(2,1)S(1)} %bitcast.241, bf16[1,64,2048]{2,1,0:T(8,128)(2,1)S(1)} %get-tuple-element.86), kind=kOutput, calls=%fused_computation.70 | convolution fusion | flops 1075314688 | bytes 6291456 | tf_op jit(solution)/shard_map/dot_general | solution.py:19
  295.5 1.3 convolution_add_fusion.1
  299.2 3.7 %fusion.23 = f32[4,64,1024]{2,1,0:T(8,128)S(1)} fusion(bf16[1024,2048,1]{1,0,2:T(8,128)(2,1)} %reshape.307, bf16[1,64,2048]{2,1,0:T(8,128)(2,1)S(1)} %copy-done.35, bf16[1,64,2048]{2,1,0:T(8,128)(2,1)S(1)} %copy-done.34, bf16[1,64,2048]{2,1,0:T(8,128)(2,1)S(1)} %bitcast.245, bf16[1,64,2048]{2,1,0:T(8,128)(2,1)S(1)} %copy-done.15), kind=kOutput, calls=%fused_computation.55 | convolution fusion | flops 1075314688 | bytes 6291456 | tf_op jit(solution)/shard_map/dot_general | solution.py:19
  302.9 2.2 convolution_add_fusion.2
  305.2 2.1 reshape.259
  310.3 1.4 fusion.8
  312.7 1.3 convolution_add_fusion.3
  317.8 2.7 collective-permute-start.36
  322.8 2.6 collective-permute-done.48
  325.4 6.8 %collective-permute-done.36 = bf16[4,2,32,512]{3,2,1,0:T(8,128)(2,1)S(1)} collective-permute-done((bf16[4,2,32,512]{3,2,1,0:T(8,128)(2,1)S(1)}, bf16[4,2,32,512]{3,2,1,0:T(8,128)(2,1)S(1)}, u32[]{:S(2)}, u32[]{:S(2)}) %collective-permute-start.36) | collective-permute-done | bytes 262176 | tf_op jit(solution)/shard_map/ppermute | solution.py:74
  332.3 12.3 %collective-permute-done.24 = bf16[4,2,32,512]{3,2,1,0:T(8,128)(2,1)S(1)} collective-permute-done((bf16[4,2,32,512]{3,2,1,0:T(8,128)(2,1)S(1)}, bf16[4,2,32,512]{3,2,1,0:T(8,128)(2,1)S(1)}, u32[]{:S(2)}, u32[]{:S(2)}) %collective-permute-start.24) | collective-permute-done | bytes 262176 | tf_op jit(solution)/shard_map/ppermute | solution.py:74
  345.5 9.8 %all_to_all.30 = bf16[8,32,1,512]{3,1,2,0:T(8,128)(2,1)S(1)} all-to-all(bf16[8,32,1,512]{3,1,2,0:T(8,128)(2,1)S(1)} %select_bitcast_fusion), channel_id=1, replica_groups=mesh['dp'=8,'et'=4] {'dp'}, dimensions={0} | all-to-all | bytes 524288 | tf_op jit(solution)/shard_map/all_to_all | solution.py:181
  355.3 1.5 convolution_convert_fusion
  (275 shorter events, 59.4 us)
Async XLA Ops:
  9.1 7.3 %copy-start.12 = (bf16[1,128,4096]{2,1,0:T(8,128)(2,1)S(1)}, bf16[1,128,4096]{2,1,0:T(8,128)(2,1)}, u32[]{:S(2)}) copy-start(bf16[1,128,4096]{2,1,0:T(8,128)(2,1)} %param.15) | copy-start | bytes 3145732
  9.1 164.0 %collective-permute-start.7 = (bf16[512,4096]{1,0:T(8,128)(2,1)}, bf16[512,4096]{1,0:T(8,128)(2,1)}, u32[]{:S(2)}, u32[]{:S(2)}) collective-permute-start(bf16[512,4096]{1,0:T(8,128)(2,1)} %pad_maximum_fusion.1), channel_id=1, source_target_pairs={{0,4},{4,0},{8,12},{12,8},{16,20},{20,16},{24,28},{28,24},{1,5},{5... | collective-permute-start | bytes 12582920 | tf_op jit(solution)/shard_map/ppermute | solution.py:74
  10.6 5.8 %copy-start.13 = (bf16[1,128,4096]{2,1,0:T(8,128)(2,1)S(1)}, bf16[1,128,4096]{2,1,0:T(8,128)(2,1)}, u32[]{:S(2)}) copy-start(bf16[1,128,4096]{2,1,0:T(8,128)(2,1)} %param.16) | copy-start | bytes 3145732
  11.5 11.8 %all-to-all-start = ((bf16[1,32,8,512]{3,1,0,2:T(8,128)(2,1)}), bf16[1,32,8,512]{3,1,0,2:T(8,128)(2,1)S(1)}, u32[]{:S(2)}, u32[]{:S(2)}) async-start(bf16[1,32,8,512]{3,1,0,2:T(8,128)(2,1)} %copy.76), calls=%async_computation | async-start | bytes 524288 | tf_op jit(solution)/shard_map/all_to_all | solution.py:117
  17.6 40.2 %collective-permute-start.4 = (bf16[2,128,2048]{2,1,0:T(8,128)(2,1)}, bf16[2,128,2048]{2,1,0:T(8,128)(2,1)}, u32[]{:S(2)}, u32[]{:S(2)}) collective-permute-start(bf16[2,128,2048]{2,1,0:T(8,128)(2,1)} %get-tuple-element.18), channel_id=1, source_target_pairs={{0,4},{4,0},{8,12},{12,8},{16,20},{20,16},{24,28},{28,24},{1,5},{5... | collective-permute-start | bytes 3145736 | tf_op jit(solution)/shard_map/ppermute | solution.py:74
  23.9 8.8 %collective-permute-start.37 = (bf16[256,512]{1,0:T(8,128)(2,1)S(1)}, bf16[256,512]{1,0:T(8,128)(2,1)}, u32[]{:S(2)}, u32[]{:S(2)}) collective-permute-start(bf16[256,512]{1,0:T(8,128)(2,1)S(1)} %bitcast.224), channel_id=1, source_target_pairs={{0,1},{1,0},{2,3},{3,2},{4,5},{5,4},{6,7},{7,6},{8,9},{9,8},{10,11... | collective-permute-start | bytes 786440 | tf_op jit(solution)/shard_map/ppermute | solution.py:74
  25.6 15.5 %collective-permute-start.25 = (bf16[256,512]{1,0:T(8,128)(2,1)S(1)}, bf16[256,512]{1,0:T(8,128)(2,1)}, u32[]{:S(2)}, u32[]{:S(2)}) collective-permute-start(bf16[256,512]{1,0:T(8,128)(2,1)S(1)} %bitcast.225), channel_id=1, source_target_pairs={{0,3},{1,2},{2,1},{3,0},{4,7},{5,6},{6,5},{7,4},{8,11},{9,10},{10,... | collective-permute-start | bytes 786440 | tf_op jit(solution)/shard_map/ppermute | solution.py:74
  28.1 22.4 %collective-permute-start.13 = (bf16[256,512]{1,0:T(8,128)(2,1)S(1)}, bf16[256,512]{1,0:T(8,128)(2,1)}, u32[]{:S(2)}, u32[]{:S(2)}) collective-permute-start(bf16[256,512]{1,0:T(8,128)(2,1)S(1)} %bitcast.226), channel_id=1, source_target_pairs={{0,2},{1,3},{2,0},{3,1},{4,6},{5,7},{6,4},{7,5},{8,10},{9,11},{10,... | collective-permute-start | bytes 786440 | tf_op jit(solution)/shard_map/ppermute | solution.py:74
  34.4 20.8 %collective-permute-start.38 = (bf16[256,512]{1,0:T(8,128)(2,1)}, bf16[256,512]{1,0:T(8,128)(2,1)}, u32[]{:S(2)}, u32[]{:S(2)}) collective-permute-start(bf16[256,512]{1,0:T(8,128)(2,1)} %bitcast.238), channel_id=1, source_target_pairs={{0,4},{4,0},{8,12},{12,8},{16,20},{20,16},{24,28},{28,24},{1,5},{5... | collective-permute-start | bytes 786440 | tf_op jit(solution)/shard_map/ppermute | solution.py:74
  42.8 13.9 %collective-permute-start.26 = (bf16[256,512]{1,0:T(8,128)(2,1)}, bf16[256,512]{1,0:T(8,128)(2,1)}, u32[]{:S(2)}, u32[]{:S(2)}) collective-permute-start(bf16[256,512]{1,0:T(8,128)(2,1)} %bitcast.237), channel_id=1, source_target_pairs={{0,4},{4,0},{8,12},{12,8},{16,20},{20,16},{24,28},{28,24},{1,5},{5... | collective-permute-start | bytes 786440 | tf_op jit(solution)/shard_map/ppermute | solution.py:74
  52.2 4.5 %copy-start.17 = (bf16[4,2,32,512]{3,2,1,0:T(8,128)(2,1)S(1)}, bf16[4,2,32,512]{3,2,1,0:T(8,128)(2,1)}, u32[]{:S(2)}) copy-start(bf16[4,2,32,512]{3,2,1,0:T(8,128)(2,1)} %rev.24) | copy-start | bytes 786436
  52.2 5.6 %collective-permute-start.14 = (bf16[256,512]{1,0:T(8,128)(2,1)}, bf16[256,512]{1,0:T(8,128)(2,1)S(1)}, u32[]{:S(2)}, u32[]{:S(2)}) collective-permute-start(bf16[256,512]{1,0:T(8,128)(2,1)} %bitcast.236), channel_id=1, source_target_pairs={{0,4},{4,0},{8,12},{12,8},{16,20},{20,16},{24,28},{28,24},{1,5},{5... | collective-permute-start | bytes 786440 | tf_op jit(solution)/shard_map/ppermute | solution.py:74
  55.2 4.5 %collective-permute-start.1 = (bf16[2048,512]{1,0:T(8,128)(2,1)}, bf16[2048,512]{1,0:T(8,128)(2,1)S(1)}, u32[]{:S(2)}, u32[]{:S(2)}) collective-permute-start(bf16[2048,512]{1,0:T(8,128)(2,1)} %get-tuple-element.9), channel_id=1, source_target_pairs={{0,4},{4,0},{8,12},{12,8},{16,20},{20,16},{24,28},{28,24},{1,5},{5... | collective-permute-start | bytes 6291464 | tf_op jit(solution)/shard_map/ppermute | solution.py:74
  56.7 12.2 %collective-permute-start = (bf16[256,512]{1,0:T(8,128)(2,1)S(1)}, bf16[256,512]{1,0:T(8,128)(2,1)S(1)}, u32[]{:S(2)}, u32[]{:S(2)}) collective-permute-start(bf16[256,512]{1,0:T(8,128)(2,1)S(1)} %bitcast.235), channel_id=1, source_target_pairs={{0,4},{4,0},{8,12},{12,8},{16,20},{20,16},{24,28},{28,24},{1,5},{5... | collective-permute-start | bytes 786440 | tf_op jit(solution)/shard_map/ppermute | solution.py:74
  65.2 9.2 %collective-permute-start.43 = (bf16[128,1024]{1,0:T(8,128)(2,1)S(1)}, bf16[128,1024]{1,0:T(8,128)(2,1)S(1)}, u32[]{:S(2)}, u32[]{:S(2)}) collective-permute-start(bf16[128,1024]{1,0:T(8,128)(2,1)S(1)} %concatenate.148), channel_id=1, source_target_pairs={{0,16},{4,20},{8,24},{12,28},{16,0},{20,4},{24,8},{28,12},{1,17},{... | collective-permute-start | bytes 786440 | tf_op jit(solution)/shard_map/ppermute | solution.py:74
  65.9 9.2 %collective-permute-start.39 = (bf16[128,1024]{1,0:T(8,128)(2,1)S(1)}, bf16[128,1024]{1,0:T(8,128)(2,1)S(1)}, u32[]{:S(2)}, u32[]{:S(2)}) collective-permute-start(bf16[128,1024]{1,0:T(8,128)(2,1)S(1)} %pad_maximum_fusion.23), channel_id=1, source_target_pairs={{0,8},{4,12},{8,0},{12,4},{16,24},{20,28},{24,16},{28,20},{1,9},{5... | collective-permute-start | bytes 786440 | tf_op jit(solution)/shard_map/ppermute | solution.py:74
  67.1 12.9 %collective-permute-start.31 = (bf16[128,1024]{1,0:T(8,128)(2,1)S(1)}, bf16[128,1024]{1,0:T(8,128)(2,1)S(1)}, u32[]{:S(2)}, u32[]{:S(2)}) collective-permute-start(bf16[128,1024]{1,0:T(8,128)(2,1)S(1)} %concatenate.147), channel_id=1, source_target_pairs={{0,16},{4,20},{8,24},{12,28},{16,0},{20,4},{24,8},{28,12},{1,17},{... | collective-permute-start | bytes 786440 | tf_op jit(solution)/shard_map/ppermute | solution.py:74
  68.9 11.8 %collective-permute-start.27 = (bf16[128,1024]{1,0:T(8,128)(2,1)S(1)}, bf16[128,1024]{1,0:T(8,128)(2,1)S(1)}, u32[]{:S(2)}, u32[]{:S(2)}) collective-permute-start(bf16[128,1024]{1,0:T(8,128)(2,1)S(1)} %pad_maximum_fusion.20), channel_id=1, source_target_pairs={{0,8},{4,12},{8,0},{12,4},{16,24},{20,28},{24,16},{28,20},{1,9},{5... | collective-permute-start | bytes 786440 | tf_op jit(solution)/shard_map/ppermute | solution.py:74
  74.4 11.2 %collective-permute-start.19 = (bf16[128,1024]{1,0:T(8,128)(2,1)S(1)}, bf16[128,1024]{1,0:T(8,128)(2,1)S(1)}, u32[]{:S(2)}, u32[]{:S(2)}) collective-permute-start(bf16[128,1024]{1,0:T(8,128)(2,1)S(1)} %concatenate.146), channel_id=1, source_target_pairs={{0,16},{4,20},{8,24},{12,28},{16,0},{20,4},{24,8},{28,12},{1,17},{... | collective-permute-start | bytes 786440 | tf_op jit(solution)/shard_map/ppermute | solution.py:74
  75.1 11.9 %collective-permute-start.15 = (bf16[128,1024]{1,0:T(8,128)(2,1)S(1)}, bf16[128,1024]{1,0:T(8,128)(2,1)S(1)}, u32[]{:S(2)}, u32[]{:S(2)}) collective-permute-start(bf16[128,1024]{1,0:T(8,128)(2,1)S(1)} %pad_maximum_fusion.17), channel_id=1, source_target_pairs={{0,8},{4,12},{8,0},{12,4},{16,24},{20,28},{24,16},{28,20},{1,9},{5... | collective-permute-start | bytes 786440 | tf_op jit(solution)/shard_map/ppermute | solution.py:74
  80.0 11.2 %collective-permute-start.8 = (bf16[128,1024]{1,0:T(8,128)(2,1)S(1)}, bf16[128,1024]{1,0:T(8,128)(2,1)S(1)}, u32[]{:S(2)}, u32[]{:S(2)}) collective-permute-start(bf16[128,1024]{1,0:T(8,128)(2,1)S(1)} %concatenate.145), channel_id=1, source_target_pairs={{0,16},{4,20},{8,24},{12,28},{16,0},{20,4},{24,8},{28,12},{1,17},{... | collective-permute-start | bytes 786440 | tf_op jit(solution)/shard_map/ppermute | solution.py:74
  80.7 11.9 %collective-permute-start.2 = (bf16[128,1024]{1,0:T(8,128)(2,1)S(1)}, bf16[128,1024]{1,0:T(8,128)(2,1)S(1)}, u32[]{:S(2)}, u32[]{:S(2)}) collective-permute-start(bf16[128,1024]{1,0:T(8,128)(2,1)S(1)} %pad_maximum_fusion.14), channel_id=1, source_target_pairs={{0,8},{4,12},{8,0},{12,4},{16,24},{20,28},{24,16},{28,20},{1,9},{5... | collective-permute-start | bytes 786440 | tf_op jit(solution)/shard_map/ppermute | solution.py:74
  85.6 9.1 %collective-permute-start.44 = (bf16[64,1024]{1,0:T(8,128)(2,1)S(1)}, bf16[64,1024]{1,0:T(8,128)(2,1)S(1)}, u32[]{:S(2)}, u32[]{:S(2)}) collective-permute-start(bf16[64,1024]{1,0:T(8,128)(2,1)S(1)} %add_convert_fusion.1), channel_id=1, source_target_pairs={{0,8},{4,12},{8,0},{12,4},{16,24},{20,28},{24,16},{28,20},{1,9},{5... | collective-permute-start | bytes 393224 | tf_op jit(solution)/shard_map/ppermute | solution.py:74
  87.0 9.2 %collective-permute-start.40 = (bf16[64,1024]{1,0:T(8,128)(2,1)S(1)}, bf16[64,1024]{1,0:T(8,128)(2,1)S(1)}, u32[]{:S(2)}, u32[]{:S(2)}) collective-permute-start(bf16[64,1024]{1,0:T(8,128)(2,1)S(1)} %add_convert_fusion.2), channel_id=1, source_target_pairs={{0,16},{4,20},{8,24},{12,28},{16,0},{20,4},{24,8},{28,12},{1,17},{... | collective-permute-start | bytes 393224 | tf_op jit(solution)/shard_map/ppermute | solution.py:74
  91.2 6.8 %collective-permute-start.32 = (bf16[64,1024]{1,0:T(8,128)(2,1)S(1)}, bf16[64,1024]{1,0:T(8,128)(2,1)S(1)}, u32[]{:S(2)}, u32[]{:S(2)}) collective-permute-start(bf16[64,1024]{1,0:T(8,128)(2,1)S(1)} %add_convert_fusion.3), channel_id=1, source_target_pairs={{0,8},{4,12},{8,0},{12,4},{16,24},{20,28},{24,16},{28,20},{1,9},{5... | collective-permute-start | bytes 393224 | tf_op jit(solution)/shard_map/ppermute | solution.py:74
  92.6 6.5 %collective-permute-start.28 = (bf16[64,1024]{1,0:T(8,128)(2,1)S(1)}, bf16[64,1024]{1,0:T(8,128)(2,1)S(1)}, u32[]{:S(2)}, u32[]{:S(2)}) collective-permute-start(bf16[64,1024]{1,0:T(8,128)(2,1)S(1)} %add_convert_fusion.4), channel_id=1, source_target_pairs={{0,16},{4,20},{8,24},{12,28},{16,0},{20,4},{24,8},{28,12},{1,17},{... | collective-permute-start | bytes 393224 | tf_op jit(solution)/shard_map/ppermute | solution.py:74
  94.8 6.2 %collective-permute-start.20 = (bf16[64,1024]{1,0:T(8,128)(2,1)S(1)}, bf16[64,1024]{1,0:T(8,128)(2,1)S(1)}, u32[]{:S(2)}, u32[]{:S(2)}) collective-permute-start(bf16[64,1024]{1,0:T(8,128)(2,1)S(1)} %add_convert_fusion.5), channel_id=1, source_target_pairs={{0,8},{4,12},{8,0},{12,4},{16,24},{20,28},{24,16},{28,20},{1,9},{5... | collective-permute-start | bytes 393224 | tf_op jit(solution)/shard_map/ppermute | solution.py:74
  96.1 6.4 %collective-permute-start.16 = (bf16[64,1024]{1,0:T(8,128)(2,1)S(1)}, bf16[64,1024]{1,0:T(8,128)(2,1)S(1)}, u32[]{:S(2)}, u32[]{:S(2)}) collective-permute-start(bf16[64,1024]{1,0:T(8,128)(2,1)S(1)} %add_convert_fusion.6), channel_id=1, source_target_pairs={{0,16},{4,20},{8,24},{12,28},{16,0},{20,4},{24,8},{28,12},{1,17},{... | collective-permute-start | bytes 393224 | tf_op jit(solution)/shard_map/ppermute | solution.py:74
  98.1 6.9 %collective-permute-start.9 = (bf16[64,1024]{1,0:T(8,128)(2,1)S(1)}, bf16[64,1024]{1,0:T(8,128)(2,1)S(1)}, u32[]{:S(2)}, u32[]{:S(2)}) collective-permute-start(bf16[64,1024]{1,0:T(8,128)(2,1)S(1)} %add_convert_fusion.7), channel_id=1, source_target_pairs={{0,8},{4,12},{8,0},{12,4},{16,24},{20,28},{24,16},{28,20},{1,9},{5... | collective-permute-start | bytes 393224 | tf_op jit(solution)/shard_map/ppermute | solution.py:74
  99.1 7.5 %collective-permute-start.3 = (bf16[64,1024]{1,0:T(8,128)(2,1)S(1)}, bf16[64,1024]{1,0:T(8,128)(2,1)S(1)}, u32[]{:S(2)}, u32[]{:S(2)}) collective-permute-start(bf16[64,1024]{1,0:T(8,128)(2,1)S(1)} %add_convert_fusion.8), channel_id=1, source_target_pairs={{0,16},{4,20},{8,24},{12,28},{16,0},{20,4},{24,8},{28,12},{1,17},{... | collective-permute-start | bytes 393224 | tf_op jit(solution)/shard_map/ppermute | solution.py:74
  100.9 9.3 %collective-permute-start.45 = (bf16[64,2048]{1,0:T(8,128)(2,1)S(1)}, bf16[64,2048]{1,0:T(8,128)(2,1)S(1)}, u32[]{:S(2)}, u32[]{:S(2)}) collective-permute-start(bf16[64,2048]{1,0:T(8,128)(2,1)S(1)} %get-tuple-element.91), channel_id=1, source_target_pairs={{0,8},{4,12},{8,0},{12,4},{16,24},{20,28},{24,16},{28,20},{1,9},{5... | collective-permute-start | bytes 786440 | tf_op jit(solution)/shard_map/ppermute | solution.py:74
  102.6 9.2 %collective-permute-start.41 = (bf16[64,2048]{1,0:T(8,128)(2,1)S(1)}, bf16[64,2048]{1,0:T(8,128)(2,1)S(1)}, u32[]{:S(2)}, u32[]{:S(2)}) collective-permute-start(bf16[64,2048]{1,0:T(8,128)(2,1)S(1)} %get-tuple-element.89), channel_id=1, source_target_pairs={{0,16},{4,20},{8,24},{12,28},{16,0},{20,4},{24,8},{28,12},{1,17},{... | collective-permute-start | bytes 786440 | tf_op jit(solution)/shard_map/ppermute | solution.py:74
  105.0 10.9 %collective-permute-start.33 = (bf16[64,2048]{1,0:T(8,128)(2,1)S(1)}, bf16[64,2048]{1,0:T(8,128)(2,1)S(1)}, u32[]{:S(2)}, u32[]{:S(2)}) collective-permute-start(bf16[64,2048]{1,0:T(8,128)(2,1)S(1)} %get-tuple-element.87), channel_id=1, source_target_pairs={{0,8},{4,12},{8,0},{12,4},{16,24},{20,28},{24,16},{28,20},{1,9},{5... | collective-permute-start | bytes 786440 | tf_op jit(solution)/shard_map/ppermute | solution.py:74
  106.6 10.8 %collective-permute-start.29 = (bf16[64,2048]{1,0:T(8,128)(2,1)S(1)}, bf16[64,2048]{1,0:T(8,128)(2,1)S(1)}, u32[]{:S(2)}, u32[]{:S(2)}) collective-permute-start(bf16[64,2048]{1,0:T(8,128)(2,1)S(1)} %get-tuple-element.85), channel_id=1, source_target_pairs={{0,16},{4,20},{8,24},{12,28},{16,0},{20,4},{24,8},{28,12},{1,17},{... | collective-permute-start | bytes 786440 | tf_op jit(solution)/shard_map/ppermute | solution.py:74
  110.2 11.2 %collective-permute-start.21 = (bf16[64,2048]{1,0:T(8,128)(2,1)S(1)}, bf16[64,2048]{1,0:T(8,128)(2,1)S(1)}, u32[]{:S(2)}, u32[]{:S(2)}) collective-permute-start(bf16[64,2048]{1,0:T(8,128)(2,1)S(1)} %get-tuple-element.83), channel_id=1, source_target_pairs={{0,8},{4,12},{8,0},{12,4},{16,24},{20,28},{24,16},{28,20},{1,9},{5... | collective-permute-start | bytes 786440 | tf_op jit(solution)/shard_map/ppermute | solution.py:74
  111.8 11.2 %collective-permute-start.17 = (bf16[64,2048]{1,0:T(8,128)(2,1)S(1)}, bf16[64,2048]{1,0:T(8,128)(2,1)S(1)}, u32[]{:S(2)}, u32[]{:S(2)}) collective-permute-start(bf16[64,2048]{1,0:T(8,128)(2,1)S(1)} %get-tuple-element.81), channel_id=1, source_target_pairs={{0,16},{4,20},{8,24},{12,28},{16,0},{20,4},{24,8},{28,12},{1,17},{... | collective-permute-start | bytes 786440 | tf_op jit(solution)/shard_map/ppermute | solution.py:74
  115.9 11.2 %collective-permute-start.10 = (bf16[64,2048]{1,0:T(8,128)(2,1)S(1)}, bf16[64,2048]{1,0:T(8,128)(2,1)S(1)}, u32[]{:S(2)}, u32[]{:S(2)}) collective-permute-start(bf16[64,2048]{1,0:T(8,128)(2,1)S(1)} %get-tuple-element.79), channel_id=1, source_target_pairs={{0,8},{4,12},{8,0},{12,4},{16,24},{20,28},{24,16},{28,20},{1,9},{5... | collective-permute-start | bytes 786440 | tf_op jit(solution)/shard_map/ppermute | solution.py:74
  117.4 11.2 %collective-permute-start.5 = (bf16[64,2048]{1,0:T(8,128)(2,1)S(1)}, bf16[64,2048]{1,0:T(8,128)(2,1)S(1)}, u32[]{:S(2)}, u32[]{:S(2)}) collective-permute-start(bf16[64,2048]{1,0:T(8,128)(2,1)S(1)} %get-tuple-element.77), channel_id=1, source_target_pairs={{0,16},{4,20},{8,24},{12,28},{16,0},{20,4},{24,8},{28,12},{1,17},{... | collective-permute-start | bytes 786440 | tf_op jit(solution)/shard_map/ppermute | solution.py:74
  121.5 8.4 %copy-start.24 = (bf16[64,2048]{1,0:T(8,128)(2,1)}, bf16[64,2048]{1,0:T(8,128)(2,1)S(1)}, u32[]{:S(2)}) copy-start(bf16[64,2048]{1,0:T(8,128)(2,1)S(1)} %collective-permute-done.21) | copy-start | bytes 786436
  121.5 18.4 %collective-permute-start.46 = (bf16[128,2048]{1,0:T(8,128)(2,1)S(1)}, bf16[128,2048]{1,0:T(8,128)(2,1)S(1)}, u32[]{:S(2)}, u32[]{:S(2)}) collective-permute-start(bf16[128,2048]{1,0:T(8,128)(2,1)S(1)} %pad_maximum_fusion.11), channel_id=1, source_target_pairs={{0,16},{4,20},{8,24},{12,28},{16,0},{20,4},{24,8},{28,12},{1,17},{... | collective-permute-start | bytes 1572872 | tf_op jit(solution)/shard_map/ppermute | solution.py:74
  123.0 5.6 %copy-start.26 = (bf16[64,2048]{1,0:T(8,128)(2,1)}, bf16[64,2048]{1,0:T(8,128)(2,1)S(1)}, u32[]{:S(2)}) copy-start(bf16[64,2048]{1,0:T(8,128)(2,1)S(1)} %collective-permute-done.17) | copy-start | bytes 786436
  123.1 18.3 %collective-permute-start.42 = (bf16[128,2048]{1,0:T(8,128)(2,1)S(1)}, bf16[128,2048]{1,0:T(8,128)(2,1)S(1)}, u32[]{:S(2)}, u32[]{:S(2)}) collective-permute-start(bf16[128,2048]{1,0:T(8,128)(2,1)S(1)} %pad_maximum_fusion.10), channel_id=1, source_target_pairs={{0,8},{4,12},{8,0},{12,4},{16,24},{20,28},{24,16},{28,20},{1,9},{5... | collective-permute-start | bytes 1572872 | tf_op jit(solution)/shard_map/ppermute | solution.py:74
  127.1 24.1 %collective-permute-start.34 = (bf16[128,2048]{1,0:T(8,128)(2,1)S(1)}, bf16[128,2048]{1,0:T(8,128)(2,1)S(1)}, u32[]{:S(2)}, u32[]{:S(2)}) collective-permute-start(bf16[128,2048]{1,0:T(8,128)(2,1)S(1)} %pad_maximum_fusion.9), channel_id=1, source_target_pairs={{0,16},{4,20},{8,24},{12,28},{16,0},{20,4},{24,8},{28,12},{1,17},{... | collective-permute-start | bytes 1572872 | tf_op jit(solution)/shard_map/ppermute | solution.py:74
  128.7 24.8 %copy-start.22 = (bf16[64,2048]{1,0:T(8,128)(2,1)}, bf16[64,2048]{1,0:T(8,128)(2,1)S(1)}, u32[]{:S(2)}) copy-start(bf16[64,2048]{1,0:T(8,128)(2,1)S(1)} %collective-permute-done.5) | copy-start | bytes 786436
  128.7 24.8 %collective-permute-start.30 = (bf16[128,2048]{1,0:T(8,128)(2,1)S(1)}, bf16[128,2048]{1,0:T(8,128)(2,1)S(1)}, u32[]{:S(2)}, u32[]{:S(2)}) collective-permute-start(bf16[128,2048]{1,0:T(8,128)(2,1)S(1)} %pad_maximum_fusion.8), channel_id=1, source_target_pairs={{0,8},{4,12},{8,0},{12,4},{16,24},{20,28},{24,16},{28,20},{1,9},{5... | collective-permute-start | bytes 1572872 | tf_op jit(solution)/shard_map/ppermute | solution.py:74
  139.9 22.5 %collective-permute-start.22 = (bf16[128,2048]{1,0:T(8,128)(2,1)S(1)}, bf16[128,2048]{1,0:T(8,128)(2,1)S(1)}, u32[]{:S(2)}, u32[]{:S(2)}) collective-permute-start(bf16[128,2048]{1,0:T(8,128)(2,1)S(1)} %pad_maximum_fusion.7), channel_id=1, source_target_pairs={{0,16},{4,20},{8,24},{12,28},{16,0},{20,4},{24,8},{28,12},{1,17},{... | collective-permute-start | bytes 1572872 | tf_op jit(solution)/shard_map/ppermute | solution.py:74
  141.4 21.8 %collective-permute-start.18 = (bf16[128,2048]{1,0:T(8,128)(2,1)S(1)}, bf16[128,2048]{1,0:T(8,128)(2,1)S(1)}, u32[]{:S(2)}, u32[]{:S(2)}) collective-permute-start(bf16[128,2048]{1,0:T(8,128)(2,1)S(1)} %pad_maximum_fusion.6), channel_id=1, source_target_pairs={{0,8},{4,12},{8,0},{12,4},{16,24},{20,28},{24,16},{28,20},{1,9},{5... | collective-permute-start | bytes 1572872 | tf_op jit(solution)/shard_map/ppermute | solution.py:74
  151.1 20.3 %collective-permute-start.11 = (bf16[128,2048]{1,0:T(8,128)(2,1)S(1)}, bf16[128,2048]{1,0:T(8,128)(2,1)S(1)}, u32[]{:S(2)}, u32[]{:S(2)}) collective-permute-start(bf16[128,2048]{1,0:T(8,128)(2,1)S(1)} %pad_maximum_fusion.5), channel_id=1, source_target_pairs={{0,16},{4,20},{8,24},{12,28},{16,0},{20,4},{24,8},{28,12},{1,17},{... | collective-permute-start | bytes 1572872 | tf_op jit(solution)/shard_map/ppermute | solution.py:74
  153.5 18.8 %collective-permute-start.6 = (bf16[128,2048]{1,0:T(8,128)(2,1)S(1)}, bf16[128,2048]{1,0:T(8,128)(2,1)S(1)}, u32[]{:S(2)}, u32[]{:S(2)}) collective-permute-start(bf16[128,2048]{1,0:T(8,128)(2,1)S(1)} %pad_maximum_fusion.4), channel_id=1, source_target_pairs={{0,8},{4,12},{8,0},{12,4},{16,24},{20,28},{24,16},{28,20},{1,9},{5... | collective-permute-start | bytes 1572872 | tf_op jit(solution)/shard_map/ppermute | solution.py:74
  155.0 18.1 %copy-start.1 = (bf16[512,2048]{1,0:T(8,128)(2,1)S(1)}, bf16[512,2048]{1,0:T(8,128)(2,1)}, u32[]{:S(2)}) copy-start(bf16[512,2048]{1,0:T(8,128)(2,1)} %get-tuple-element.12) | copy-start | bytes 6291460
  155.0 18.1 %copy-start.2 = (bf16[512,2048]{1,0:T(8,128)(2,1)S(1)}, bf16[512,2048]{1,0:T(8,128)(2,1)}, u32[]{:S(2)}) copy-start(bf16[512,2048]{1,0:T(8,128)(2,1)} %get-tuple-element.93) | copy-start | bytes 6291460
  206.6 32.9 %copy-start = (bf16[1024,2,2,1024]{3,2,1,0:T(2,128)(2,1)S(1)}, bf16[1024,2,2,1024]{3,2,1,0:T(2,128)(2,1)}, u32[]{:S(2)}) copy-start(bf16[1024,2,2,1024]{3,2,1,0:T(2,128)(2,1)} %reshape.255) | copy-start | bytes 25165828
  290.4 5.1 %copy-start.8 = (f32[4,2,32,2,512]{4,3,2,1,0:T(2,128)}, f32[4,2,32,2,512]{4,3,2,1,0:T(2,128)S(1)}, u32[]{:S(2)}) copy-start(f32[4,2,32,2,512]{4,3,2,1,0:T(2,128)S(1)} %reshape.265) | copy-start | bytes 3145732
  297.7 5.1 %copy-start.9 = (f32[4,2,32,2,512]{4,3,2,1,0:T(2,128)}, f32[4,2,32,2,512]{4,3,2,1,0:T(2,128)S(1)}, u32[]{:S(2)}) copy-start(f32[4,2,32,2,512]{4,3,2,1,0:T(2,128)S(1)} %reshape.262) | copy-start | bytes 3145732
  299.2 3.7 %copy-start.38 = (bf16[1,64,2048]{2,1,0:T(8,128)(2,1)S(1)}, bf16[1,64,2048]{2,1,0:T(8,128)(2,1)}, u32[]{:S(2)}) copy-start(bf16[1,64,2048]{2,1,0:T(8,128)(2,1)} %get-tuple-element.46) | copy-start | bytes 786436
  299.2 3.7 %copy-start.39 = (bf16[1,64,2048]{2,1,0:T(8,128)(2,1)S(1)}, bf16[1,64,2048]{2,1,0:T(8,128)(2,1)}, u32[]{:S(2)}) copy-start(bf16[1,64,2048]{2,1,0:T(8,128)(2,1)} %get-tuple-element.47) | copy-start | bytes 786436
  308.7 6.9 %collective-permute-start.47 = (bf16[4,2,32,512]{3,2,1,0:T(8,128)(2,1)}, bf16[4,2,32,512]{3,2,1,0:T(8,128)(2,1)}, u32[]{:S(2)}, u32[]{:S(2)}) collective-permute-start(bf16[4,2,32,512]{3,2,1,0:T(8,128)(2,1)} %fusion.149), channel_id=1, source_target_pairs={{0,4},{4,0},{8,12},{12,8},{16,20},{20,16},{24,28},{28,24},{1,5},{5... | collective-permute-start | bytes 786440 | tf_op jit(solution)/shard_map/ppermute | solution.py:74
  308.8 8.0 %collective-permute-start.35 = (bf16[4,2,32,512]{3,2,1,0:T(8,128)(2,1)S(1)}, bf16[4,2,32,512]{3,2,1,0:T(8,128)(2,1)}, u32[]{:S(2)}, u32[]{:S(2)}) collective-permute-start(bf16[4,2,32,512]{3,2,1,0:T(8,128)(2,1)S(1)} %fusion.148), channel_id=1, source_target_pairs={{0,4},{4,0},{8,12},{12,8},{16,20},{20,16},{24,28},{28,24},{1,5},{5... | collective-permute-start | bytes 786440 | tf_op jit(solution)/shard_map/ppermute | solution.py:74
  309.4 11.1 %collective-permute-start.23 = (bf16[4,2,32,512]{3,2,1,0:T(8,128)(2,1)S(1)}, bf16[4,2,32,512]{3,2,1,0:T(8,128)(2,1)}, u32[]{:S(2)}, u32[]{:S(2)}) collective-permute-start(bf16[4,2,32,512]{3,2,1,0:T(8,128)(2,1)S(1)} %fusion.147), channel_id=1, source_target_pairs={{0,4},{4,0},{8,12},{12,8},{16,20},{20,16},{24,28},{28,24},{1,5},{5... | collective-permute-start | bytes 786440 | tf_op jit(solution)/shard_map/ppermute | solution.py:74
  314.9 5.7 %slice-start.2 = ((f32[4,2,32,2,512]{4,3,2,1,0:T(2,128)}), f32[4,2,32,1,512]{4,3,2,1,0:T(1,128)S(1)}, s32[]{:S(2)}) async-start(f32[4,2,32,2,512]{4,3,2,1,0:T(2,128)} %copy-done.10), calls=%async_computation.4 | async-start | bytes 1048576 | tf_op jit(solution)/shard_map/slice | solution.py:173
  315.6 7.3 %collective-permute-start.12 = (bf16[4,2,32,512]{3,2,1,0:T(8,128)(2,1)S(1)}, bf16[4,2,32,512]{3,2,1,0:T(8,128)(2,1)S(1)}, u32[]{:S(2)}, u32[]{:S(2)}) collective-permute-start(bf16[4,2,32,512]{3,2,1,0:T(8,128)(2,1)S(1)} %fusion.146), channel_id=1, source_target_pairs={{0,4},{4,0},{8,12},{12,8},{16,20},{20,16},{24,28},{28,24},{1,5},{5... | collective-permute-start | bytes 786440 | tf_op jit(solution)/shard_map/ppermute | solution.py:74
  316.7 8.8 %collective-permute-start.48 = (bf16[4,2,32,512]{3,2,1,0:T(8,128)(2,1)S(1)}, bf16[4,2,32,512]{3,2,1,0:T(8,128)(2,1)S(1)}, u32[]{:S(2)}, u32[]{:S(2)}) collective-permute-start(bf16[4,2,32,512]{3,2,1,0:T(8,128)(2,1)S(1)} %fusion.67), channel_id=1, source_target_pairs={{0,1},{1,0},{2,3},{3,2},{4,5},{5,4},{6,7},{7,6},{8,9},{9,8},{10,11... | collective-permute-start | bytes 786440 | tf_op jit(solution)/shard_map/ppermute | solution.py:74
  317.8 14.4 %collective-permute-start.36 = (bf16[4,2,32,512]{3,2,1,0:T(8,128)(2,1)S(1)}, bf16[4,2,32,512]{3,2,1,0:T(8,128)(2,1)S(1)}, u32[]{:S(2)}, u32[]{:S(2)}) collective-permute-start(bf16[4,2,32,512]{3,2,1,0:T(8,128)(2,1)S(1)} %fusion.69), channel_id=1, source_target_pairs={{0,3},{1,2},{2,1},{3,0},{4,7},{5,6},{6,5},{7,4},{8,11},{9,10},{10,... | collective-permute-start | bytes 786440 | tf_op jit(solution)/shard_map/ppermute | solution.py:74
  321.6 23.0 %collective-permute-start.24 = (bf16[4,2,32,512]{3,2,1,0:T(8,128)(2,1)S(1)}, bf16[4,2,32,512]{3,2,1,0:T(8,128)(2,1)S(1)}, u32[]{:S(2)}, u32[]{:S(2)}) collective-permute-start(bf16[4,2,32,512]{3,2,1,0:T(8,128)(2,1)S(1)} %fusion.71), channel_id=1, source_target_pairs={{0,2},{1,3},{2,0},{3,1},{4,6},{5,7},{6,4},{7,5},{8,10},{9,11},{10,... | collective-permute-start | bytes 786440 | tf_op jit(solution)/shard_map/ppermute | solution.py:74
  (34 other events, 83.9 us)

commit v3 on v1

--- a/solution.py
+++ b/solution.py
@@ -1,7 +1,19 @@
 import jax
 import jax.numpy as jnp
 from jax import lax
+from jax.experimental import pallas as pl
+from jax.experimental.pallas import tpu as pltpu
 from jax.sharding import PartitionSpec as P
+
+
+CHUNKS = (((0,), 0, 32), ((2,), 0, 32), ((3,), 0, 32), ((1,), 0, 32))
+GATHERED = 4
+ORDER = (
+    (0, 0), (0, 1), (1, 0), (0, 2), (1, 1), (2, 0), (0, 3), (1, 2),
+    (2, 1), (3, 0), (1, 3), (0, 4), (2, 2), (3, 1), (0, 5), (2, 3),
+    (1, 4), (3, 2), (0, 6), (1, 5), (3, 3), (2, 4), (1, 6), (2, 5),
+    (3, 4), (2, 6), (3, 5), (3, 6),
+)
 
 
 def swiglu_grads(upstream, gate_pre, up_pre):
@@ -42,7 +54,7 @@
     return placing, weight_zero * factor
 
 
-def per_device(out_grad, routes, gates, lengths, saved_gate, saved_up, w_gate, w_up, w_down):
+def plain_exchange(out_grad, routes, gates, lengths, saved_gate, saved_up, w_gate, w_up, w_down):
     group_size = lax.axis_size("et")
     groups = lax.axis_size("dp")
     group_rows = saved_gate.shape[1]
@@ -69,6 +81,348 @@
     return input_grad.astype(jnp.bfloat16)
 
 
+def swap(values, axis, offset):
+    size = lax.axis_size(axis)
+    return lax.ppermute(values, axis, [(i, i ^ offset) for i in range(size)])
+
+
+def exchange(values, turn):
+    size = lax.axis_size("dp")
+    return lax.ppermute(values, "dp", [(i, i ^ (2 if (i + turn) % 2 == 0 else 4)) for i in range(size)])
+
+
+def whole(array):
+    return pl.BlockSpec(array.shape, lambda i, where: (0,) * len(array.shape))
+
+
+def shape(rows, columns, kind=jnp.bfloat16):
+    return jax.ShapeDtypeStruct((rows, columns), kind)
+
+
+class Steps:
+    def __init__(self, where):
+        self.where = where
+        self.last = []
+        self.waits = []
+
+    def call(self, kernel, out_shape, flops, moved, grid, in_specs, out_specs, operands, scratch_shapes=()):
+        after = self.last + self.waits
+        self.waits = []
+        inputs = 1 + len(operands)
+
+        def ordered(*refs):
+            kernel(*refs[1:inputs], *refs[inputs + len(after) :])
+
+        results = pl.pallas_call(
+            ordered,
+            out_shape=out_shape,
+            cost_estimate=pl.CostEstimate(flops=flops, bytes_accessed=moved, transcendentals=0),
+            compiler_params=pltpu.CompilerParams(vmem_limit_bytes=48 * 1024 * 1024),
+            grid_spec=pltpu.PrefetchScalarGridSpec(
+                num_scalar_prefetch=1,
+                grid=grid,
+                in_specs=list(in_specs) + [pl.BlockSpec(memory_space=pl.ANY)] * len(after),
+                out_specs=out_specs,
+                scratch_shapes=scratch_shapes,
+            ),
+        )(self.where, *operands, *after)
+        self.last = list(results[:1])
+        return results
+
+
+def whole(array):
+    return pl.BlockSpec(array.shape, lambda i, where: (0,) * len(array.shape))
+
+
+def shape(rows, columns, kind=jnp.bfloat16):
+    return jax.ShapeDtypeStruct((rows, columns), kind)
+
+
+PARTNER_CHIP = (0, 2, 1, 3)
+
+
+def partial_sums(steps, chunk, here, there, own_down, other_down, slots):
+    offsets, low, high = chunk
+    members, count = len(offsets), high - low
+    width = own_down.shape[1]
+    block = members * 2 * count
+    half = own_down.shape[0] // 2
+    step = half // 4
+
+    def kernel(*refs):
+        here_refs, there_refs = refs[:members], refs[members : 2 * members]
+        own_ref, other_ref, send, keep, left = refs[2 * members :]
+
+        @pl.when(pl.program_id(0) == 0)
+        def _():
+            for q in range(members):
+                for chip in range(4):
+                    for core in range(2):
+                        to = chip * block + (q * 2 + core) * count
+                        at = (chip * 2 + core) * slots + low
+                        left[to : to + count, :width] = here_refs[q][0, at : at + count, :]
+                        at = (PARTNER_CHIP[chip] * 2 + 1 - core) * slots + low
+                        left[to : to + count, width:] = there_refs[q][0, at : at + count, :]
+
+        sums = contract_last(left[:, :width], own_ref[...]) + contract_last(left[:, width:], other_ref[...])
+        sums = sums.astype(jnp.bfloat16)
+        keep[:block], send[:block] = sums[:block], sums[block : 2 * block]
+        keep[block:], send[block:] = sums[2 * block : 3 * block], sums[3 * block :]
+
+    weight = pl.BlockSpec((step, width), lambda i, where: (where[0] * 4 + i, 0))
+    rows = here[0][0].shape[1]
+
+    def row_spec(array, index):
+        return pl.BlockSpec((1, rows, width), lambda i, where: (index(where), 0, 0))
+
+    return steps.call(
+        kernel,
+        [shape(2 * block, half)] * 2,
+        16 * block * width * half,
+        4 * half * width + 8 * block * (2 * width + half),
+        (4,),
+        [row_spec(*x) for x in here + there] + [weight, weight],
+        [pl.BlockSpec((2 * block, step), lambda i, where: (0, i))] * 2,
+        [x[0] for x in here + there] + [own_down, other_down],
+        [pltpu.VMEM((4 * block, 2 * width), jnp.bfloat16)],
+    )
+
+
+def second_terms(steps, keep, got):
+    rows, columns = keep.shape[0] // 2, keep.shape[1]
+
+    def kernel(keep, got, send):
+        send[...] = (keep[...].astype(jnp.float32) + got[...].astype(jnp.float32)).astype(jnp.bfloat16)
+
+    return steps.call(
+        kernel,
+        [shape(rows, columns)],
+        rows * columns,
+        6 * rows * columns,
+        (1,),
+        [pl.BlockSpec((rows, columns), lambda i, where: (1, 0))] * 2,
+        [pl.BlockSpec((rows, columns), lambda i, where: (0, 0))],
+        [keep, got],
+    )[0]
+
+
+def hidden_grads(steps, chunk, keep, got, last, saved):
+    offsets, low, high = chunk
+    members, count = len(offsets), high - low
+    rows, columns = last.shape
+
+    def kernel(keep, got, last, *refs):
+        out = refs[-1]
+        for q in range(members):
+            for core in range(2):
+                take = pl.ds((q * 2 + core) * count, count)
+                upstream = (
+                    keep[take, :].astype(jnp.float32)
+                    + got[take, :].astype(jnp.float32)
+                    + last[take, :].astype(jnp.float32)
+                )
+                gate, up = refs[(q * 2 + core) * 2 : (q * 2 + core) * 2 + 2]
+                grad_gate, grad_up = swiglu_grads(upstream, gate[0], up[0])
+                out[take, :columns] = grad_gate
+                out[take, columns:] = grad_up
+
+    upper = pl.BlockSpec((rows, columns), lambda i, where: (0, 0))
+    slots = saved[0].shape[1] // lax.axis_size("et")
+
+    def saved_spec(offset):
+        return pl.BlockSpec(
+            (1, count, columns),
+            lambda i, where: (0, ((where[1] ^ offset) * slots + low) // count, where[0]),
+        )
+
+    return steps.call(
+        kernel,
+        [shape(rows, 2 * columns)],
+        40 * rows * columns,
+        14 * rows * columns,
+        (1,),
+        [upper] * 3 + [saved_spec(offset) for offset in offsets for _ in range(4)],
+        [pl.BlockSpec((rows, 2 * columns), lambda i, where: (0, 0))],
+        [keep, got, last] + saved * members,
+    )[0]
+
+
+def input_terms(steps, chunk, grads, weights):
+    offsets, low, high = chunk
+    members, count = len(offsets), high - low
+    block, half = grads[0].shape[0], grads[0].shape[1] // 2
+    rows = 4 * block
+    width = weights[0].shape[0]
+    step = width // 2
+
+    def kernel(own, first_block, second_block, far_block, own_gate, own_up, other_gate, other_up, own_out, other_out, left):
+        i = pl.program_id(0)
+
+        @pl.when(i == 0)
+        def _():
+            for chip, source in enumerate((own, first_block, second_block, far_block)):
+                left[chip * block : (chip + 1) * block, :] = source[...]
+
+        def terms_of(gate, up):
+            return contract_last(left[:, :half], gate[...]) + contract_last(left[:, half:], up[...])
+
+        @pl.when(i < 2)
+        def _():
+            terms = terms_of(own_gate, own_up)
+            for q in range(members):
+                for chip in range(4):
+                    to, at = (q * 4 + chip) * 2 * count, chip * block + q * 2 * count
+                    own_out[to : to + 2 * count, :] = terms[at : at + 2 * count]
+
+        @pl.when(i >= 2)
+        def _():
+            terms = terms_of(other_gate, other_up).astype(jnp.bfloat16)
+            for q in range(members):
+                for chip in range(4):
+                    for core in range(2):
+                        to = ((q * 4 + PARTNER_CHIP[chip]) * 2 + 1 - core) * count
+                        at = chip * block + (q * 2 + core) * count
+                        other_out[to : to + count, :] = terms[at : at + count]
+
+    def first(i):
+        return jnp.minimum(i, 1)
+
+    def second(i):
+        return jnp.maximum(i - 2, 0)
+
+    own_weight = pl.BlockSpec((step, half), lambda i, where: (first(i), where[0]))
+    other_weight = pl.BlockSpec((step, half), lambda i, where: (second(i), where[0]))
+    return steps.call(
+        kernel,
+        [shape(rows, width, jnp.float32), shape(rows, width)],
+        8 * rows * width * half,
+        8 * width * half + 4 * rows * half + 6 * rows * width,
+        (4,),
+        [whole(x) for x in grads] + [own_weight] * 2 + [other_weight] * 2,
+        [
+            pl.BlockSpec((rows, step), lambda i, where: (0, first(i))),
+            pl.BlockSpec((rows, step), lambda i, where: (0, second(i))),
+        ],
+        grads + weights,
+        [pltpu.VMEM((rows, 2 * half), jnp.bfloat16)],
+    )
+
+
+def summed_terms(steps, own_terms, got, members):
+    rows, width = own_terms.shape[0] // members, own_terms.shape[1]
+
+    def kernel(own_terms, got, *outs):
+        terms = (own_terms[...] + got[...].astype(jnp.float32)).astype(jnp.bfloat16)
+        for q in range(members):
+            outs[q][...] = terms[q * rows : (q + 1) * rows]
+
+    return steps.call(
+        kernel,
+        [shape(rows, width)] * members,
+        members * rows * width,
+        8 * members * rows * width,
+        (1,),
+        [whole(own_terms), whole(got)],
+        [pl.BlockSpec((rows, width), lambda i, where: (0, 0))] * members,
+        [own_terms, got],
+    )
+
+
+def chunk_steps(steps, chunk, here, there, saved, weights, downs, slots):
+    offsets, low, high = chunk
+    send, keep = partial_sums(steps, chunk, here, there, *downs, slots)
+    got = exchange(send, 0)
+    yield
+    last = exchange(second_terms(steps, keep, got), 1)
+    yield
+    own = hidden_grads(steps, chunk, keep, got, last, saved)
+    from_second, from_first = exchange(own, 1), exchange(own, 0)
+    yield
+    far = exchange(from_second, 0)
+    steps.waits = steps.waits + [from_second]
+    yield
+    own_terms, other_terms = input_terms(steps, chunk, [own, from_first, from_second, far], weights)
+    got = swap(other_terms, "dp", 1)
+    yield
+    terms = summed_terms(steps, own_terms, got, len(offsets))
+    terms = [part if offset == 0 else swap(part, "et", offset) for offset, part in zip(offsets, terms)]
+    yield
+    steps.waits = steps.waits + terms
+    yield terms
+
+
+def per_device(out_grad, routes, gates, lengths, saved_gate, saved_up, w_gate, w_up, w_down):
+    planes = lax.axis_size("et")
+    groups = lax.axis_size("dp")
+    slots = saved_gate.shape[1] // planes
+    width = w_gate.shape[0]
+    me = lax.axis_index("dp")
+    core = me % 2
+    where = jnp.stack([core, lax.axis_index("et")]).astype(jnp.int32)
+
+    downs = [w_down, swap(w_down, "dp", 1)]
+    saved = [saved_gate, saved_up, swap(saved_gate, "dp", 1), swap(saved_up, "dp", 1)]
+    weights = [w_gate, w_up, swap(w_gate, "dp", 1), swap(w_up, "dp", 1)]
+
+    placing, coef = place_rows(routes, gates, lengths, slots)
+    scaled = (out_grad.astype(jnp.float32) * coef[:, None]).astype(jnp.bfloat16)
+    packed = jnp.dot(placing, scaled, preferred_element_type=jnp.float32).astype(jnp.bfloat16)
+    rows = lax.all_to_all(packed.reshape(slots, groups, width), "dp", split_axis=1, concat_axis=0)
+    rows = rows.reshape(groups, slots, width)
+    chips = jnp.where(core == 0, jnp.array([0, 2, 4, 6]), jnp.array([0, 4, 2, 6]))
+    place = me ^ (chips[:, None] + jnp.arange(2)[None, :]).reshape(groups)
+    inverse = jnp.where(core == 0, jnp.arange(groups), jnp.array([0, 1, 4, 5, 2, 3, 6, 7]))
+    inverse = jnp.take(inverse, me ^ jnp.arange(groups))
+    rows = jnp.take(rows, place, axis=0).reshape(1, groups * slots, width)
+
+    def here_index(offset):
+        return lambda where: 0
+
+    def plane_index(offset):
+        return lambda where: where[1] ^ offset
+
+    steps = Steps(where)
+    sources, partners = {}, {}
+    for offset in sorted({offset for offsets, _, _ in CHUNKS for offset in offsets}):
+        if offset < GATHERED:
+            source = rows if offset == 0 else swap(rows, "et", offset)
+            sources[offset] = (source, here_index(offset))
+            partners[offset] = (swap(source, "dp", 1), here_index(offset))
+    if GATHERED < planes:
+        gathered = lax.all_gather(rows, "et", axis=0, tiled=True)
+        gathered_partner = swap(gathered, "dp", 1)
+        for offset in range(GATHERED, planes):
+            sources[offset] = (gathered, plane_index(offset))
+            partners[offset] = (gathered_partner, plane_index(offset))
+    chunks = [
+        chunk_steps(
+            steps,
+            chunk,
+            [sources[offset] for offset in chunk[0]],
+            [partners[offset] for offset in chunk[0]],
+            saved,
+            weights,
+            downs,
+            slots,
+        )
+        for chunk in CHUNKS
+    ]
+    steps.waits = saved[2:] + weights[2:]
+    parts = {}
+    for k, _ in ORDER:
+        for offset, part in zip(CHUNKS[k][0], next(chunks[k]) or []):
+            parts.setdefault(offset, []).append(part.reshape(groups, -1, width))
+    total = sum(jnp.concatenate(part, axis=1).astype(jnp.float32) for part in parts.values())
+    summed = total.astype(jnp.bfloat16)
+    summed = jnp.take(summed, inverse, axis=0)
+    summed = lax.all_to_all(summed, "dp", split_axis=0, concat_axis=1)
+    summed = summed.reshape(slots, groups * width)
+    input_grad = lax.dot_general(
+        placing, summed, (((0,), (0,)), ((), ())), preferred_element_type=jnp.float32
+    )
+    return input_grad.astype(jnp.bfloat16)
+
+
 def solution(mesh):
     in_specs = (
         P(("dp", "et"), None),
@@ -82,6 +436,7 @@
         P("et", "dp"),
     )
     out_specs = P(("dp", "et"), None)
+    body = per_device if mesh.shape["dp"] == 8 and mesh.shape["et"] == 4 else plain_exchange
     return jax.shard_map(
-        per_device, mesh=mesh, in_specs=in_specs, out_specs=out_specs, check_vma=False
-    )
+        body, mesh=mesh, in_specs=in_specs, out_specs=out_specs, check_vma=False
+    )

time: 292 us -> 198 us (0.68)
  waiting for transfers between devices: 215 us -> 69.3 us
  Pallas kernels: 0 us -> 57.2 us
  starting transfers between devices: 0.31 us -> 48.9 us
  matrix products: 29.9 us -> 3.06 us
  blocking collectives: 22.6 us -> 9.35 us
  between operations: 13.2 us -> 0.37 us
  other arithmetic: 7.84 us -> 4.47 us
    all_gather x2 -> x0, waiting for transfers between devices: 117 us -> none  [the longest x1 89.8 us: per_device(): grads = lax.all_gather(grads, 'dp', axis=0)]
    reduce_scatter x2 -> x0, waiting for transfers between devices: 98.1 us -> none  [the longest x1 70.9 us: per_device(): lax.psum_scatter(partial_up, 'dp', scatter_dimension=0, tiled=True)]
    ppermute x0 -> x39, waiting for transfers between devices: none -> 62.4 us  [the longest x20 33.1 us: exchange(): lax.ppermute(values, 'dp', [(i, i ^ (2 if (i + turn) % 2 == 0 else 4)) fo...]
    pallas_call x0 -> x20, Pallas kernels: none -> 57.2 us  [call(): pl.pallas_call(ordered, out_shape=out_shape, cost_estimate=pl.CostEstimat...]
    ppermute x0 -> x39, starting transfers between devices: none -> 44 us  [the longest x19 24.4 us: swap(): return lax.ppermute(values, axis, [(i, i ^ offset) for i in range(size)])]
    dot_general x3 -> x0, matrix products: 26.9 us -> none  [contract_last(): lax.dot_general(left, right, (((axis,), (1,)), ((), ())), preferred_eleme...]
    all_to_all x1 -> x0, blocking collectives: 12 us -> none  [per_device(): lax.all_to_all(packed.reshape(slots, groups, width), 'dp', split_axis=1,...]
    all_to_all x0 -> x1, waiting for transfers between devices: none -> 6.88 us  [per_device(): lax.all_to_all(packed.reshape(slots, groups, width), 'dp', split_axis=1,...]
  transfers between devices with their start and end apart: 4 -> 40, of which waited for: 4 -> 18; matrix products, arithmetic and copies ran while one was open for 0% -> 4% of each run, Pallas kernels for 0% -> 25%
where the time goes in v3:
time: 198 us; the launch traced here: 197 us
  waiting for transfers between devices  69.3 us (35%)
  Pallas kernels  57.2 us (29%)
  starting transfers between devices  48.9 us (25%)
  blocking collectives  9.35 us (5%)
  local copies, waits for them, and re-layouts  4.76 us (2%)
  other arithmetic  4.47 us (2%)
  matrix products  3.06 us (2%)
    pallas_call x20, Pallas kernels, call(): pl.pallas_call(ordered, out_shape=out_shape, cost_estimate=pl.CostEstimat...  57.2 us
    ppermute x20, waiting for transfers between devices, exchange(): lax.ppermute(values, 'dp', [(i, i ^ (2 if (i + turn) % 2 == 0 else 4)) fo...  33.1 us
    ppermute x19, waiting for transfers between devices, swap(): return lax.ppermute(values, axis, [(i, i ^ offset) for i in range(size)])  29.3 us
    ppermute x19, starting transfers between devices, swap(): return lax.ppermute(values, axis, [(i, i ^ offset) for i in range(size)])  24.4 us
    ppermute x20, starting transfers between devices, exchange(): lax.ppermute(values, 'dp', [(i, i ^ (2 if (i + turn) % 2 == 0 else 4)) fo...  19.7 us
    all_to_all x1, blocking collectives, per_device(): summed = lax.all_to_all(summed, 'dp', split_axis=0, concat_axis=1)  9.35 us
    all_to_all x1, waiting for transfers between devices, per_device(): lax.all_to_all(packed.reshape(slots, groups, width), 'dp', split_axis=1,...  6.88 us
    all_to_all x1, starting transfers between devices, per_device(): lax.all_to_all(packed.reshape(slots, groups, width), 'dp', split_axis=1,...  4.83 us
  transfers between devices with their start and end apart: 40, of which 18 were waited for; matrix products, arithmetic and copies ran while one was open for 4% of the time, Pallas kernels for 25%

profile of v3, /device:TPU:0, one launch (start us, length us, event | category | flops | bytes accessed | tf_op | source)
XLA Modules:
  0.0 197.3 jit_solution(7745270685928304848)
XLA Ops:
  1.0 0.7 fusion.11
  2.0 0.8 reduce-window.14
  2.8 0.7 select_reduce_fusion.1
  3.5 0.7 divide_bitcast_fusion
  4.2 0.7 fusion.10
  5.0 1.6 convolution_convert_fusion.1
  6.7 0.8 copy.24
  7.5 4.8 %all-to-all-start = ((bf16[1,32,8,512]{3,1,0,2:T(8,128)(2,1)}), bf16[1,32,8,512]{3,1,0,2:T(8,128)(2,1)S(1)}, u32[]{:S(2)}, u32[]{:S(2)}) async-start(bf16[1,32,8,512]{3,1,0,2:T(8,128)(2,1)} %copy.24), calls=%async_computation | async-start | bytes 524288 | tf_op jit(solution)/shard_map/all_to_all | solution.py:370
  12.5 6.9 %all-to-all-done = bf16[1,32,8,512]{3,1,0,2:T(8,128)(2,1)S(1)} async-done(((bf16[1,32,8,512]{3,1,0,2:T(8,128)(2,1)}), bf16[1,32,8,512]{3,1,0,2:T(8,128)(2,1)S(1)}, u32[]{:S(2)}, u32[]{:S(2)}) %all-to-all-start) | async-done | bytes 262176 | tf_op jit(solution)/shard_map/all_to_all | solution.py:370
  20.7 1.0 collective-permute-done.refs_2_
  21.7 0.7 copy-done.4
  23.2 2.1 %collective-permute-done.3.refs_6_.refs_7_ = bf16[1,128,4096]{2,1,0:T(8,128)(2,1)S(1)} collective-permute-done((bf16[1,128,4096]{2,1,0:T(8,128)(2,1)}, bf16[1,128,4096]{2,1,0:T(8,128)(2,1)S(1)}, u32[]{:S(2)}, u32[]{:S(2)}) %collective-permute-start.3) | collective-permute-done | bytes 1048608 | tf_op jit(solution)/shard_map/ppermute | solution.py:86
  25.3 1.2 copy-done.5
  26.5 4.9 %shard_map.118 = (bf16[128,2048]{1,0:T(8,128)(2,1)S(1)}, bf16[128,2048]{1,0:T(8,128)(2,1)S(1)}) custom-call(s32[2]{0:T(128)S(1)} %pad_add_fusion.refs_0_, bf16[1,256,512]{2,1,0:T(8,128)(2,1)S(1)} %bitcast.41, bf16[1,256,512]{2,1,0:T(8,128)(2,1)S(1)} %copy-done.5, bf16[4096,512]{1,0:T(8,128)(2,1)} %refs_3_.7, ...), custom_call_target="tpu_custom_call" | custom-call | flops 1073741824 | bytes 5767168 | tf_op jit(solution)/shard_map/pallas_call | solution.py:116
  31.4 0.9 collective-permute-start.6
  32.3 2.6 %collective-permute-start.8 = (bf16[1,256,512]{2,1,0:T(8,128)(2,1)S(1)}, bf16[1,256,512]{2,1,0:T(8,128)(2,1)S(1)}, u32[]{:S(2)}, u32[]{:S(2)}) collective-permute-start(bf16[1,256,512]{2,1,0:T(8,128)(2,1)S(1)} %bitcast.42), channel_id=1, source_target_pairs={{0,2},{1,3},{2,0},{3,1},{4,6},{5,7},{6,4},{7,5},{8,10},{9,11},{10,... | collective-permute-start | bytes 786440 | tf_op jit(solution)/shard_map/ppermute | solution.py:86
  34.9 12.0 %collective-permute-done.8.refs_1_ = bf16[1,256,512]{2,1,0:T(8,128)(2,1)S(1)} collective-permute-done((bf16[1,256,512]{2,1,0:T(8,128)(2,1)S(1)}, bf16[1,256,512]{2,1,0:T(8,128)(2,1)S(1)}, u32[]{:S(2)}, u32[]{:S(2)}) %collective-permute-start.8) | collective-permute-done | bytes 262176 | tf_op jit(solution)/shard_map/ppermute | solution.py:86
  47.5 1.2 collective-permute-start.7
  48.8 4.2 %shard_map.120 = (bf16[128,2048]{1,0:T(8,128)(2,1)S(1)}, bf16[128,2048]{1,0:T(8,128)(2,1)S(1)}) custom-call(s32[2]{0:T(128)S(1)} %pad_add_fusion.refs_0_, bf16[1,256,512]{2,1,0:T(8,128)(2,1)S(1)} %collective-permute-done.8.refs_1_, bf16[1,256,512]{2,1,0:T(8,128)(2,1)S(1)} %collective-permute-done.9.refs_2_, bf16[4096,512]{1,0:T(8,128)(2,1)S(1)} %copy-done, ...), custom_call_target="tpu_custom_call" | custom-call | flops 1073741824 | bytes 5767168 | tf_op jit(solution)/shard_map/pallas_call | solution.py:116
  53.0 1.2 collective-permute-start.17
  54.2 3.5 %collective-permute-start.15 = (bf16[1,256,512]{2,1,0:T(8,128)(2,1)S(1)}, bf16[1,256,512]{2,1,0:T(8,128)(2,1)S(1)}, u32[]{:S(2)}, u32[]{:S(2)}) collective-permute-start(bf16[1,256,512]{2,1,0:T(8,128)(2,1)S(1)} %bitcast.43), channel_id=1, source_target_pairs={{0,3},{1,2},{2,1},{3,0},{4,7},{5,6},{6,5},{7,4},{8,11},{9,10},{10,... | collective-permute-start | bytes 786440 | tf_op jit(solution)/shard_map/ppermute | solution.py:86
  57.7 1.8 shard_map.121.refs_3_.refs_1_
  59.5 1.3 collective-permute-start.11
  60.9 3.1 %collective-permute-done.15.refs_1_ = bf16[1,256,512]{2,1,0:T(8,128)(2,1)S(1)} collective-permute-done((bf16[1,256,512]{2,1,0:T(8,128)(2,1)S(1)}, bf16[1,256,512]{2,1,0:T(8,128)(2,1)S(1)}, u32[]{:S(2)}, u32[]{:S(2)}) %collective-permute-start.15) | collective-permute-done | bytes 262176 | tf_op jit(solution)/shard_map/ppermute | solution.py:86
  64.6 1.6 collective-permute-start.19
  66.2 4.2 %shard_map.123 = (bf16[128,2048]{1,0:T(8,128)(2,1)S(1)}, bf16[128,2048]{1,0:T(8,128)(2,1)S(1)}) custom-call(s32[2]{0:T(128)S(1)} %pad_add_fusion.refs_0_, bf16[1,256,512]{2,1,0:T(8,128)(2,1)S(1)} %collective-permute-done.15.refs_1_, bf16[1,256,512]{2,1,0:T(8,128)(2,1)S(1)} %collective-permute-done.16.refs_2_, bf16[4096,512]{1,0:T(8,128)(2,1)S(1)} %copy-done, ...), custom_call_target="tpu_custom_call" | custom-call | flops 1073741824 | bytes 5767168 | tf_op jit(solution)/shard_map/pallas_call | solution.py:116
  70.4 0.8 collective-permute-start.18
  71.2 4.4 %collective-permute-start.13 = (bf16[1,256,512]{2,1,0:T(8,128)(2,1)S(1)}, bf16[1,256,512]{2,1,0:T(8,128)(2,1)S(1)}, u32[]{:S(2)}, u32[]{:S(2)}) collective-permute-start(bf16[1,256,512]{2,1,0:T(8,128)(2,1)S(1)} %bitcast.44), channel_id=1, source_target_pairs={{0,1},{1,0},{2,3},{3,2},{4,5},{5,4},{6,7},{7,6},{8,9},{9,8},{10,11... | collective-permute-start | bytes 786440 | tf_op jit(solution)/shard_map/ppermute | solution.py:86
  75.6 1.3 collective-permute-start.10
  76.9 1.8 shard_map.124.refs_3_.refs_1_
  78.7 0.9 collective-permute-start.20
  79.7 0.7 collective-permute-start.12
  80.4 1.7 collective-permute-done.13.refs_1_
  82.1 1.3 collective-permute-start.24
  84.5 4.2 %shard_map.126 = (bf16[128,2048]{1,0:T(8,128)(2,1)S(1)}, bf16[128,2048]{1,0:T(8,128)(2,1)S(1)}) custom-call(s32[2]{0:T(128)S(1)} %pad_add_fusion.refs_0_, bf16[1,256,512]{2,1,0:T(8,128)(2,1)S(1)} %collective-permute-done.13.refs_1_, bf16[1,256,512]{2,1,0:T(8,128)(2,1)S(1)} %collective-permute-done.14.refs_2_, bf16[4096,512]{1,0:T(8,128)(2,1)S(1)} %copy-done, ...), custom_call_target="tpu_custom_call" | custom-call | flops 1073741824 | bytes 5767168 | tf_op jit(solution)/shard_map/pallas_call | solution.py:116
  88.8 1.4 collective-permute-done.10.refs_2_
  90.2 0.7 collective-permute-start.22
  91.0 2.7 %collective-permute-done.20.refs_10_.refs_3_ = bf16[64,4096]{1,0:T(8,128)(2,1)S(1)} collective-permute-done((bf16[64,4096]{1,0:T(8,128)(2,1)S(1)}, bf16[64,4096]{1,0:T(8,128)(2,1)S(1)}, u32[]{:S(2)}, u32[]{:S(2)}) %collective-permute-start.20) | collective-permute-done | bytes 524320 | tf_op jit(solution)/shard_map/ppermute | solution.py:91
  93.7 5.7 %collective-permute-done.12.refs_4_ = bf16[64,4096]{1,0:T(8,128)(2,1)S(1)} collective-permute-done((bf16[64,4096]{1,0:T(8,128)(2,1)S(1)}, bf16[64,4096]{1,0:T(8,128)(2,1)S(1)}, u32[]{:S(2)}, u32[]{:S(2)}) %collective-permute-start.12) | collective-permute-done | bytes 524320 | tf_op jit(solution)/shard_map/ppermute | solution.py:91
  99.3 6.9 %shard_map.127 = (f32[256,512]{1,0:T(8,128)S(1)}, bf16[256,512]{1,0:T(8,128)(2,1)S(1)}) custom-call(s32[2]{0:T(128)S(1)} %pad_add_fusion.refs_0_, bf16[64,4096]{1,0:T(8,128)(2,1)S(1)} %shard_map.121.refs_3_.refs_1_, bf16[64,4096]{1,0:T(8,128)(2,1)S(1)} %collective-permute-done.10.refs_2_, bf16[64,4096]{1,0:T(8,128)(2,1)S(1)} %collective-permute-done.11.refs_9_.refs_3_, ...), custom_call_target="tpu_custom_call" | custom-call | flops 2147483648 | bytes 11272192 | tf_op jit(solution)/shard_map/pallas_call | solution.py:116
  106.2 1.8 shard_map.128.refs_3_.refs_1_
  108.1 0.9 collective-permute-start.26
  109.0 0.8 collective-permute-start.25
  109.8 2.5 %collective-permute-done.22.refs_2_ = bf16[128,2048]{1,0:T(8,128)(2,1)S(1)} collective-permute-done((bf16[128,2048]{1,0:T(8,128)(2,1)S(1)}, bf16[128,2048]{1,0:T(8,128)(2,1)S(1)}, u32[]{:S(2)}, u32[]{:S(2)}) %collective-permute-start.22) | collective-permute-done | bytes 524320 | tf_op jit(solution)/shard_map/ppermute | solution.py:91
  114.0 7.1 %collective-permute-done.26.refs_10_.refs_3_ = bf16[64,4096]{1,0:T(8,128)(2,1)S(1)} collective-permute-done((bf16[64,4096]{1,0:T(8,128)(2,1)S(1)}, bf16[64,4096]{1,0:T(8,128)(2,1)S(1)}, u32[]{:S(2)}, u32[]{:S(2)}) %collective-permute-start.26) | collective-permute-done | bytes 524320 | tf_op jit(solution)/shard_map/ppermute | solution.py:91
  121.0 2.8 %collective-permute-done.25.refs_4_ = bf16[64,4096]{1,0:T(8,128)(2,1)S(1)} collective-permute-done((bf16[64,4096]{1,0:T(8,128)(2,1)S(1)}, bf16[64,4096]{1,0:T(8,128)(2,1)S(1)}, u32[]{:S(2)}, u32[]{:S(2)}) %collective-permute-start.25) | collective-permute-done | bytes 524320 | tf_op jit(solution)/shard_map/ppermute | solution.py:91
  123.8 6.9 %shard_map.131 = (f32[256,512]{1,0:T(8,128)S(1)}, bf16[256,512]{1,0:T(8,128)(2,1)S(1)}) custom-call(s32[2]{0:T(128)S(1)} %pad_add_fusion.refs_0_, bf16[64,4096]{1,0:T(8,128)(2,1)S(1)} %shard_map.124.refs_3_.refs_1_, bf16[64,4096]{1,0:T(8,128)(2,1)S(1)} %collective-permute-done.24.refs_2_, bf16[64,4096]{1,0:T(8,128)(2,1)S(1)} %collective-permute-done.20.refs_10_.refs_3_, ...), custom_call_target="tpu_custom_call" | custom-call | flops 2147483648 | bytes 11272192 | tf_op jit(solution)/shard_map/pallas_call | solution.py:116
  130.7 1.8 shard_map.132.refs_3_.refs_1_
  132.6 1.2 collective-permute-start.32
  133.8 0.8 collective-permute-start.30
  134.6 1.2 collective-permute-start.31
  135.8 0.8 collective-permute-start.35
  136.6 10.8 %collective-permute-done.32.refs_10_.refs_3_ = bf16[64,4096]{1,0:T(8,128)(2,1)S(1)} collective-permute-done((bf16[64,4096]{1,0:T(8,128)(2,1)S(1)}, bf16[64,4096]{1,0:T(8,128)(2,1)S(1)}, u32[]{:S(2)}, u32[]{:S(2)}) %collective-permute-start.32) | collective-permute-done | bytes 524320 | tf_op jit(solution)/shard_map/ppermute | solution.py:91
  147.5 0.8 collective-permute-start.36
  148.9 4.1 %collective-permute-start.29 = (bf16[256,512]{1,0:T(8,128)(2,1)S(1)}, bf16[256,512]{1,0:T(8,128)(2,1)S(1)}, u32[]{:S(2)}, u32[]{:S(2)}) collective-permute-start(bf16[256,512]{1,0:T(8,128)(2,1)S(1)} %shard_map.133.refs_9_), channel_id=1, source_target_pairs={{0,2},{1,3},{2,0},{3,1},{4,6},{5,7},{6,4},{7,5},{8,10},{9,11},{10,... | collective-permute-start | bytes 786440 | tf_op jit(solution)/shard_map/ppermute | solution.py:86
  153.0 6.9 %shard_map.134 = (f32[256,512]{1,0:T(8,128)S(1)}, bf16[256,512]{1,0:T(8,128)(2,1)S(1)}) custom-call(s32[2]{0:T(128)S(1)} %pad_add_fusion.refs_0_, bf16[64,4096]{1,0:T(8,128)(2,1)S(1)} %shard_map.128.refs_3_.refs_1_, bf16[64,4096]{1,0:T(8,128)(2,1)S(1)} %collective-permute-done.30.refs_2_, bf16[64,4096]{1,0:T(8,128)(2,1)S(1)} %collective-permute-done.26.refs_10_.refs_3_, ...), custom_call_target="tpu_custom_call" | custom-call | flops 2147483648 | bytes 11272192 | tf_op jit(solution)/shard_map/pallas_call | solution.py:116
  160.2 1.3 collective-permute-done.33.refs_2_
  162.1 2.7 %collective-permute-start.34 = (bf16[256,512]{1,0:T(8,128)(2,1)S(1)}, bf16[256,512]{1,0:T(8,128)(2,1)S(1)}, u32[]{:S(2)}, u32[]{:S(2)}) collective-permute-start(bf16[256,512]{1,0:T(8,128)(2,1)S(1)} %shard_map.135.refs_9_), channel_id=1, source_target_pairs={{0,3},{1,2},{2,1},{3,0},{4,7},{5,6},{6,5},{7,4},{8,11},{9,10},{10,... | collective-permute-start | bytes 786440 | tf_op jit(solution)/shard_map/ppermute | solution.py:86
  164.8 6.9 %shard_map.136 = (f32[256,512]{1,0:T(8,128)S(1)}, bf16[256,512]{1,0:T(8,128)(2,1)S(1)}) custom-call(s32[2]{0:T(128)S(1)} %pad_add_fusion.refs_0_, bf16[64,4096]{1,0:T(8,128)(2,1)S(1)} %shard_map.132.refs_3_.refs_1_, bf16[64,4096]{1,0:T(8,128)(2,1)S(1)} %collective-permute-done.35.refs_2_, bf16[64,4096]{1,0:T(8,128)(2,1)S(1)} %collective-permute-done.32.refs_10_.refs_3_, ...), custom_call_target="tpu_custom_call" | custom-call | flops 2147483648 | bytes 11272192 | tf_op jit(solution)/shard_map/pallas_call | solution.py:116
  172.5 0.8 collective-permute-done.37.refs_2_
  173.9 5.3 %collective-permute-start.38 = (bf16[256,512]{1,0:T(8,128)(2,1)S(1)}, bf16[256,512]{1,0:T(8,128)(2,1)S(1)}, u32[]{:S(2)}, u32[]{:S(2)}) collective-permute-start(bf16[256,512]{1,0:T(8,128)(2,1)S(1)} %shard_map.137), channel_id=1, source_target_pairs={{0,1},{1,0},{2,3},{3,2},{4,5},{5,4},{6,7},{7,6},{8,9},{9,8},{10,11... | collective-permute-start | bytes 786440 | tf_op jit(solution)/shard_map/ppermute | solution.py:86
  179.2 6.5 %collective-permute-done.38 = bf16[256,512]{1,0:T(8,128)(2,1)S(1)} collective-permute-done((bf16[256,512]{1,0:T(8,128)(2,1)S(1)}, bf16[256,512]{1,0:T(8,128)(2,1)S(1)}, u32[]{:S(2)}, u32[]{:S(2)}) %collective-permute-start.38) | collective-permute-done | bytes 262176 | tf_op jit(solution)/shard_map/ppermute | solution.py:86
  186.5 9.3 %all_to_all.30 = bf16[8,32,1,512]{3,1,2,0:T(8,128)(2,1)S(1)} all-to-all(bf16[8,32,1,512]{3,1,2,0:T(8,128)(2,1)S(1)} %select_bitcast_fusion), channel_id=1, replica_groups=mesh['dp'=8,'et'=4] {'dp'}, dimensions={0} | all-to-all | bytes 524288 | tf_op jit(solution)/shard_map/all_to_all | solution.py:418
  195.9 1.5 convolution_convert_fusion
  (85 shorter events, 11.3 us)
Async XLA Ops:
  0.0 20.3 %copy-start.2 = (bf16[1,128,4096]{2,1,0:T(8,128)(2,1)S(1)}, bf16[1,128,4096]{2,1,0:T(8,128)(2,1)}, u32[]{:S(2)}) copy-start(bf16[1,128,4096]{2,1,0:T(8,128)(2,1)} %refs_4_.7) | copy-start | bytes 3145732
  0.0 25.3 %collective-permute-start.4 = (bf16[512,4096]{1,0:T(8,128)(2,1)}, bf16[512,4096]{1,0:T(8,128)(2,1)}, u32[]{:S(2)}, u32[]{:S(2)}) collective-permute-start(bf16[512,4096]{1,0:T(8,128)(2,1)} %refs_5_.15), channel_id=1, source_target_pairs={{0,4},{4,0},{8,12},{12,8},{16,20},{20,16},{24,28},{28,24},{1,5},{5... | collective-permute-start | bytes 12582920 | tf_op jit(solution)/shard_map/ppermute | solution.py:86
  0.5 24.8 %collective-permute-start.5 = (bf16[512,4096]{1,0:T(8,128)(2,1)}, bf16[512,4096]{1,0:T(8,128)(2,1)}, u32[]{:S(2)}, u32[]{:S(2)}) collective-permute-start(bf16[512,4096]{1,0:T(8,128)(2,1)} %refs_6_.7), channel_id=1, source_target_pairs={{0,4},{4,0},{8,12},{12,8},{16,20},{20,16},{24,28},{28,24},{1,5},{5... | collective-permute-start | bytes 12582920 | tf_op jit(solution)/shard_map/ppermute | solution.py:86
  0.5 24.8 %collective-permute-start.1 = (bf16[4096,512]{1,0:T(8,128)(2,1)}, bf16[4096,512]{1,0:T(8,128)(2,1)}, u32[]{:S(2)}, u32[]{:S(2)}) collective-permute-start(bf16[4096,512]{1,0:T(8,128)(2,1)} %refs_3_.7), channel_id=1, source_target_pairs={{0,4},{4,0},{8,12},{12,8},{16,20},{20,16},{24,28},{28,24},{1,5},{5... | collective-permute-start | bytes 12582920 | tf_op jit(solution)/shard_map/ppermute | solution.py:86
  7.5 11.9 %all-to-all-start = ((bf16[1,32,8,512]{3,1,0,2:T(8,128)(2,1)}), bf16[1,32,8,512]{3,1,0,2:T(8,128)(2,1)S(1)}, u32[]{:S(2)}, u32[]{:S(2)}) async-start(bf16[1,32,8,512]{3,1,0,2:T(8,128)(2,1)} %copy.24), calls=%async_computation | async-start | bytes 524288 | tf_op jit(solution)/shard_map/all_to_all | solution.py:370
  20.1 1.6 collective-permute-start
  20.3 2.9 %collective-permute-start.2 = (bf16[1,128,4096]{2,1,0:T(8,128)(2,1)S(1)}, bf16[1,128,4096]{2,1,0:T(8,128)(2,1)S(1)}, u32[]{:S(2)}, u32[]{:S(2)}) collective-permute-start(bf16[1,128,4096]{2,1,0:T(8,128)(2,1)S(1)} %copy-done.2), channel_id=1, source_target_pairs={{0,4},{4,0},{8,12},{12,8},{16,20},{20,16},{24,28},{28,24},{1,5},{5... | collective-permute-start | bytes 3145736 | tf_op jit(solution)/shard_map/ppermute | solution.py:86
  21.7 0.7 copy-start.4
  22.4 2.9 %collective-permute-start.3 = (bf16[1,128,4096]{2,1,0:T(8,128)(2,1)}, bf16[1,128,4096]{2,1,0:T(8,128)(2,1)S(1)}, u32[]{:S(2)}, u32[]{:S(2)}) collective-permute-start(bf16[1,128,4096]{2,1,0:T(8,128)(2,1)} %refs_5_.13), channel_id=1, source_target_pairs={{0,4},{4,0},{8,12},{12,8},{16,20},{20,16},{24,28},{28,24},{1,5},{5... | collective-permute-start | bytes 3145736 | tf_op jit(solution)/shard_map/ppermute | solution.py:86
  25.3 6.1 %copy-start.1 = (bf16[1,128,4096]{2,1,0:T(8,128)(2,1)}, bf16[1,128,4096]{2,1,0:T(8,128)(2,1)S(1)}, u32[]{:S(2)}) copy-start(bf16[1,128,4096]{2,1,0:T(8,128)(2,1)S(1)} %collective-permute-done.3.refs_6_.refs_7_) | copy-start | bytes 3145732
  25.3 1.2 copy-start.5
  26.5 22.3 %copy-start = (bf16[4096,512]{1,0:T(8,128)(2,1)S(1)}, bf16[4096,512]{1,0:T(8,128)(2,1)}, u32[]{:S(2)}) copy-start(bf16[4096,512]{1,0:T(8,128)(2,1)} %refs_3_.7) | copy-start | bytes 12582916
  31.4 15.5 %collective-permute-start.6 = (bf16[128,2048]{1,0:T(8,128)(2,1)S(1)}, bf16[128,2048]{1,0:T(8,128)(2,1)S(1)}, u32[]{:S(2)}, u32[]{:S(2)}) collective-permute-start(bf16[128,2048]{1,0:T(8,128)(2,1)S(1)} %get-tuple-element.23.refs_3_), channel_id=1, source_target_pairs={{0,8},{4,20},{8,0},{12,28},{16,24},{20,4},{24,16},{28,12},{1,9},{5... | collective-permute-start | bytes 1572872 | tf_op jit(solution)/shard_map/ppermute | solution.py:91
  32.3 14.6 %collective-permute-start.8 = (bf16[1,256,512]{2,1,0:T(8,128)(2,1)S(1)}, bf16[1,256,512]{2,1,0:T(8,128)(2,1)S(1)}, u32[]{:S(2)}, u32[]{:S(2)}) collective-permute-start(bf16[1,256,512]{2,1,0:T(8,128)(2,1)S(1)} %bitcast.42), channel_id=1, source_target_pairs={{0,2},{1,3},{2,0},{3,1},{4,6},{5,7},{6,4},{7,5},{8,10},{9,11},{10,... | collective-permute-start | bytes 786440 | tf_op jit(solution)/shard_map/ppermute | solution.py:86
  46.9 1.9 collective-permute-start.9
  47.5 10.2 %copy-start.3 = (bf16[1,128,4096]{2,1,0:T(8,128)(2,1)S(1)}, bf16[1,128,4096]{2,1,0:T(8,128)(2,1)}, u32[]{:S(2)}) copy-start(bf16[1,128,4096]{2,1,0:T(8,128)(2,1)} %refs_5_.13) | copy-start | bytes 3145732
  47.5 10.2 %collective-permute-start.7 = (bf16[64,2048]{1,0:T(8,128)(2,1)S(1)}, bf16[64,2048]{1,0:T(8,128)(2,1)S(1)}, u32[]{:S(2)}, u32[]{:S(2)}) collective-permute-start(bf16[64,2048]{1,0:T(8,128)(2,1)S(1)} %shard_map.119.refs_5_), channel_id=1, source_target_pairs={{0,16},{4,12},{8,24},{12,4},{16,0},{20,28},{24,8},{28,20},{1,17},{... | collective-permute-start | bytes 786440 | tf_op jit(solution)/shard_map/ppermute | solution.py:91
  53.0 11.0 %collective-permute-start.17 = (bf16[128,2048]{1,0:T(8,128)(2,1)S(1)}, bf16[128,2048]{1,0:T(8,128)(2,1)S(1)}, u32[]{:S(2)}, u32[]{:S(2)}) collective-permute-start(bf16[128,2048]{1,0:T(8,128)(2,1)S(1)} %get-tuple-element.24.refs_8_), channel_id=1, source_target_pairs={{0,8},{4,20},{8,0},{12,28},{16,24},{20,4},{24,16},{28,12},{1,9},{5... | collective-permute-start | bytes 1572872 | tf_op jit(solution)/shard_map/ppermute | solution.py:91
  54.2 9.7 %collective-permute-start.15 = (bf16[1,256,512]{2,1,0:T(8,128)(2,1)S(1)}, bf16[1,256,512]{2,1,0:T(8,128)(2,1)S(1)}, u32[]{:S(2)}, u32[]{:S(2)}) collective-permute-start(bf16[1,256,512]{2,1,0:T(8,128)(2,1)S(1)} %bitcast.43), channel_id=1, source_target_pairs={{0,3},{1,2},{2,1},{3,0},{4,7},{5,6},{6,5},{7,4},{8,11},{9,10},{10,... | collective-permute-start | bytes 786440 | tf_op jit(solution)/shard_map/ppermute | solution.py:86
  59.5 17.4 %collective-permute-start.11 = (bf16[64,4096]{1,0:T(8,128)(2,1)S(1)}, bf16[64,4096]{1,0:T(8,128)(2,1)S(1)}, u32[]{:S(2)}, u32[]{:S(2)}) collective-permute-start(bf16[64,4096]{1,0:T(8,128)(2,1)S(1)} %shard_map.121.refs_3_.refs_1_), channel_id=1, source_target_pairs={{0,16},{4,12},{8,24},{12,4},{16,0},{20,28},{24,8},{28,20},{1,17},{... | collective-permute-start | bytes 1572872 | tf_op jit(solution)/shard_map/ppermute | solution.py:91
  64.0 2.2 %collective-permute-start.16 = (bf16[1,256,512]{2,1,0:T(8,128)(2,1)S(1)}, bf16[1,256,512]{2,1,0:T(8,128)(2,1)S(1)}, u32[]{:S(2)}, u32[]{:S(2)}) collective-permute-start(bf16[1,256,512]{2,1,0:T(8,128)(2,1)S(1)} %collective-permute-done.15.refs_1_), channel_id=1, source_target_pairs={{0,4},{4,0},{8,12},{12,8},{16,20},{20,16},{24,28},{28,24},{1,5},{5... | collective-permute-start | bytes 786440 | tf_op jit(solution)/shard_map/ppermute | solution.py:86
  64.6 12.3 %collective-permute-start.19 = (bf16[64,2048]{1,0:T(8,128)(2,1)S(1)}, bf16[64,2048]{1,0:T(8,128)(2,1)S(1)}, u32[]{:S(2)}, u32[]{:S(2)}) collective-permute-start(bf16[64,2048]{1,0:T(8,128)(2,1)S(1)} %shard_map.122.refs_5_), channel_id=1, source_target_pairs={{0,16},{4,12},{8,24},{12,4},{16,0},{20,28},{24,8},{28,20},{1,17},{... | collective-permute-start | bytes 786440 | tf_op jit(solution)/shard_map/ppermute | solution.py:91
  70.4 11.7 %collective-permute-start.18 = (bf16[128,2048]{1,0:T(8,128)(2,1)S(1)}, bf16[128,2048]{1,0:T(8,128)(2,1)S(1)}, u32[]{:S(2)}, u32[]{:S(2)}) collective-permute-start(bf16[128,2048]{1,0:T(8,128)(2,1)S(1)} %get-tuple-element.27.refs_8_), channel_id=1, source_target_pairs={{0,8},{4,20},{8,0},{12,28},{16,24},{20,4},{24,16},{28,12},{1,9},{5... | collective-permute-start | bytes 1572872 | tf_op jit(solution)/shard_map/ppermute | solution.py:91
  71.2 10.8 %collective-permute-start.13 = (bf16[1,256,512]{2,1,0:T(8,128)(2,1)S(1)}, bf16[1,256,512]{2,1,0:T(8,128)(2,1)S(1)}, u32[]{:S(2)}, u32[]{:S(2)}) collective-permute-start(bf16[1,256,512]{2,1,0:T(8,128)(2,1)S(1)} %bitcast.44), channel_id=1, source_target_pairs={{0,1},{1,0},{2,3},{3,2},{4,5},{5,4},{6,7},{7,6},{8,9},{9,8},{10,11... | collective-permute-start | bytes 786440 | tf_op jit(solution)/shard_map/ppermute | solution.py:86
  75.6 14.6 %collective-permute-start.10 = (bf16[64,4096]{1,0:T(8,128)(2,1)S(1)}, bf16[64,4096]{1,0:T(8,128)(2,1)S(1)}, u32[]{:S(2)}, u32[]{:S(2)}) collective-permute-start(bf16[64,4096]{1,0:T(8,128)(2,1)S(1)} %shard_map.121.refs_3_.refs_1_), channel_id=1, source_target_pairs={{0,8},{4,20},{8,0},{12,28},{16,24},{20,4},{24,16},{28,12},{1,9},{5... | collective-permute-start | bytes 1572872 | tf_op jit(solution)/shard_map/ppermute | solution.py:91
  78.7 14.9 %collective-permute-start.20 = (bf16[64,4096]{1,0:T(8,128)(2,1)S(1)}, bf16[64,4096]{1,0:T(8,128)(2,1)S(1)}, u32[]{:S(2)}, u32[]{:S(2)}) collective-permute-start(bf16[64,4096]{1,0:T(8,128)(2,1)S(1)} %shard_map.124.refs_3_.refs_1_), channel_id=1, source_target_pairs={{0,16},{4,12},{8,24},{12,4},{16,0},{20,28},{24,8},{28,20},{1,17},{... | collective-permute-start | bytes 1572872 | tf_op jit(solution)/shard_map/ppermute | solution.py:91
  79.7 19.7 %collective-permute-start.12 = (bf16[64,4096]{1,0:T(8,128)(2,1)S(1)}, bf16[64,4096]{1,0:T(8,128)(2,1)S(1)}, u32[]{:S(2)}, u32[]{:S(2)}) collective-permute-start(bf16[64,4096]{1,0:T(8,128)(2,1)S(1)} %collective-permute-done.11.refs_9_.refs_3_), channel_id=1, source_target_pairs={{0,8},{4,20},{8,0},{12,28},{16,24},{20,4},{24,16},{28,12},{1,9},{5... | collective-permute-start | bytes 1572872 | tf_op jit(solution)/shard_map/ppermute | solution.py:91
  82.1 1.9 collective-permute-start.14
  82.1 31.9 %collective-permute-start.24 = (bf16[64,4096]{1,0:T(8,128)(2,1)S(1)}, bf16[64,4096]{1,0:T(8,128)(2,1)S(1)}, u32[]{:S(2)}, u32[]{:S(2)}) collective-permute-start(bf16[64,4096]{1,0:T(8,128)(2,1)S(1)} %shard_map.124.refs_3_.refs_1_), channel_id=1, source_target_pairs={{0,8},{4,20},{8,0},{12,28},{16,24},{20,4},{24,16},{28,12},{1,9},{5... | collective-permute-start | bytes 1572872 | tf_op jit(solution)/shard_map/ppermute | solution.py:91
  84.0 22.3 %collective-permute-start.23 = (bf16[64,2048]{1,0:T(8,128)(2,1)S(1)}, bf16[64,2048]{1,0:T(8,128)(2,1)S(1)}, u32[]{:S(2)}, u32[]{:S(2)}) collective-permute-start(bf16[64,2048]{1,0:T(8,128)(2,1)S(1)} %shard_map.125.refs_5_), channel_id=1, source_target_pairs={{0,16},{4,12},{8,24},{12,4},{16,0},{20,28},{24,8},{28,20},{1,17},{... | collective-permute-start | bytes 786440 | tf_op jit(solution)/shard_map/ppermute | solution.py:91
  90.2 22.1 %collective-permute-start.22 = (bf16[128,2048]{1,0:T(8,128)(2,1)S(1)}, bf16[128,2048]{1,0:T(8,128)(2,1)S(1)}, u32[]{:S(2)}, u32[]{:S(2)}) collective-permute-start(bf16[128,2048]{1,0:T(8,128)(2,1)S(1)} %get-tuple-element.28.refs_9_), channel_id=1, source_target_pairs={{0,8},{4,20},{8,0},{12,28},{16,24},{20,4},{24,16},{28,12},{1,9},{5... | collective-permute-start | bytes 1572872 | tf_op jit(solution)/shard_map/ppermute | solution.py:91
  108.1 13.0 %collective-permute-start.26 = (bf16[64,4096]{1,0:T(8,128)(2,1)S(1)}, bf16[64,4096]{1,0:T(8,128)(2,1)S(1)}, u32[]{:S(2)}, u32[]{:S(2)}) collective-permute-start(bf16[64,4096]{1,0:T(8,128)(2,1)S(1)} %shard_map.128.refs_3_.refs_1_), channel_id=1, source_target_pairs={{0,16},{4,12},{8,24},{12,4},{16,0},{20,28},{24,8},{28,20},{1,17},{... | collective-permute-start | bytes 1572872 | tf_op jit(solution)/shard_map/ppermute | solution.py:91
  109.0 14.9 %collective-permute-start.25 = (bf16[64,4096]{1,0:T(8,128)(2,1)S(1)}, bf16[64,4096]{1,0:T(8,128)(2,1)S(1)}, u32[]{:S(2)}, u32[]{:S(2)}) collective-permute-start(bf16[64,4096]{1,0:T(8,128)(2,1)S(1)} %collective-permute-done.20.refs_10_.refs_3_), channel_id=1, source_target_pairs={{0,8},{4,20},{8,0},{12,28},{16,24},{20,4},{24,16},{28,12},{1,9},{5... | collective-permute-start | bytes 1572872 | tf_op jit(solution)/shard_map/ppermute | solution.py:91
  109.8 3.5 %collective-permute-start.21 = (bf16[256,512]{1,0:T(8,128)(2,1)S(1)}, bf16[256,512]{1,0:T(8,128)(2,1)S(1)}, u32[]{:S(2)}, u32[]{:S(2)}) collective-permute-start(bf16[256,512]{1,0:T(8,128)(2,1)S(1)} %get-tuple-element.30), channel_id=1, source_target_pairs={{0,4},{4,0},{8,12},{12,8},{16,20},{20,16},{24,28},{28,24},{1,5},{5... | collective-permute-start | bytes 786440 | tf_op jit(solution)/shard_map/ppermute | solution.py:86
  112.9 17.8 %collective-permute-start.28 = (bf16[64,2048]{1,0:T(8,128)(2,1)S(1)}, bf16[64,2048]{1,0:T(8,128)(2,1)S(1)}, u32[]{:S(2)}, u32[]{:S(2)}) collective-permute-start(bf16[64,2048]{1,0:T(8,128)(2,1)S(1)} %shard_map.129.refs_3_), channel_id=1, source_target_pairs={{0,16},{4,12},{8,24},{12,4},{16,0},{20,28},{24,8},{28,20},{1,17},{... | collective-permute-start | bytes 786440 | tf_op jit(solution)/shard_map/ppermute | solution.py:91
  132.6 14.9 %collective-permute-start.32 = (bf16[64,4096]{1,0:T(8,128)(2,1)S(1)}, bf16[64,4096]{1,0:T(8,128)(2,1)S(1)}, u32[]{:S(2)}, u32[]{:S(2)}) collective-permute-start(bf16[64,4096]{1,0:T(8,128)(2,1)S(1)} %shard_map.132.refs_3_.refs_1_), channel_id=1, source_target_pairs={{0,16},{4,12},{8,24},{12,4},{16,0},{20,28},{24,8},{28,20},{1,17},{... | collective-permute-start | bytes 1572872 | tf_op jit(solution)/shard_map/ppermute | solution.py:91
  133.8 19.2 %collective-permute-start.30 = (bf16[64,4096]{1,0:T(8,128)(2,1)S(1)}, bf16[64,4096]{1,0:T(8,128)(2,1)S(1)}, u32[]{:S(2)}, u32[]{:S(2)}) collective-permute-start(bf16[64,4096]{1,0:T(8,128)(2,1)S(1)} %shard_map.128.refs_3_.refs_1_), channel_id=1, source_target_pairs={{0,8},{4,20},{8,0},{12,28},{16,24},{20,4},{24,16},{28,12},{1,9},{5... | collective-permute-start | bytes 1572872 | tf_op jit(solution)/shard_map/ppermute | solution.py:91
  134.6 18.4 %collective-permute-start.31 = (bf16[64,4096]{1,0:T(8,128)(2,1)S(1)}, bf16[64,4096]{1,0:T(8,128)(2,1)S(1)}, u32[]{:S(2)}, u32[]{:S(2)}) collective-permute-start(bf16[64,4096]{1,0:T(8,128)(2,1)S(1)} %collective-permute-done.26.refs_10_.refs_3_), channel_id=1, source_target_pairs={{0,8},{4,20},{8,0},{12,28},{16,24},{20,4},{24,16},{28,12},{1,9},{5... | collective-permute-start | bytes 1572872 | tf_op jit(solution)/shard_map/ppermute | solution.py:91
  135.8 12.5 %collective-permute-start.27 = (bf16[256,512]{1,0:T(8,128)(2,1)S(1)}, bf16[256,512]{1,0:T(8,128)(2,1)S(1)}, u32[]{:S(2)}, u32[]{:S(2)}) collective-permute-start(bf16[256,512]{1,0:T(8,128)(2,1)S(1)} %get-tuple-element.33), channel_id=1, source_target_pairs={{0,4},{4,0},{8,12},{12,8},{16,20},{20,16},{24,28},{28,24},{1,5},{5... | collective-permute-start | bytes 786440 | tf_op jit(solution)/shard_map/ppermute | solution.py:86
  135.8 29.0 %collective-permute-start.35 = (bf16[64,4096]{1,0:T(8,128)(2,1)S(1)}, bf16[64,4096]{1,0:T(8,128)(2,1)S(1)}, u32[]{:S(2)}, u32[]{:S(2)}) collective-permute-start(bf16[64,4096]{1,0:T(8,128)(2,1)S(1)} %shard_map.132.refs_3_.refs_1_), channel_id=1, source_target_pairs={{0,8},{4,20},{8,0},{12,28},{16,24},{20,4},{24,16},{28,12},{1,9},{5... | collective-permute-start | bytes 1572872 | tf_op jit(solution)/shard_map/ppermute | solution.py:91
  147.5 17.4 %collective-permute-start.36 = (bf16[64,4096]{1,0:T(8,128)(2,1)S(1)}, bf16[64,4096]{1,0:T(8,128)(2,1)S(1)}, u32[]{:S(2)}, u32[]{:S(2)}) collective-permute-start(bf16[64,4096]{1,0:T(8,128)(2,1)S(1)} %collective-permute-done.32.refs_10_.refs_3_), channel_id=1, source_target_pairs={{0,8},{4,20},{8,0},{12,28},{16,24},{20,4},{24,16},{28,12},{1,9},{5... | collective-permute-start | bytes 1572872 | tf_op jit(solution)/shard_map/ppermute | solution.py:91
  148.9 11.3 %collective-permute-start.29 = (bf16[256,512]{1,0:T(8,128)(2,1)S(1)}, bf16[256,512]{1,0:T(8,128)(2,1)S(1)}, u32[]{:S(2)}, u32[]{:S(2)}) collective-permute-start(bf16[256,512]{1,0:T(8,128)(2,1)S(1)} %shard_map.133.refs_9_), channel_id=1, source_target_pairs={{0,2},{1,3},{2,0},{3,1},{4,6},{5,7},{6,4},{7,5},{8,10},{9,11},{10,... | collective-permute-start | bytes 786440 | tf_op jit(solution)/shard_map/ppermute | solution.py:86
  159.9 1.6 collective-permute-start.33
  162.1 9.7 %copy-start.6 = (s32[8]{0:T(128)S(1)}, s32[8]{0:T(128)}, u32[]{:S(2)}) copy-start(s32[8]{0:T(128)} %constant.73.clone) | copy-start | bytes 100
  162.1 10.4 %collective-permute-start.34 = (bf16[256,512]{1,0:T(8,128)(2,1)S(1)}, bf16[256,512]{1,0:T(8,128)(2,1)S(1)}, u32[]{:S(2)}, u32[]{:S(2)}) collective-permute-start(bf16[256,512]{1,0:T(8,128)(2,1)S(1)} %shard_map.135.refs_9_), channel_id=1, source_target_pairs={{0,3},{1,2},{2,1},{3,0},{4,7},{5,6},{6,5},{7,4},{8,11},{9,10},{10,... | collective-permute-start | bytes 786440 | tf_op jit(solution)/shard_map/ppermute | solution.py:86
  171.7 1.6 collective-permute-start.37
  173.9 11.8 %collective-permute-start.38 = (bf16[256,512]{1,0:T(8,128)(2,1)S(1)}, bf16[256,512]{1,0:T(8,128)(2,1)S(1)}, u32[]{:S(2)}, u32[]{:S(2)}) collective-permute-start(bf16[256,512]{1,0:T(8,128)(2,1)S(1)} %shard_map.137), channel_id=1, source_target_pairs={{0,1},{1,0},{2,3},{3,2},{4,5},{5,4},{6,7},{7,6},{8,9},{9,8},{10,11... | collective-permute-start | bytes 786440 | tf_op jit(solution)/shard_map/ppermute | solution.py:86

commit v4 on v3

v4 whole, which is shorter than its diff:
```python
import jax
import jax.numpy as jnp
from jax import lax
from jax.experimental import pallas as pl
from jax.experimental.pallas import tpu as pltpu
from jax.sharding import PartitionSpec as P


VMEM_LIMIT = 24*1024*1024
PACK_LIMIT = 60 * 1024 * 1024
CHUNKS = (((0,), 0, 32), ((2,), 0, 32), ((3,), 0, 32), ((1,), 0, 32))
K1_STEPS = 4
K1_LIMIT = None
ORDER = (0, 1, -1, 0, 1, 0, 2, 2, 1, 0, 3, 1, 2, 3, 1, 0, 2, 3, 0, 2, 1, 3, 0, 1, 3, 2, 1, 2, 3, 2, 3, 3)


def swiglu_grads(upstream, gate_pre, up_pre):
    gate_value = gate_pre.astype(jnp.float32)
    up_value = up_pre.astype(jnp.float32)
    sigmoid_gate = jax.nn.sigmoid(gate_value)
    slope = sigmoid_gate * (1.0 + gate_value * (1.0 - sigmoid_gate))
    grad_gate = (upstream * up_value * slope).astype(jnp.bfloat16)
    grad_up = (upstream * gate_value * sigmoid_gate).astype(jnp.bfloat16)
    return (grad_gate, grad_up)


def contract_last(left, right):
    axis = left.ndim - 1
    return lax.dot_general(
        left, right, (((axis,), (1,)), ((), ())), preferred_element_type=jnp.float32
    )


def place_rows(routes, gates, lengths, slots):
    tok_rows = routes.shape[0]
    hit_zero = routes == 0
    weight_zero = jnp.sum(jnp.where(hit_zero, gates, 0.0), axis=1)
    chosen = jnp.any(hit_zero, axis=1)
    doc_len = lengths[0]
    ends = jnp.cumsum(doc_len)
    starts = ends - doc_len
    position = jnp.arange(tok_rows, dtype=jnp.int32)
    inside = (position[:, None] >= starts[None, :]) & (position[:, None] < ends[None, :])
    mean_len = tok_rows / doc_len.shape[0]
    factor = jnp.sum(
        jnp.where(inside, mean_len / doc_len.astype(jnp.float32)[None, :], 0.0), axis=1
    )
    slot_of = jnp.cumsum(chosen.astype(jnp.int32)) - 1
    placing = (
        (slot_of[None, :] == jnp.arange(slots, dtype=jnp.int32)[:, None]) & chosen[None, :]
    ).astype(jnp.bfloat16)
    return placing, weight_zero * factor


def plain_exchange(out_grad, routes, gates, lengths, saved_gate, saved_up, w_gate, w_up, w_down):
    group_size = lax.axis_size("et")
    groups = lax.axis_size("dp")
    group_rows = saved_gate.shape[1]
    slots = group_rows // group_size
    width = w_gate.shape[0]
    placing, coef = place_rows(routes, gates, lengths, slots)
    scaled = (out_grad.astype(jnp.float32) * coef[:, None]).astype(jnp.bfloat16)
    packed = jnp.dot(placing, scaled, preferred_element_type=jnp.float32).astype(jnp.bfloat16)
    rows = lax.all_to_all(packed.reshape(slots, groups, width), "dp", split_axis=1, concat_axis=0)
    rows = rows.reshape(groups, slots, width)
    rows = lax.all_gather(rows, "et", axis=1)
    partial_up = contract_last(rows.reshape(groups * group_rows, width), w_down).astype(jnp.bfloat16)
    upstream = lax.psum_scatter(partial_up, "dp", scatter_dimension=0, tiled=True).astype(jnp.float32)
    grads = jnp.stack(swiglu_grads(upstream, saved_gate[0], saved_up[0]))
    grads = lax.all_gather(grads, "dp", axis=0)
    terms = contract_last(grads[:, 0], w_gate) + contract_last(grads[:, 1], w_up)
    terms = terms.astype(jnp.bfloat16).reshape(groups, group_size, slots, width)
    summed = lax.psum_scatter(terms, "et", scatter_dimension=1, tiled=False)
    summed = lax.all_to_all(summed, "dp", split_axis=0, concat_axis=1)
    summed = summed.reshape(slots, groups * width)
    input_grad = lax.dot_general(
        placing, summed, (((0,), (0,)), ((), ())), preferred_element_type=jnp.float32
    )
    return input_grad.astype(jnp.bfloat16)


def swap(values, axis, offset):
    size = lax.axis_size(axis)
    return lax.ppermute(values, axis, [(i, i ^ offset) for i in range(size)])


def exchange(values, turn):
    size = lax.axis_size("dp")
    return lax.ppermute(values, "dp", [(i, i ^ (2 if (i + turn) % 2 == 0 else 4)) for i in range(size)])


def whole(array):
    return pl.BlockSpec(array.shape, lambda i, where: (0,) * len(array.shape))


def shape(rows, columns, kind=jnp.bfloat16):
    return jax.ShapeDtypeStruct((rows, columns), kind)


class Steps:
    def __init__(self, where):
        self.where = where
        self.last = []
        self.waits = []

    def call(self, kernel, out_shape, flops, moved, grid, in_specs, out_specs, operands, scratch_shapes=(), limit=None):
        after = self.last + self.waits
        self.waits = []
        inputs = 1 + len(operands)

        def ordered(*refs):
            kernel(*refs[:inputs], *refs[inputs + len(after) :])

        results = pl.pallas_call(
            ordered,
            out_shape=out_shape,
            cost_estimate=pl.CostEstimate(flops=flops, bytes_accessed=moved, transcendentals=0),
            compiler_params=pltpu.CompilerParams(vmem_limit_bytes=limit or VMEM_LIMIT),
            grid_spec=pltpu.PrefetchScalarGridSpec(
                num_scalar_prefetch=1,
                grid=grid,
                in_specs=list(in_specs) + [pl.BlockSpec(memory_space=pl.ANY)] * len(after),
                out_specs=out_specs,
                scratch_shapes=scratch_shapes,
            ),
        )(self.where, *operands, *after)
        self.last = list(results[:1])
        return results


def whole(array):
    return pl.BlockSpec(array.shape, lambda i, where: (0,) * len(array.shape))


def shape(rows, columns, kind=jnp.bfloat16):
    return jax.ShapeDtypeStruct((rows, columns), kind)


def packed_rows(steps, out_grad, routes, gates, lengths, groups, slots):
    tokens, columns = out_grad.shape
    width = columns // groups
    documents = lengths.shape[1]
    strips = 2
    each = groups // strips

    def kernel(where, grad_ref, routes_ref, gates_ref, lengths_ref, rows_ref, placing_ref, coef_ref):
        @pl.when(pl.program_id(0) == 0)
        def _():
            hit_zero = routes_ref[...] == 0
            weight_zero = jnp.sum(jnp.where(hit_zero, gates_ref[...], 0.0), axis=0, keepdims=True)
            chosen = jnp.sum(jnp.where(hit_zero, 1.0, 0.0), axis=0, keepdims=True)
            position = lax.broadcasted_iota(jnp.int32, (1, tokens), 1)
            own_len = jnp.ones((1, tokens), jnp.float32)
            start = 0
            for document in range(documents):
                length = lengths_ref[0, document]
                inside = (position >= start) & (position < start + length)
                own_len = jnp.where(inside, length.astype(jnp.float32), own_len)
                start = start + length
            coef = weight_zero * ((tokens / documents) / own_len)
            token = lax.broadcasted_iota(jnp.int32, (tokens, tokens), 0)
            earlier = jnp.where(token <= lax.broadcasted_iota(jnp.int32, (tokens, tokens), 1), 1.0, 0.0).astype(jnp.bfloat16)
            counts = jnp.dot(
                jnp.broadcast_to(chosen, (slots, tokens)).astype(jnp.bfloat16),
                earlier,
                preferred_element_type=jnp.float32,
            )
            slot = lax.broadcasted_iota(jnp.int32, (slots, tokens), 0)
            taken = (counts.astype(jnp.int32) - 1 == slot) & (chosen > 0.0)
            placing_ref[...] = jnp.where(taken, 1.0, 0.0).astype(jnp.bfloat16)
            coef_ref[...] = jnp.sum(jnp.where(taken, coef, 0.0), axis=1, keepdims=True)

        rows = jnp.dot(placing_ref[...], grad_ref[...], preferred_element_type=jnp.float32)
        rows = (rows * coef_ref[...]).astype(jnp.bfloat16)
        for k in range(each):
            rows_ref[k] = rows[:, k * width : (k + 1) * width]

    return steps.call(
        kernel,
        [jax.ShapeDtypeStruct((groups, slots, width), jnp.bfloat16), shape(slots, tokens)],
        2 * tokens * slots * columns,
        2 * tokens * columns + 2 * slots * columns,
        (strips,),
        [
            pl.BlockSpec((tokens, columns // strips), lambda i, where: (0, i)),
            whole(routes),
            whole(gates),
            pl.BlockSpec(memory_space=pltpu.SMEM),
        ],
        [
            pl.BlockSpec((each, slots, width), lambda i, where: (i, 0, 0)),
            pl.BlockSpec((slots, tokens), lambda i, where: (0, 0)),
        ],
        [out_grad, routes, gates, lengths],
        [pltpu.VMEM((slots, 1), jnp.float32)],
        PACK_LIMIT,
    )


def other_halves(steps, weights, saved):
    width, hidden = weights[0].shape
    rows = saved[0].shape[1]
    half = hidden // 2
    parts = 4

    def kernel(where, gate, up, saved_gate, saved_up, weights_out, saved_out):
        weights_out[0], weights_out[1] = gate[...], up[...]
        saved_out[0], saved_out[1] = saved_gate[0], saved_up[0]

    return steps.call(
        kernel,
        [
            jax.ShapeDtypeStruct((2, width, half), jnp.bfloat16),
            jax.ShapeDtypeStruct((2, rows, half), jnp.bfloat16),
        ],
        0,
        8 * (width + rows) * half,
        (parts,),
        [pl.BlockSpec((width // parts, half), lambda i, where: (i, 1 - where[0]))] * 2
        + [pl.BlockSpec((1, rows // parts, half), lambda i, where: (0, i, 1 - where[0]))] * 2,
        [
            pl.BlockSpec((2, width // parts, half), lambda i, where: (0, i, 0)),
            pl.BlockSpec((2, rows // parts, half), lambda i, where: (0, i, 0)),
        ],
        weights + saved,
    )


def arrived(steps, rows):
    def kernel(where, rows, out):
        out[...] = rows[...]

    return steps.call(
        kernel,
        [jax.ShapeDtypeStruct(rows.shape, rows.dtype)],
        0,
        4 * rows.size,
        (1,),
        [whole(rows)],
        [whole(rows)],
        [rows],
    )[0]


def partial_sums(steps, chunk, here, there, own_down, other_down):
    offsets, low, high = chunk
    members, count = len(offsets), high - low
    width = own_down.shape[1]
    block = members * 2 * count
    half = own_down.shape[0] // 2
    step = half // K1_STEPS

    def kernel(where, *refs):
        own_ref, other_ref, send, keep, left = refs[2 * members :]

        @pl.when(pl.program_id(0) == 0)
        def _():
            for q in range(members):
                for place in range(8):
                    to = place // 2 * block + (q * 2 + place % 2) * count
                    group = where[2 + place]
                    left[to : to + count, :width] = refs[q][group, low:high, :]
                    left[to : to + count, width:] = refs[members + q][group, low:high, :]

        sums = contract_last(left[:, :width], own_ref[...]) + contract_last(left[:, width:], other_ref[...])
        sums = sums.astype(jnp.bfloat16)
        keep[:block], send[:block] = sums[:block], sums[block : 2 * block]
        keep[block:], send[block:] = sums[2 * block : 3 * block], sums[3 * block :]

    weight = pl.BlockSpec((step, width), lambda i, where: (where[0] * K1_STEPS + i, 0))
    return steps.call(
        kernel,
        [shape(2 * block, half)] * 2,
        16 * block * width * half,
        4 * half * width + 8 * block * (2 * width + half),
        (K1_STEPS,),
        [whole(x) for x in here + there] + [weight, weight],
        [pl.BlockSpec((2 * block, step), lambda i, where: (0, i))] * 2,
        here + there + [own_down, other_down],
        [pltpu.VMEM((4 * block, 2 * width), jnp.bfloat16)],
        K1_LIMIT,
    )


def second_terms(steps, keep, got):
    rows, columns = keep.shape[0] // 2, keep.shape[1]

    def kernel(where, keep, got, send):
        send[...] = (keep[...].astype(jnp.float32) + got[...].astype(jnp.float32)).astype(jnp.bfloat16)

    return steps.call(
        kernel,
        [shape(rows, columns)],
        rows * columns,
        6 * rows * columns,
        (1,),
        [pl.BlockSpec((rows, columns), lambda i, where: (1, 0))] * 2,
        [pl.BlockSpec((rows, columns), lambda i, where: (0, 0))],
        [keep, got],
    )[0]


def hidden_grads(steps, chunk, keep, got, last, saved):
    offsets, low, high = chunk
    members, count = len(offsets), high - low
    rows, columns = last.shape

    def kernel(where, keep, got, last, *refs):
        out = refs[-1]
        for q in range(members):
            for core in range(2):
                take = pl.ds((q * 2 + core) * count, count)
                upstream = (
                    keep[take, :].astype(jnp.float32)
                    + got[take, :].astype(jnp.float32)
                    + last[take, :].astype(jnp.float32)
                )
                gate, up = refs[(q * 2 + core) * 2 : (q * 2 + core) * 2 + 2]
                grad_gate, grad_up = swiglu_grads(upstream, gate[0], up[0])
                out[take, :columns] = grad_gate
                out[take, columns:] = grad_up

    upper = pl.BlockSpec((rows, columns), lambda i, where: (0, 0))
    slots = saved[0].shape[1] // lax.axis_size("et")

    def row(where, offset):
        return ((where[1] ^ offset) * slots + low) // count

    def own_spec(offset):
        return pl.BlockSpec((1, count, columns), lambda i, where: (0, row(where, offset), where[0]))

    def other_spec(offset, which):
        return pl.BlockSpec((1, count, columns), lambda i, where: (which, row(where, offset), 0))

    saved_specs = [
        spec for offset in offsets for spec in [own_spec(offset)] * 2 + [other_spec(offset, k) for k in range(2)]
    ]
    return steps.call(
        kernel,
        [shape(rows, 2 * columns)],
        40 * rows * columns,
        14 * rows * columns,
        (1,),
        [upper] * 3 + saved_specs,
        [pl.BlockSpec((rows, 2 * columns), lambda i, where: (0, 0))],
        [keep, got, last] + (saved[:2] + [saved[2]] * 2) * members,
    )[0]


def input_terms(steps, chunk, grads, weights):
    offsets, low, high = chunk
    members, count = len(offsets), high - low
    block, half = grads[0].shape[0], grads[0].shape[1] // 2
    rows = 4 * block
    width = weights[0].shape[0]
    step = width // 2

    def kernel(where, own, first_block, second_block, far_block, own_gate, own_up, other_gate, other_up, *refs):
        own_out, other_out, left = refs
        i = pl.program_id(0)

        @pl.when(i == 0)
        def _():
            for chip, source in enumerate((own, first_block, second_block, far_block)):
                left[chip * block : (chip + 1) * block, :] = source[...]

        def terms_of(gate, up):
            return contract_last(left[:, :half], gate) + contract_last(left[:, half:], up)

        @pl.when(i < 2)
        def _():
            terms = terms_of(own_gate[...], own_up[...])
            for q in range(members):
                for place in range(8):
                    at = place // 2 * block + (q * 2 + place % 2) * count
                    own_out[q, where[2 + place]] = terms[at : at + count]

        @pl.when(i >= 2)
        def _():
            terms = terms_of(other_gate[0], other_up[0]).astype(jnp.bfloat16)
            for q in range(members):
                for place in range(8):
                    at = place // 2 * block + (q * 2 + place % 2) * count
                    other_out[q, where[2 + place]] = terms[at : at + count]

    def first(i):
        return jnp.minimum(i, 1)

    def second(i):
        return jnp.maximum(i - 2, 0)

    own_weight = pl.BlockSpec((step, half), lambda i, where: (first(i), where[0]))
    other_weights = [
        pl.BlockSpec((1, step, half), lambda i, where, k=k: (k, second(i), 0)) for k in range(2)
    ]
    return steps.call(
        kernel,
        [
            jax.ShapeDtypeStruct((members, 8, count, width), jnp.float32),
            jax.ShapeDtypeStruct((members, 8, count, width), jnp.bfloat16),
        ],
        8 * rows * width * half,
        8 * width * half + 4 * rows * half + 6 * rows * width,
        (4,),
        [whole(x) for x in grads] + [own_weight] * 2 + other_weights,
        [
            pl.BlockSpec((members, 8, count, step), lambda i, where: (0, 0, 0, first(i))),
            pl.BlockSpec((members, 8, count, step), lambda i, where: (0, 0, 0, second(i))),
        ],
        grads + weights[:2] + [weights[2]] * 2,
        [pltpu.VMEM((rows, 2 * half), jnp.bfloat16)],
    )


def summed_terms(steps, own_terms, got):
    members, *rest = own_terms.shape

    def kernel(where, own_terms, got, *outs):
        for q in range(members):
            outs[q][...] = (own_terms[q] + got[q].astype(jnp.float32)).astype(jnp.bfloat16)

    return steps.call(
        kernel,
        [jax.ShapeDtypeStruct(rest, jnp.bfloat16)] * members,
        own_terms.size,
        8 * own_terms.size,
        (1,),
        [whole(own_terms), whole(got)],
        [pl.BlockSpec(rest, lambda i, where: (0, 0, 0))] * members,
        [own_terms, got],
    )


def chunk_steps(steps, chunk, here, saved, weights, downs):
    offsets, low, high = chunk
    if any(offsets):
        here = [arrived(steps, x) for x in here]
        yield
    there = [swap(x, "dp", 1) for x in here]
    send, keep = partial_sums(steps, chunk, here, there, *downs)
    got = exchange(send, 0)
    yield
    last = exchange(second_terms(steps, keep, got), 1)
    yield
    own = hidden_grads(steps, chunk, keep, got, last, saved)
    from_second, from_first = exchange(own, 1), exchange(own, 0)
    yield
    far = exchange(from_second, 0)
    steps.waits = steps.waits + [from_second]
    yield
    own_terms, other_terms = input_terms(steps, chunk, [own, from_first, from_second, far], weights)
    got = swap(other_terms, "dp", 1)
    yield
    terms = summed_terms(steps, own_terms, got)
    terms = [part if offset == 0 else swap(part, "et", offset) for offset, part in zip(offsets, terms)]
    yield
    steps.waits = steps.waits + terms
    yield terms


def per_device(out_grad, routes, gates, lengths, saved_gate, saved_up, w_gate, w_up, w_down):
    groups = lax.axis_size("dp")
    slots = saved_gate.shape[1] // lax.axis_size("et")
    width = w_gate.shape[0]
    me = lax.axis_index("dp")
    core = me % 2
    first, second = 2 + 2 * core, 4 - 2 * core
    place = [me ^ (chip + pair) for chip in (0, first, second, 6) for pair in (0, 1)]
    where = jnp.stack([core, lax.axis_index("et")] + place).astype(jnp.int32)

    downs = [w_down, swap(w_down, "dp", 1)]
    saved = [saved_gate, saved_up]
    weights = [w_gate, w_up]

    steps = Steps(where)
    rows, placing = packed_rows(steps, out_grad, routes.T, gates.T, lengths, groups, slots)
    rows = lax.all_to_all(rows, "dp", split_axis=0, concat_axis=0, tiled=True)
    sources = {
        offset: rows if offset == 0 else swap(rows, "et", offset)
        for offset in sorted({offset for offsets, _, _ in CHUNKS for offset in offsets})
    }
    chunks = [
        chunk_steps(steps, chunk, [sources[offset] for offset in chunk[0]], saved, weights, downs)
        for chunk in CHUNKS
    ]
    parts = {}
    steps.waits = [rows]
    for k in ORDER:
        if k < 0:
            other_weights, other_saved = other_halves(steps, weights, saved)
            weights.append(swap(other_weights, "dp", 1))
            saved.append(swap(other_saved, "dp", 1))
            continue
        for offset, part in zip(CHUNKS[k][0], next(chunks[k]) or []):
            parts.setdefault(offset, []).append(part)
    total = sum(jnp.concatenate(part, axis=1).astype(jnp.float32) for part in parts.values())
    summed = total.astype(jnp.bfloat16)
    summed = lax.all_to_all(summed, "dp", split_axis=0, concat_axis=1)
    summed = summed.reshape(slots, groups * width)
    input_grad = lax.dot_general(
        placing, summed, (((0,), (0,)), ((), ())), preferred_element_type=jnp.float32
    )
    return input_grad.astype(jnp.bfloat16)


def solution(mesh):
    in_specs = (
        P(("dp", "et"), None),
        P(("dp", "et"), None),
        P(("dp", "et"), None),
        P(("dp", "et"), None),
        P("dp", None, "et"),
        P("dp", None, "et"),
        P("dp", "et"),
        P("dp", "et"),
        P("et", "dp"),
    )
    out_specs = P(("dp", "et"), None)
    body = per_device if mesh.shape["dp"] == 8 and mesh.shape["et"] == 4 else plain_exchange
    return jax.shard_map(
        body, mesh=mesh, in_specs=in_specs, out_specs=out_specs, check_vma=False
    )
```

time: 198 us -> 182 us (0.919)
  blocking collectives: 9.35 us -> 21.4 us
  starting transfers between devices: 48.9 us -> 39.1 us
  Pallas kernels: 57.2 us -> 48.8 us
  other arithmetic: 4.47 us -> 0.15 us
  waiting for transfers between devices: 69.3 us -> 66.1 us
    ppermute x20, waiting for transfers between devices: 33.1 us -> 44.8 us  [exchange(): lax.ppermute(values, 'dp', [(i, i ^ (2 if (i + turn) % 2 == 0 else 4)) fo...]
    all_to_all x0 -> x1, blocking collectives: none -> 11.8 us  [per_device(): rows = lax.all_to_all(rows, 'dp', split_axis=0, concat_axis=0, tiled=True)]
    pallas_call x20 -> x25, Pallas kernels: 57.2 us -> 48.8 us  [call(): pl.pallas_call(ordered, out_shape=out_shape, cost_estimate=pl.CostEstimat...]
    ppermute x19 -> x17, waiting for transfers between devices: 29.3 us -> 21.2 us  [swap(): return lax.ppermute(values, axis, [(i, i ^ offset) for i in range(size)])]
    all_to_all x1 -> x0, waiting for transfers between devices: 6.88 us -> none  [per_device(): lax.all_to_all(packed.reshape(slots, groups, width), 'dp', split_axis=1,...]
    ppermute x19 -> x17, starting transfers between devices: 24.4 us -> 18.2 us  [swap(): return lax.ppermute(values, axis, [(i, i ^ offset) for i in range(size)])]
    all_to_all x1 -> x0, starting transfers between devices: 4.83 us -> none  [per_device(): lax.all_to_all(packed.reshape(slots, groups, width), 'dp', split_axis=1,...]
  transfers between devices with their start and end apart: 40 -> 37, of which waited for: 18 -> 12; matrix products, arithmetic and copies ran while one was open for 4% -> 0% of each run, Pallas kernels for 25% -> 25%
where the time goes in v4:
time: 182 us
  waiting for transfers between devices  66.1 us (36%)
  Pallas kernels  48.8 us (27%)
  starting transfers between devices  39.1 us (21%)
  blocking collectives  21.4 us (12%)
  local copies, waits for them, and re-layouts  4.52 us (2%)
    pallas_call x25, Pallas kernels, call(): pl.pallas_call(ordered, out_shape=out_shape, cost_estimate=pl.CostEstimat...  48.8 us
    ppermute x20, waiting for transfers between devices, exchange(): lax.ppermute(values, 'dp', [(i, i ^ (2 if (i + turn) % 2 == 0 else 4)) fo...  44.8 us
    ppermute x17, waiting for transfers between devices, swap(): return lax.ppermute(values, axis, [(i, i ^ offset) for i in range(size)])  21.2 us
    ppermute x20, starting transfers between devices, exchange(): lax.ppermute(values, 'dp', [(i, i ^ (2 if (i + turn) % 2 == 0 else 4)) fo...  21 us
    ppermute x17, starting transfers between devices, swap(): return lax.ppermute(values, axis, [(i, i ^ offset) for i in range(size)])  18.2 us
    all_to_all x1, blocking collectives, per_device(): rows = lax.all_to_all(rows, 'dp', split_axis=0, concat_axis=0, tiled=True)  11.8 us
    all_to_all x1, blocking collectives, per_device(): summed = lax.all_to_all(summed, 'dp', split_axis=0, concat_axis=1)  9.62 us
    unnamed x19, local copies, waits for them, and re-layouts  3.85 us
  transfers between devices with their start and end apart: 37, of which 12 were waited for; matrix products, arithmetic and copies ran while one was open for 0% of the time, Pallas kernels for 25%

profile of v4, /device:TPU:0, one launch (start us, length us, event | category | flops | bytes accessed | tf_op | source)
XLA Modules:
  0.0 181.9 jit_solution(5469680395693379242)
XLA Ops:
  0.5 0.7 stack.43.refs_0_
  1.1 3.2 %shard_map.91 = (bf16[8,32,512]{2,1,0:T(8,128)(2,1)}, bf16[32,128]{1,0:T(8,128)(2,1)}) custom-call(s32[10]{0:T(128)} %stack.43.refs_0_, bf16[128,4096]{1,0:T(8,128)(2,1)} %refs_1_.2, s32[2,128]{1,0:T(2,128)} %bitcast.29, f32[2,128]{1,0:T(2,128)} %bitcast.30, s32[1,8]{1,0:T(1,128)} %refs_4_.6), custom_call_target="tpu_custom_call" | custom-call | flops 33554432 | bytes 1310720 | tf_op jit(solution)/shard_map/pallas_call | solution.py:114
  4.3 11.8 %all_to_all.20.refs_1_.refs_6_ = bf16[8,32,512]{2,1,0:T(8,128)(2,1)S(1)} all-to-all(bf16[8,32,512]{2,1,0:T(8,128)(2,1)} %get-tuple-element.26.refs_5_), channel_id=1, replica_groups=mesh['dp'=8,'et'=4] {'dp'}, dimensions={0} | all-to-all | bytes 524288 | tf_op jit(solution)/shard_map/all_to_all | solution.py:477
  16.1 2.6 %collective-permute-start.3 = (bf16[8,32,512]{2,1,0:T(8,128)(2,1)S(1)}, bf16[8,32,512]{2,1,0:T(8,128)(2,1)S(1)}, u32[]{:S(2)}, u32[]{:S(2)}) collective-permute-start(bf16[8,32,512]{2,1,0:T(8,128)(2,1)S(1)} %all_to_all.20.refs_1_.refs_6_), channel_id=1, source_target_pairs={{0,2},{1,3},{2,0},{3,1},{4,6},{5,7},{6,4},{7,5},{8,10},{9,11},{10,... | collective-permute-start | bytes 786440 | tf_op jit(solution)/shard_map/ppermute | solution.py:84
  18.7 2.2 %copy-done.2 = bf16[4096,512]{1,0:T(8,128)(2,1)S(1)} copy-done((bf16[4096,512]{1,0:T(8,128)(2,1)S(1)}, bf16[4096,512]{1,0:T(8,128)(2,1)}, u32[]{:S(2)}) %copy-start.2) | copy-done | bytes 4194328
  20.9 0.9 copy-done.6
  21.9 0.7 copy-done.7
  22.6 4.2 %shard_map.92 = (bf16[128,2048]{1,0:T(8,128)(2,1)S(1)}, bf16[128,2048]{1,0:T(8,128)(2,1)S(1)}) custom-call(s32[10]{0:T(128)S(1)} %copy-done.7, bf16[8,32,512]{2,1,0:T(8,128)(2,1)S(1)} %all_to_all.20.refs_1_.refs_6_, bf16[8,32,512]{2,1,0:T(8,128)(2,1)S(1)} %collective-permute-done.refs_2_, bf16[4096,512]{1,0:T(8,128)(2,1)S(1)} %copy-done.2, ...), custom_call_target="tpu_custom_call" | custom-call | flops 1073741824 | bytes 5767168 | tf_op jit(solution)/shard_map/pallas_call | solution.py:114
  26.8 4.5 %collective-permute-done.3.refs_1_ = bf16[8,32,512]{2,1,0:T(8,128)(2,1)S(1)} collective-permute-done((bf16[8,32,512]{2,1,0:T(8,128)(2,1)S(1)}, bf16[8,32,512]{2,1,0:T(8,128)(2,1)S(1)}, u32[]{:S(2)}, u32[]{:S(2)}) %collective-permute-start.3) | collective-permute-done | bytes 262176 | tf_op jit(solution)/shard_map/ppermute | solution.py:84
  31.9 1.8 %shard_map.94 = (bf16[2,512,2048]{2,1,0:T(8,128)(2,1)S(1)}, bf16[2,128,2048]{2,1,0:T(8,128)(2,1)S(1)}) custom-call(s32[10]{0:T(128)S(1)} %copy-done.7, bf16[512,4096]{1,0:T(8,128)(2,1)S(1)} %copy-done, bf16[512,4096]{1,0:T(8,128)(2,1)S(1)} %copy-done.1, bf16[1,128,4096]{2,1,0:T(8,128)(2,1)S(1)} %copy-done.4, bf16[1,128,4096]{2,1,0:T(8,128)(2,1)S(1)} %copy-done.5, ...), custom_call_target="tpu_custom_call" | custom-call | bytes 10485760 | tf_op jit(solution)/shard_map/pallas_call | solution.py:114
  34.9 8.6 %collective-permute-done.2.refs_2_ = bf16[128,2048]{1,0:T(8,128)(2,1)S(1)} collective-permute-done((bf16[128,2048]{1,0:T(8,128)(2,1)S(1)}, bf16[128,2048]{1,0:T(8,128)(2,1)S(1)}, u32[]{:S(2)}, u32[]{:S(2)}) %collective-permute-start.2) | collective-permute-done | bytes 524320 | tf_op jit(solution)/shard_map/ppermute | solution.py:89
  43.5 0.6 shard_map.95.refs_5_
  44.1 0.6 collective-permute-start.4
  44.8 3.5 %collective-permute-start.13 = (bf16[8,32,512]{2,1,0:T(8,128)(2,1)S(1)}, bf16[8,32,512]{2,1,0:T(8,128)(2,1)S(1)}, u32[]{:S(2)}, u32[]{:S(2)}) collective-permute-start(bf16[8,32,512]{2,1,0:T(8,128)(2,1)S(1)} %all_to_all.20.refs_1_.refs_6_), channel_id=1, source_target_pairs={{0,3},{1,2},{2,1},{3,0},{4,7},{5,6},{6,5},{7,4},{8,11},{9,10},{10,... | collective-permute-start | bytes 786440 | tf_op jit(solution)/shard_map/ppermute | solution.py:84
  48.3 4.2 %shard_map.96 = (bf16[128,2048]{1,0:T(8,128)(2,1)S(1)}, bf16[128,2048]{1,0:T(8,128)(2,1)S(1)}) custom-call(s32[10]{0:T(128)S(1)} %copy-done.7, bf16[8,32,512]{2,1,0:T(8,128)(2,1)S(1)} %shard_map.93.refs_5_.refs_1_, bf16[8,32,512]{2,1,0:T(8,128)(2,1)S(1)} %collective-permute-done.6.refs_2_, bf16[4096,512]{1,0:T(8,128)(2,1)S(1)} %copy-done.3, ...), custom_call_target="tpu_custom_call" | custom-call | flops 1073741824 | bytes 5767168 | tf_op jit(solution)/shard_map/pallas_call | solution.py:114
  52.5 0.6 collective-permute-start.12
  53.1 0.9 shard_map.97.refs_2_.refs_1_
  54.7 1.5 collective-permute-start.8
  56.2 4.3 %shard_map.99 = (bf16[128,2048]{1,0:T(8,128)(2,1)S(1)}, bf16[128,2048]{1,0:T(8,128)(2,1)S(1)}) custom-call(s32[10]{0:T(128)S(1)} %copy-done.7, bf16[8,32,512]{2,1,0:T(8,128)(2,1)S(1)} %shard_map.98.refs_1_.refs_5_, bf16[8,32,512]{2,1,0:T(8,128)(2,1)S(1)} %collective-permute-done.14.refs_2_, bf16[4096,512]{1,0:T(8,128)(2,1)S(1)} %copy-done.3, ...), custom_call_target="tpu_custom_call" | custom-call | flops 1073741824 | bytes 5767168 | tf_op jit(solution)/shard_map/pallas_call | solution.py:114
  60.5 1.5 collective-permute-start.16
  62.0 4.2 %collective-permute-start.11 = (bf16[8,32,512]{2,1,0:T(8,128)(2,1)S(1)}, bf16[8,32,512]{2,1,0:T(8,128)(2,1)S(1)}, u32[]{:S(2)}, u32[]{:S(2)}) collective-permute-start(bf16[8,32,512]{2,1,0:T(8,128)(2,1)S(1)} %all_to_all.20.refs_1_.refs_6_), channel_id=1, source_target_pairs={{0,1},{1,0},{2,3},{3,2},{4,5},{5,4},{6,7},{7,6},{8,9},{9,8},{10,11... | collective-permute-start | bytes 786440 | tf_op jit(solution)/shard_map/ppermute | solution.py:84
  66.2 0.6 shard_map.100.refs_2_
  66.8 1.0 collective-permute-start.17
  67.8 3.8 %collective-permute-done.11.refs_1_ = bf16[8,32,512]{2,1,0:T(8,128)(2,1)S(1)} collective-permute-done((bf16[8,32,512]{2,1,0:T(8,128)(2,1)S(1)}, bf16[8,32,512]{2,1,0:T(8,128)(2,1)S(1)}, u32[]{:S(2)}, u32[]{:S(2)}) %collective-permute-start.11) | collective-permute-done | bytes 262176 | tf_op jit(solution)/shard_map/ppermute | solution.py:84
  71.6 1.4 collective-permute-start.7
  73.1 0.6 collective-permute-start.9
  74.2 0.9 shard_map.102.refs_3_.refs_1_
  75.1 1.5 collective-permute-start.18
  76.7 0.6 shard_map.103.refs_5_
  77.3 0.9 collective-permute-done.15.refs_2_
  78.2 1.1 collective-permute-start.21
  79.3 4.2 %shard_map.104 = (bf16[128,2048]{1,0:T(8,128)(2,1)S(1)}, bf16[128,2048]{1,0:T(8,128)(2,1)S(1)}) custom-call(s32[10]{0:T(128)S(1)} %copy-done.7, bf16[8,32,512]{2,1,0:T(8,128)(2,1)S(1)} %shard_map.101.refs_8_.refs_1_, bf16[8,32,512]{2,1,0:T(8,128)(2,1)S(1)} %collective-permute-done.15.refs_2_, bf16[4096,512]{1,0:T(8,128)(2,1)S(1)} %copy-done.3, ...), custom_call_target="tpu_custom_call" | custom-call | flops 1073741824 | bytes 5767168 | tf_op jit(solution)/shard_map/pallas_call | solution.py:114
  83.5 0.9 collective-permute-done.7.refs_2_
  84.9 10.6 %collective-permute-done.9.refs_4_ = bf16[64,4096]{1,0:T(8,128)(2,1)S(1)} collective-permute-done((bf16[64,4096]{1,0:T(8,128)(2,1)S(1)}, bf16[64,4096]{1,0:T(8,128)(2,1)S(1)}, u32[]{:S(2)}, u32[]{:S(2)}) %collective-permute-start.9) | collective-permute-done | bytes 524320 | tf_op jit(solution)/shard_map/ppermute | solution.py:89
  95.5 0.7 collective-permute-start.20
  96.1 1.4 collective-permute-start.23
  97.5 4.2 %shard_map.105 = (f32[1,8,32,512]{3,2,1,0:T(8,128)S(1)}, bf16[1,8,32,512]{3,2,1,0:T(8,128)(2,1)S(1)}) custom-call(s32[10]{0:T(128)S(1)} %copy-done.7, bf16[64,4096]{1,0:T(8,128)(2,1)S(1)} %shard_map.97.refs_2_.refs_1_, bf16[64,4096]{1,0:T(8,128)(2,1)S(1)} %collective-permute-done.7.refs_2_, bf16[64,4096]{1,0:T(8,128)(2,1)S(1)} %collective-permute-done.8.refs_3_, ...), custom_call_target="tpu_custom_call" | custom-call | flops 2147483648 | bytes 11272192 | tf_op jit(solution)/shard_map/pallas_call | solution.py:114
  101.7 0.9 shard_map.106.refs_3_.refs_1_
  102.6 1.5 collective-permute-start.24
  104.2 8.0 %collective-permute-done.20.refs_2_ = bf16[128,2048]{1,0:T(8,128)(2,1)S(1)} collective-permute-done((bf16[128,2048]{1,0:T(8,128)(2,1)S(1)}, bf16[128,2048]{1,0:T(8,128)(2,1)S(1)}, u32[]{:S(2)}, u32[]{:S(2)}) %collective-permute-start.20) | collective-permute-done | bytes 524320 | tf_op jit(solution)/shard_map/ppermute | solution.py:89
  112.2 0.6 shard_map.107.refs_3_
  112.8 1.3 collective-permute-start.26
  114.1 0.6 shard_map.108.refs_9_.refs_4_
  114.7 6.1 %collective-permute-done.23.refs_4_ = bf16[64,4096]{1,0:T(8,128)(2,1)S(1)} collective-permute-done((bf16[64,4096]{1,0:T(8,128)(2,1)S(1)}, bf16[64,4096]{1,0:T(8,128)(2,1)S(1)}, u32[]{:S(2)}, u32[]{:S(2)}) %collective-permute-start.23) | collective-permute-done | bytes 524320 | tf_op jit(solution)/shard_map/ppermute | solution.py:89
  120.7 4.2 %shard_map.109 = (f32[1,8,32,512]{3,2,1,0:T(8,128)S(1)}, bf16[1,8,32,512]{3,2,1,0:T(8,128)(2,1)S(1)}) custom-call(s32[10]{0:T(128)S(1)} %copy-done.7, bf16[64,4096]{1,0:T(8,128)(2,1)S(1)} %shard_map.102.refs_3_.refs_1_, bf16[64,4096]{1,0:T(8,128)(2,1)S(1)} %collective-permute-done.22.refs_2_, bf16[64,4096]{1,0:T(8,128)(2,1)S(1)} %collective-permute-done.18.refs_10_.refs_3_, ...), custom_call_target="tpu_custom_call" | custom-call | flops 2147483648 | bytes 11272192 | tf_op jit(solution)/shard_map/pallas_call | solution.py:114
  125.0 0.9 shard_map.110.refs_3_.refs_1_
  125.9 1.5 collective-permute-start.30
  127.4 0.7 collective-permute-start.28
  128.1 1.3 collective-permute-start.29
  129.4 0.7 collective-permute-start.33
  130.1 10.7 %collective-permute-done.30.refs_10_.refs_3_ = bf16[64,4096]{1,0:T(8,128)(2,1)S(1)} collective-permute-done((bf16[64,4096]{1,0:T(8,128)(2,1)S(1)}, bf16[64,4096]{1,0:T(8,128)(2,1)S(1)}, u32[]{:S(2)}, u32[]{:S(2)}) %collective-permute-start.30) | collective-permute-done | bytes 524320 | tf_op jit(solution)/shard_map/ppermute | solution.py:89
  140.8 0.8 collective-permute-start.34
  142.2 1.5 collective-permute-start.27
  143.8 4.2 %shard_map.112 = (f32[1,8,32,512]{3,2,1,0:T(8,128)S(1)}, bf16[1,8,32,512]{3,2,1,0:T(8,128)(2,1)S(1)}) custom-call(s32[10]{0:T(128)S(1)} %copy-done.7, bf16[64,4096]{1,0:T(8,128)(2,1)S(1)} %shard_map.106.refs_3_.refs_1_, bf16[64,4096]{1,0:T(8,128)(2,1)S(1)} %collective-permute-done.28.refs_2_, bf16[64,4096]{1,0:T(8,128)(2,1)S(1)} %collective-permute-done.24.refs_10_.refs_3_, ...), custom_call_target="tpu_custom_call" | custom-call | flops 2147483648 | bytes 11272192 | tf_op jit(solution)/shard_map/pallas_call | solution.py:114
  148.1 4.3 %collective-permute-done.27.refs_4_ = bf16[8,32,512]{2,1,0:T(8,128)(2,1)S(1)} collective-permute-done((bf16[8,32,512]{2,1,0:T(8,128)(2,1)S(1)}, bf16[8,32,512]{2,1,0:T(8,128)(2,1)S(1)}, u32[]{:S(2)}, u32[]{:S(2)}) %collective-permute-start.27) | collective-permute-done | bytes 262176 | tf_op jit(solution)/shard_map/ppermute | solution.py:84
  152.4 0.6 shard_map.113.refs_9_
  153.0 1.3 collective-permute-start.32
  154.2 4.2 %shard_map.114 = (f32[1,8,32,512]{3,2,1,0:T(8,128)S(1)}, bf16[1,8,32,512]{3,2,1,0:T(8,128)(2,1)S(1)}) custom-call(s32[10]{0:T(128)S(1)} %copy-done.7, bf16[64,4096]{1,0:T(8,128)(2,1)S(1)} %shard_map.110.refs_3_.refs_1_, bf16[64,4096]{1,0:T(8,128)(2,1)S(1)} %collective-permute-done.33.refs_2_, bf16[64,4096]{1,0:T(8,128)(2,1)S(1)} %collective-permute-done.30.refs_10_.refs_3_, ...), custom_call_target="tpu_custom_call" | custom-call | flops 2147483648 | bytes 11272192 | tf_op jit(solution)/shard_map/pallas_call | solution.py:114
  158.5 2.8 %collective-permute-done.32.refs_4_ = bf16[8,32,512]{2,1,0:T(8,128)(2,1)S(1)} collective-permute-done((bf16[8,32,512]{2,1,0:T(8,128)(2,1)S(1)}, bf16[8,32,512]{2,1,0:T(8,128)(2,1)S(1)}, u32[]{:S(2)}, u32[]{:S(2)}) %collective-permute-start.32) | collective-permute-done | bytes 262176 | tf_op jit(solution)/shard_map/ppermute | solution.py:84
  161.3 0.6 shard_map.115
  161.9 3.8 %collective-permute-start.36 = (bf16[8,32,512]{2,1,0:T(8,128)(2,1)S(1)}, bf16[8,32,512]{2,1,0:T(8,128)(2,1)S(1)}, u32[]{:S(2)}, u32[]{:S(2)}) collective-permute-start(bf16[8,32,512]{2,1,0:T(8,128)(2,1)S(1)} %shard_map.115), channel_id=1, source_target_pairs={{0,1},{1,0},{2,3},{3,2},{4,5},{5,4},{6,7},{7,6},{8,9},{9,8},{10,11... | collective-permute-start | bytes 786440 | tf_op jit(solution)/shard_map/ppermute | solution.py:84
  165.7 4.9 %collective-permute-done.36 = bf16[8,32,512]{2,1,0:T(8,128)(2,1)S(1)} collective-permute-done((bf16[8,32,512]{2,1,0:T(8,128)(2,1)S(1)}, bf16[8,32,512]{2,1,0:T(8,128)(2,1)S(1)}, u32[]{:S(2)}, u32[]{:S(2)}) %collective-permute-start.36) | collective-permute-done | bytes 262176 | tf_op jit(solution)/shard_map/ppermute | solution.py:84
  170.8 9.6 %all_to_all.21 = bf16[8,32,1,512]{3,1,2,0:T(8,128)(2,1)S(1)} all-to-all(bf16[8,32,1,512]{3,1,2,0:T(8,128)(2,1)S(1)} %fusion), channel_id=1, replica_groups=mesh['dp'=8,'et'=4] {'dp'}, dimensions={0} | all-to-all | bytes 524288 | tf_op jit(solution)/shard_map/all_to_all | solution.py:498
  180.4 1.4 convolution_convert_fusion
  (59 shorter events, 4.8 us)
Async XLA Ops:
  0.0 18.7 %collective-permute-start.1 = (bf16[4096,512]{1,0:T(8,128)(2,1)}, bf16[4096,512]{1,0:T(8,128)(2,1)}, u32[]{:S(2)}, u32[]{:S(2)}) collective-permute-start(bf16[4096,512]{1,0:T(8,128)(2,1)} %refs_3_.9), channel_id=1, source_target_pairs={{0,4},{4,0},{8,12},{12,8},{16,20},{20,16},{24,28},{28,24},{1,5},{5... | collective-permute-start | bytes 12582920 | tf_op jit(solution)/shard_map/ppermute | solution.py:84
  1.1 30.8 %copy-start.4 = (bf16[1,128,4096]{2,1,0:T(8,128)(2,1)S(1)}, bf16[1,128,4096]{2,1,0:T(8,128)(2,1)}, u32[]{:S(2)}) copy-start(bf16[1,128,4096]{2,1,0:T(8,128)(2,1)} %refs_4_.11) | copy-start | bytes 3145732
  16.1 15.8 %copy-start = (bf16[512,4096]{1,0:T(8,128)(2,1)S(1)}, bf16[512,4096]{1,0:T(8,128)(2,1)}, u32[]{:S(2)}) copy-start(bf16[512,4096]{1,0:T(8,128)(2,1)} %refs_5_.15) | copy-start | bytes 12582916
  16.1 15.8 %copy-start.1 = (bf16[512,4096]{1,0:T(8,128)(2,1)S(1)}, bf16[512,4096]{1,0:T(8,128)(2,1)}, u32[]{:S(2)}) copy-start(bf16[512,4096]{1,0:T(8,128)(2,1)} %refs_6_.7) | copy-start | bytes 12582916
  16.1 2.7 %collective-permute-start = (bf16[8,32,512]{2,1,0:T(8,128)(2,1)S(1)}, bf16[8,32,512]{2,1,0:T(8,128)(2,1)S(1)}, u32[]{:S(2)}, u32[]{:S(2)}) collective-permute-start(bf16[8,32,512]{2,1,0:T(8,128)(2,1)S(1)} %all_to_all.20.refs_1_.refs_6_), channel_id=1, source_target_pairs={{0,4},{4,0},{8,12},{12,8},{16,20},{20,16},{24,28},{28,24},{1,5},{5... | collective-permute-start | bytes 786440 | tf_op jit(solution)/shard_map/ppermute | solution.py:84
  16.1 15.2 %collective-permute-start.3 = (bf16[8,32,512]{2,1,0:T(8,128)(2,1)S(1)}, bf16[8,32,512]{2,1,0:T(8,128)(2,1)S(1)}, u32[]{:S(2)}, u32[]{:S(2)}) collective-permute-start(bf16[8,32,512]{2,1,0:T(8,128)(2,1)S(1)} %all_to_all.20.refs_1_.refs_6_), channel_id=1, source_target_pairs={{0,2},{1,3},{2,0},{3,1},{4,6},{5,7},{6,4},{7,5},{8,10},{9,11},{10,... | collective-permute-start | bytes 786440 | tf_op jit(solution)/shard_map/ppermute | solution.py:84
  18.7 2.2 %copy-start.2 = (bf16[4096,512]{1,0:T(8,128)(2,1)S(1)}, bf16[4096,512]{1,0:T(8,128)(2,1)}, u32[]{:S(2)}) copy-start(bf16[4096,512]{1,0:T(8,128)(2,1)} %refs_3_.9) | copy-start | bytes 12582916
  20.9 0.9 copy-start.6
  21.9 0.7 copy-start.7
  22.5 9.4 %copy-start.5 = (bf16[1,128,4096]{2,1,0:T(8,128)(2,1)S(1)}, bf16[1,128,4096]{2,1,0:T(8,128)(2,1)}, u32[]{:S(2)}) copy-start(bf16[1,128,4096]{2,1,0:T(8,128)(2,1)} %refs_5_.13) | copy-start | bytes 3145732
  33.8 14.5 %copy-start.3 = (bf16[4096,512]{1,0:T(8,128)(2,1)S(1)}, bf16[4096,512]{1,0:T(8,128)(2,1)}, u32[]{:S(2)}) copy-start(bf16[4096,512]{1,0:T(8,128)(2,1)} %refs_3_.9) | copy-start | bytes 12582916
  33.8 63.7 %collective-permute-start.10 = (bf16[2,512,2048]{2,1,0:T(8,128)(2,1)S(1)}, bf16[2,512,2048]{2,1,0:T(8,128)(2,1)S(1)}, u32[]{:S(2)}, u32[]{:S(2)}) collective-permute-start(bf16[2,512,2048]{2,1,0:T(8,128)(2,1)S(1)} %get-tuple-element.29.refs_3_), channel_id=1, source_target_pairs={{0,4},{4,0},{8,12},{12,8},{16,20},{20,16},{24,28},{28,24},{1,5},{5... | collective-permute-start | bytes 12582920 | tf_op jit(solution)/shard_map/ppermute | solution.py:84
  33.8 19.3 %collective-permute-start.5 = (bf16[2,128,2048]{2,1,0:T(8,128)(2,1)S(1)}, bf16[2,128,2048]{2,1,0:T(8,128)(2,1)S(1)}, u32[]{:S(2)}, u32[]{:S(2)}) collective-permute-start(bf16[2,128,2048]{2,1,0:T(8,128)(2,1)S(1)} %get-tuple-element.30), channel_id=1, source_target_pairs={{0,4},{4,0},{8,12},{12,8},{16,20},{20,16},{24,28},{28,24},{1,5},{5... | collective-permute-start | bytes 3145736 | tf_op jit(solution)/shard_map/ppermute | solution.py:84
  34.3 9.2 %collective-permute-start.2 = (bf16[128,2048]{1,0:T(8,128)(2,1)S(1)}, bf16[128,2048]{1,0:T(8,128)(2,1)S(1)}, u32[]{:S(2)}, u32[]{:S(2)}) collective-permute-start(bf16[128,2048]{1,0:T(8,128)(2,1)S(1)} %get-tuple-element.28.refs_2_), channel_id=1, source_target_pairs={{0,8},{4,20},{8,0},{12,28},{16,24},{20,4},{24,16},{28,12},{1,9},{5... | collective-permute-start | bytes 1572872 | tf_op jit(solution)/shard_map/ppermute | solution.py:89
  34.9 13.3 %collective-permute-start.6 = (bf16[8,32,512]{2,1,0:T(8,128)(2,1)S(1)}, bf16[8,32,512]{2,1,0:T(8,128)(2,1)S(1)}, u32[]{:S(2)}, u32[]{:S(2)}) collective-permute-start(bf16[8,32,512]{2,1,0:T(8,128)(2,1)S(1)} %shard_map.93.refs_5_.refs_1_), channel_id=1, source_target_pairs={{0,4},{4,0},{8,12},{12,8},{16,20},{20,16},{24,28},{28,24},{1,5},{5... | collective-permute-start | bytes 786440 | tf_op jit(solution)/shard_map/ppermute | solution.py:84
  44.1 9.0 %collective-permute-start.4 = (bf16[64,2048]{1,0:T(8,128)(2,1)S(1)}, bf16[64,2048]{1,0:T(8,128)(2,1)S(1)}, u32[]{:S(2)}, u32[]{:S(2)}) collective-permute-start(bf16[64,2048]{1,0:T(8,128)(2,1)S(1)} %shard_map.95.refs_5_), channel_id=1, source_target_pairs={{0,16},{4,12},{8,24},{12,4},{16,0},{20,28},{24,8},{28,20},{1,17},{... | collective-permute-start | bytes 786440 | tf_op jit(solution)/shard_map/ppermute | solution.py:89
  44.8 9.3 %collective-permute-start.13 = (bf16[8,32,512]{2,1,0:T(8,128)(2,1)S(1)}, bf16[8,32,512]{2,1,0:T(8,128)(2,1)S(1)}, u32[]{:S(2)}, u32[]{:S(2)}) collective-permute-start(bf16[8,32,512]{2,1,0:T(8,128)(2,1)S(1)} %all_to_all.20.refs_1_.refs_6_), channel_id=1, source_target_pairs={{0,3},{1,2},{2,1},{3,0},{4,7},{5,6},{6,5},{7,4},{8,11},{9,10},{10,... | collective-permute-start | bytes 786440 | tf_op jit(solution)/shard_map/ppermute | solution.py:84
  52.5 13.7 %collective-permute-start.12 = (bf16[128,2048]{1,0:T(8,128)(2,1)S(1)}, bf16[128,2048]{1,0:T(8,128)(2,1)S(1)}, u32[]{:S(2)}, u32[]{:S(2)}) collective-permute-start(bf16[128,2048]{1,0:T(8,128)(2,1)S(1)} %get-tuple-element.31.refs_8_), channel_id=1, source_target_pairs={{0,8},{4,20},{8,0},{12,28},{16,24},{20,4},{24,16},{28,12},{1,9},{5... | collective-permute-start | bytes 1572872 | tf_op jit(solution)/shard_map/ppermute | solution.py:89
  54.6 1.6 collective-permute-start.14
  54.7 18.4 %collective-permute-start.8 = (bf16[64,4096]{1,0:T(8,128)(2,1)S(1)}, bf16[64,4096]{1,0:T(8,128)(2,1)S(1)}, u32[]{:S(2)}, u32[]{:S(2)}) collective-permute-start(bf16[64,4096]{1,0:T(8,128)(2,1)S(1)} %shard_map.97.refs_2_.refs_1_), channel_id=1, source_target_pairs={{0,16},{4,12},{8,24},{12,4},{16,0},{20,28},{24,8},{28,20},{1,17},{... | collective-permute-start | bytes 1572872 | tf_op jit(solution)/shard_map/ppermute | solution.py:89
  60.5 16.2 %collective-permute-start.16 = (bf16[128,2048]{1,0:T(8,128)(2,1)S(1)}, bf16[128,2048]{1,0:T(8,128)(2,1)S(1)}, u32[]{:S(2)}, u32[]{:S(2)}) collective-permute-start(bf16[128,2048]{1,0:T(8,128)(2,1)S(1)} %get-tuple-element.33.refs_3_), channel_id=1, source_target_pairs={{0,8},{4,20},{8,0},{12,28},{16,24},{20,4},{24,16},{28,12},{1,9},{5... | collective-permute-start | bytes 1572872 | tf_op jit(solution)/shard_map/ppermute | solution.py:89
  62.0 9.6 %collective-permute-start.11 = (bf16[8,32,512]{2,1,0:T(8,128)(2,1)S(1)}, bf16[8,32,512]{2,1,0:T(8,128)(2,1)S(1)}, u32[]{:S(2)}, u32[]{:S(2)}) collective-permute-start(bf16[8,32,512]{2,1,0:T(8,128)(2,1)S(1)} %all_to_all.20.refs_1_.refs_6_), channel_id=1, source_target_pairs={{0,1},{1,0},{2,3},{3,2},{4,5},{5,4},{6,7},{7,6},{8,9},{9,8},{10,11... | collective-permute-start | bytes 786440 | tf_op jit(solution)/shard_map/ppermute | solution.py:84
  66.8 7.4 %collective-permute-start.17 = (bf16[64,2048]{1,0:T(8,128)(2,1)S(1)}, bf16[64,2048]{1,0:T(8,128)(2,1)S(1)}, u32[]{:S(2)}, u32[]{:S(2)}) collective-permute-start(bf16[64,2048]{1,0:T(8,128)(2,1)S(1)} %shard_map.100.refs_2_), channel_id=1, source_target_pairs={{0,16},{4,12},{8,24},{12,4},{16,0},{20,28},{24,8},{28,20},{1,17},{... | collective-permute-start | bytes 786440 | tf_op jit(solution)/shard_map/ppermute | solution.py:89
  71.6 12.8 %collective-permute-start.7 = (bf16[64,4096]{1,0:T(8,128)(2,1)S(1)}, bf16[64,4096]{1,0:T(8,128)(2,1)S(1)}, u32[]{:S(2)}, u32[]{:S(2)}) collective-permute-start(bf16[64,4096]{1,0:T(8,128)(2,1)S(1)} %shard_map.97.refs_2_.refs_1_), channel_id=1, source_target_pairs={{0,8},{4,20},{8,0},{12,28},{16,24},{20,4},{24,16},{28,12},{1,9},{5... | collective-permute-start | bytes 1572872 | tf_op jit(solution)/shard_map/ppermute | solution.py:89
  73.1 22.4 %collective-permute-start.9 = (bf16[64,4096]{1,0:T(8,128)(2,1)S(1)}, bf16[64,4096]{1,0:T(8,128)(2,1)S(1)}, u32[]{:S(2)}, u32[]{:S(2)}) collective-permute-start(bf16[64,4096]{1,0:T(8,128)(2,1)S(1)} %collective-permute-done.8.refs_3_), channel_id=1, source_target_pairs={{0,8},{4,20},{8,0},{12,28},{16,24},{20,4},{24,16},{28,12},{1,9},{5... | collective-permute-start | bytes 1572872 | tf_op jit(solution)/shard_map/ppermute | solution.py:89
  75.1 21.0 %collective-permute-start.18 = (bf16[64,4096]{1,0:T(8,128)(2,1)S(1)}, bf16[64,4096]{1,0:T(8,128)(2,1)S(1)}, u32[]{:S(2)}, u32[]{:S(2)}) collective-permute-start(bf16[64,4096]{1,0:T(8,128)(2,1)S(1)} %shard_map.102.refs_3_.refs_1_), channel_id=1, source_target_pairs={{0,16},{4,12},{8,24},{12,4},{16,0},{20,28},{24,8},{28,20},{1,17},{... | collective-permute-start | bytes 1572872 | tf_op jit(solution)/shard_map/ppermute | solution.py:89
  76.6 1.5 collective-permute-start.15
  78.2 23.5 %collective-permute-start.21 = (bf16[64,2048]{1,0:T(8,128)(2,1)S(1)}, bf16[64,2048]{1,0:T(8,128)(2,1)S(1)}, u32[]{:S(2)}, u32[]{:S(2)}) collective-permute-start(bf16[64,2048]{1,0:T(8,128)(2,1)S(1)} %shard_map.103.refs_5_), channel_id=1, source_target_pairs={{0,16},{4,12},{8,24},{12,4},{16,0},{20,28},{24,8},{28,20},{1,17},{... | collective-permute-start | bytes 786440 | tf_op jit(solution)/shard_map/ppermute | solution.py:89
  84.4 30.3 %collective-permute-start.22 = (bf16[64,4096]{1,0:T(8,128)(2,1)S(1)}, bf16[64,4096]{1,0:T(8,128)(2,1)S(1)}, u32[]{:S(2)}, u32[]{:S(2)}) collective-permute-start(bf16[64,4096]{1,0:T(8,128)(2,1)S(1)} %shard_map.102.refs_3_.refs_1_), channel_id=1, source_target_pairs={{0,8},{4,20},{8,0},{12,28},{16,24},{20,4},{24,16},{28,12},{1,9},{5... | collective-permute-start | bytes 1572872 | tf_op jit(solution)/shard_map/ppermute | solution.py:89
  95.5 16.7 %collective-permute-start.20 = (bf16[128,2048]{1,0:T(8,128)(2,1)S(1)}, bf16[128,2048]{1,0:T(8,128)(2,1)S(1)}, u32[]{:S(2)}, u32[]{:S(2)}) collective-permute-start(bf16[128,2048]{1,0:T(8,128)(2,1)S(1)} %get-tuple-element.35.refs_9_), channel_id=1, source_target_pairs={{0,8},{4,20},{8,0},{12,28},{16,24},{20,4},{24,16},{28,12},{1,9},{5... | collective-permute-start | bytes 1572872 | tf_op jit(solution)/shard_map/ppermute | solution.py:89
  96.1 24.6 %collective-permute-start.23 = (bf16[64,4096]{1,0:T(8,128)(2,1)S(1)}, bf16[64,4096]{1,0:T(8,128)(2,1)S(1)}, u32[]{:S(2)}, u32[]{:S(2)}) collective-permute-start(bf16[64,4096]{1,0:T(8,128)(2,1)S(1)} %collective-permute-done.18.refs_10_.refs_3_), channel_id=1, source_target_pairs={{0,8},{4,20},{8,0},{12,28},{16,24},{20,4},{24,16},{28,12},{1,9},{5... | collective-permute-start | bytes 1572872 | tf_op jit(solution)/shard_map/ppermute | solution.py:89
  102.6 18.1 %collective-permute-start.24 = (bf16[64,4096]{1,0:T(8,128)(2,1)S(1)}, bf16[64,4096]{1,0:T(8,128)(2,1)S(1)}, u32[]{:S(2)}, u32[]{:S(2)}) collective-permute-start(bf16[64,4096]{1,0:T(8,128)(2,1)S(1)} %shard_map.106.refs_3_.refs_1_), channel_id=1, source_target_pairs={{0,16},{4,12},{8,24},{12,4},{16,0},{20,28},{24,8},{28,20},{1,17},{... | collective-permute-start | bytes 1572872 | tf_op jit(solution)/shard_map/ppermute | solution.py:89
  104.2 9.9 %collective-permute-start.19 = (bf16[1,8,32,512]{3,2,1,0:T(8,128)(2,1)S(1)}, bf16[1,8,32,512]{3,2,1,0:T(8,128)(2,1)S(1)}, u32[]{:S(2)}, u32[]{:S(2)}) collective-permute-start(bf16[1,8,32,512]{3,2,1,0:T(8,128)(2,1)S(1)} %get-tuple-element.37), channel_id=1, source_target_pairs={{0,4},{4,0},{8,12},{12,8},{16,20},{20,16},{24,28},{28,24},{1,5},{5... | collective-permute-start | bytes 786440 | tf_op jit(solution)/shard_map/ppermute | solution.py:84
  112.8 12.2 %collective-permute-start.26 = (bf16[64,2048]{1,0:T(8,128)(2,1)S(1)}, bf16[64,2048]{1,0:T(8,128)(2,1)S(1)}, u32[]{:S(2)}, u32[]{:S(2)}) collective-permute-start(bf16[64,2048]{1,0:T(8,128)(2,1)S(1)} %shard_map.107.refs_3_), channel_id=1, source_target_pairs={{0,16},{4,12},{8,24},{12,4},{16,0},{20,28},{24,8},{28,20},{1,17},{... | collective-permute-start | bytes 786440 | tf_op jit(solution)/shard_map/ppermute | solution.py:89
  125.9 14.9 %collective-permute-start.30 = (bf16[64,4096]{1,0:T(8,128)(2,1)S(1)}, bf16[64,4096]{1,0:T(8,128)(2,1)S(1)}, u32[]{:S(2)}, u32[]{:S(2)}) collective-permute-start(bf16[64,4096]{1,0:T(8,128)(2,1)S(1)} %shard_map.110.refs_3_.refs_1_), channel_id=1, source_target_pairs={{0,16},{4,12},{8,24},{12,4},{16,0},{20,28},{24,8},{28,20},{1,17},{... | collective-permute-start | bytes 1572872 | tf_op jit(solution)/shard_map/ppermute | solution.py:89
  127.4 16.3 %collective-permute-start.28 = (bf16[64,4096]{1,0:T(8,128)(2,1)S(1)}, bf16[64,4096]{1,0:T(8,128)(2,1)S(1)}, u32[]{:S(2)}, u32[]{:S(2)}) collective-permute-start(bf16[64,4096]{1,0:T(8,128)(2,1)S(1)} %shard_map.106.refs_3_.refs_1_), channel_id=1, source_target_pairs={{0,8},{4,20},{8,0},{12,28},{16,24},{20,4},{24,16},{28,12},{1,9},{5... | collective-permute-start | bytes 1572872 | tf_op jit(solution)/shard_map/ppermute | solution.py:89
  128.1 15.7 %collective-permute-start.29 = (bf16[64,4096]{1,0:T(8,128)(2,1)S(1)}, bf16[64,4096]{1,0:T(8,128)(2,1)S(1)}, u32[]{:S(2)}, u32[]{:S(2)}) collective-permute-start(bf16[64,4096]{1,0:T(8,128)(2,1)S(1)} %collective-permute-done.24.refs_10_.refs_3_), channel_id=1, source_target_pairs={{0,8},{4,20},{8,0},{12,28},{16,24},{20,4},{24,16},{28,12},{1,9},{5... | collective-permute-start | bytes 1572872 | tf_op jit(solution)/shard_map/ppermute | solution.py:89
  129.4 12.2 %collective-permute-start.25 = (bf16[1,8,32,512]{3,2,1,0:T(8,128)(2,1)S(1)}, bf16[1,8,32,512]{3,2,1,0:T(8,128)(2,1)S(1)}, u32[]{:S(2)}, u32[]{:S(2)}) collective-permute-start(bf16[1,8,32,512]{3,2,1,0:T(8,128)(2,1)S(1)} %get-tuple-element.40), channel_id=1, source_target_pairs={{0,4},{4,0},{8,12},{12,8},{16,20},{20,16},{24,28},{28,24},{1,5},{5... | collective-permute-start | bytes 786440 | tf_op jit(solution)/shard_map/ppermute | solution.py:84
  129.4 24.8 %collective-permute-start.33 = (bf16[64,4096]{1,0:T(8,128)(2,1)S(1)}, bf16[64,4096]{1,0:T(8,128)(2,1)S(1)}, u32[]{:S(2)}, u32[]{:S(2)}) collective-permute-start(bf16[64,4096]{1,0:T(8,128)(2,1)S(1)} %shard_map.110.refs_3_.refs_1_), channel_id=1, source_target_pairs={{0,8},{4,20},{8,0},{12,28},{16,24},{20,4},{24,16},{28,12},{1,9},{5... | collective-permute-start | bytes 1572872 | tf_op jit(solution)/shard_map/ppermute | solution.py:89
  140.8 13.4 %collective-permute-start.34 = (bf16[64,4096]{1,0:T(8,128)(2,1)S(1)}, bf16[64,4096]{1,0:T(8,128)(2,1)S(1)}, u32[]{:S(2)}, u32[]{:S(2)}) collective-permute-start(bf16[64,4096]{1,0:T(8,128)(2,1)S(1)} %collective-permute-done.30.refs_10_.refs_3_), channel_id=1, source_target_pairs={{0,8},{4,20},{8,0},{12,28},{16,24},{20,4},{24,16},{28,12},{1,9},{5... | collective-permute-start | bytes 1572872 | tf_op jit(solution)/shard_map/ppermute | solution.py:89
  142.2 10.1 %collective-permute-start.27 = (bf16[8,32,512]{2,1,0:T(8,128)(2,1)S(1)}, bf16[8,32,512]{2,1,0:T(8,128)(2,1)S(1)}, u32[]{:S(2)}, u32[]{:S(2)}) collective-permute-start(bf16[8,32,512]{2,1,0:T(8,128)(2,1)S(1)} %shard_map.111.refs_9_), channel_id=1, source_target_pairs={{0,2},{1,3},{2,0},{3,1},{4,6},{5,7},{6,4},{7,5},{8,10},{9,11},{10,... | collective-permute-start | bytes 786440 | tf_op jit(solution)/shard_map/ppermute | solution.py:84
  148.0 4.4 %collective-permute-start.31 = (bf16[1,8,32,512]{3,2,1,0:T(8,128)(2,1)S(1)}, bf16[1,8,32,512]{3,2,1,0:T(8,128)(2,1)S(1)}, u32[]{:S(2)}, u32[]{:S(2)}) collective-permute-start(bf16[1,8,32,512]{3,2,1,0:T(8,128)(2,1)S(1)} %get-tuple-element.42), channel_id=1, source_target_pairs={{0,4},{4,0},{8,12},{12,8},{16,20},{20,16},{24,28},{28,24},{1,5},{5... | collective-permute-start | bytes 786440 | tf_op jit(solution)/shard_map/ppermute | solution.py:84
  153.0 8.3 %collective-permute-start.32 = (bf16[8,32,512]{2,1,0:T(8,128)(2,1)S(1)}, bf16[8,32,512]{2,1,0:T(8,128)(2,1)S(1)}, u32[]{:S(2)}, u32[]{:S(2)}) collective-permute-start(bf16[8,32,512]{2,1,0:T(8,128)(2,1)S(1)} %shard_map.113.refs_9_), channel_id=1, source_target_pairs={{0,3},{1,2},{2,1},{3,0},{4,7},{5,6},{6,5},{7,4},{8,11},{9,10},{10,... | collective-permute-start | bytes 786440 | tf_op jit(solution)/shard_map/ppermute | solution.py:84
  158.4 22.0 %copy-start.8 = (bf16[32,128]{1,0:T(8,128)(2,1)S(1)}, bf16[32,128]{1,0:T(8,128)(2,1)}, u32[]{:S(2)}) copy-start(bf16[32,128]{1,0:T(8,128)(2,1)} %get-tuple-element.25) | copy-start | bytes 24580
  158.5 2.9 %collective-permute-start.35 = (bf16[1,8,32,512]{3,2,1,0:T(8,128)(2,1)S(1)}, bf16[1,8,32,512]{3,2,1,0:T(8,128)(2,1)S(1)}, u32[]{:S(2)}, u32[]{:S(2)}) collective-permute-start(bf16[1,8,32,512]{3,2,1,0:T(8,128)(2,1)S(1)} %get-tuple-element.44), channel_id=1, source_target_pairs={{0,4},{4,0},{8,12},{12,8},{16,20},{20,16},{24,28},{28,24},{1,5},{5... | collective-permute-start | bytes 786440 | tf_op jit(solution)/shard_map/ppermute | solution.py:84
  161.9 8.7 %collective-permute-start.36 = (bf16[8,32,512]{2,1,0:T(8,128)(2,1)S(1)}, bf16[8,32,512]{2,1,0:T(8,128)(2,1)S(1)}, u32[]{:S(2)}, u32[]{:S(2)}) collective-permute-start(bf16[8,32,512]{2,1,0:T(8,128)(2,1)S(1)} %shard_map.115), channel_id=1, source_target_pairs={{0,1},{1,0},{2,3},{3,2},{4,5},{5,4},{6,7},{7,6},{8,9},{9,8},{10,11... | collective-permute-start | bytes 786440 | tf_op jit(solution)/shard_map/ppermute | solution.py:84

commit v5 on v4

--- a/solution.py
+++ b/solution.py
@@ -6,12 +6,11 @@
 from jax.sharding import PartitionSpec as P
 
 
-VMEM_LIMIT = 24*1024*1024
+VMEM_LIMIT = 24 * 1024 * 1024
 PACK_LIMIT = 60 * 1024 * 1024
 CHUNKS = (((0,), 0, 32), ((2,), 0, 32), ((3,), 0, 32), ((1,), 0, 32))
-K1_STEPS = 4
-K1_LIMIT = None
-ORDER = (0, 1, -1, 0, 1, 0, 2, 2, 1, 0, 3, 1, 2, 3, 1, 0, 2, 3, 0, 2, 1, 3, 0, 1, 3, 2, 1, 2, 3, 2, 3, 3)
+SUM_STEPS = 4
+ORDER = (0, 1, -1, 0, 1, 2, 0, 2, 0, 1, 3, 1, 2, 3, 1, 0, 2, 3, 0, 2, 3, 0, 1, 1, 3, 2, 1, 2, 3, 2, 3, 3)
 
 
 def swiglu_grads(upstream, gate_pre, up_pre):
@@ -103,7 +102,7 @@
         self.last = []
         self.waits = []
 
-    def call(self, kernel, out_shape, flops, moved, grid, in_specs, out_specs, operands, scratch_shapes=(), limit=None):
+    def call(self, kernel, out_shape, flops, moved, grid, in_specs, out_specs, operands, scratch_shapes=(), limit=None, where=None):
         after = self.last + self.waits
         self.waits = []
         inputs = 1 + len(operands)
@@ -123,7 +122,7 @@
                 out_specs=out_specs,
                 scratch_shapes=scratch_shapes,
             ),
-        )(self.where, *operands, *after)
+        )(self.where if where is None else where, *operands, *after)
         self.last = list(results[:1])
         return results
 
@@ -194,6 +193,7 @@
         [out_grad, routes, gates, lengths],
         [pltpu.VMEM((slots, 1), jnp.float32)],
         PACK_LIMIT,
+        jnp.zeros((1,), jnp.int32),
     )
 
 
@@ -248,7 +248,7 @@
     width = own_down.shape[1]
     block = members * 2 * count
     half = own_down.shape[0] // 2
-    step = half // K1_STEPS
+    step = half // SUM_STEPS
 
     def kernel(where, *refs):
         own_ref, other_ref, send, keep, left = refs[2 * members :]
@@ -267,18 +267,17 @@
         keep[:block], send[:block] = sums[:block], sums[block : 2 * block]
         keep[block:], send[block:] = sums[2 * block : 3 * block], sums[3 * block :]
 
-    weight = pl.BlockSpec((step, width), lambda i, where: (where[0] * K1_STEPS + i, 0))
+    weight = pl.BlockSpec((step, width), lambda i, where: (where[0] * SUM_STEPS + i, 0))
     return steps.call(
         kernel,
         [shape(2 * block, half)] * 2,
         16 * block * width * half,
         4 * half * width + 8 * block * (2 * width + half),
-        (K1_STEPS,),
+        (SUM_STEPS,),
         [whole(x) for x in here + there] + [weight, weight],
         [pl.BlockSpec((2 * block, step), lambda i, where: (0, i))] * 2,
         here + there + [own_down, other_down],
         [pltpu.VMEM((4 * block, 2 * width), jnp.bfloat16)],
-        K1_LIMIT,
     )
 
 

time: 182 us -> 175 us (0.962)
  starting transfers between devices: 39.1 us -> 33.9 us
    ppermute x20, starting transfers between devices: 21 us -> 18.1 us  [exchange(): lax.ppermute(values, 'dp', [(i, i ^ (2 if (i + turn) % 2 == 0 else 4)) fo...]
    ppermute x17, starting transfers between devices: 18.2 us -> 15.7 us  [swap(): return lax.ppermute(values, axis, [(i, i ^ offset) for i in range(size)])]
    unnamed x19 -> x17, local copies, waits for them, and re-layouts: 3.85 us -> 4.11 us
  transfers between devices with their start and end apart: 37 -> 37, of which waited for: 12 -> 18; matrix products, arithmetic and copies ran while one was open for 0% -> 0% of each run, Pallas kernels for 25% -> 26%
where the time goes in v5:
time: 175 us; the launch traced here: 174 us
  waiting for transfers between devices  64.9 us (37%)
  Pallas kernels  48.1 us (27%)
  starting transfers between devices  33.9 us (19%)
  blocking collectives  21.1 us (12%)
  local copies, waits for them, and re-layouts  4.19 us (2%)
    pallas_call x25, Pallas kernels, call(): pl.pallas_call(ordered, out_shape=out_shape, cost_estimate=pl.CostEstimat...  48.1 us
    ppermute x20, waiting for transfers between devices, exchange(): lax.ppermute(values, 'dp', [(i, i ^ (2 if (i + turn) % 2 == 0 else 4)) fo...  43.8 us
    ppermute x17, waiting for transfers between devices, swap(): return lax.ppermute(values, axis, [(i, i ^ offset) for i in range(size)])  21.1 us
    ppermute x20, starting transfers between devices, exchange(): lax.ppermute(values, 'dp', [(i, i ^ (2 if (i + turn) % 2 == 0 else 4)) fo...  18.1 us
    ppermute x17, starting transfers between devices, swap(): return lax.ppermute(values, axis, [(i, i ^ offset) for i in range(size)])  15.7 us
    all_to_all x1, blocking collectives, per_device(): rows = lax.all_to_all(rows, 'dp', split_axis=0, concat_axis=0, tiled=True)  11.8 us
    all_to_all x1, blocking collectives, per_device(): summed = lax.all_to_all(summed, 'dp', split_axis=0, concat_axis=1)  9.35 us
    unnamed x17, local copies, waits for them, and re-layouts  4.11 us
  transfers between devices with their start and end apart: 37, of which 18 were waited for; matrix products, arithmetic and copies ran while one was open for 0% of the time, Pallas kernels for 26%

profile of v5, /device:TPU:0, one launch (start us, length us, event | category | flops | bytes accessed | tf_op | source)
XLA Modules:
  0.0 174.1 jit_solution(7593983222401162122)
XLA Ops:
  0.5 2.4 %shard_map.91 = (bf16[8,32,512]{2,1,0:T(8,128)(2,1)}, bf16[32,128]{1,0:T(8,128)(2,1)}) custom-call(s32[1]{0:T(128)} %constant.23.clone.1.refs_0_, bf16[128,4096]{1,0:T(8,128)(2,1)} %refs_1_.2, s32[2,128]{1,0:T(2,128)} %bitcast.29, f32[2,128]{1,0:T(2,128)} %bitcast.30, s32[1,8]{1,0:T(1,128)} %refs_4_.6), custom_call_target="tpu_custom_call" | custom-call | flops 33554432 | bytes 1310720 | tf_op jit(solution)/shard_map/pallas_call | solution.py:113
  2.8 11.8 %all_to_all.20.refs_1_.refs_6_ = bf16[8,32,512]{2,1,0:T(8,128)(2,1)S(1)} all-to-all(bf16[8,32,512]{2,1,0:T(8,128)(2,1)} %get-tuple-element.26.refs_5_), channel_id=1, replica_groups=mesh['dp'=8,'et'=4] {'dp'}, dimensions={0} | all-to-all | bytes 524288 | tf_op jit(solution)/shard_map/all_to_all | solution.py:476
  14.6 2.6 %collective-permute-start.3 = (bf16[8,32,512]{2,1,0:T(8,128)(2,1)S(1)}, bf16[8,32,512]{2,1,0:T(8,128)(2,1)S(1)}, u32[]{:S(2)}, u32[]{:S(2)}) collective-permute-start(bf16[8,32,512]{2,1,0:T(8,128)(2,1)S(1)} %all_to_all.20.refs_1_.refs_6_), channel_id=1, source_target_pairs={{0,2},{1,3},{2,0},{3,1},{4,6},{5,7},{6,4},{7,5},{8,10},{9,11},{10,... | collective-permute-start | bytes 786440 | tf_op jit(solution)/shard_map/ppermute | solution.py:83
  17.3 2.3 %copy-done.2 = bf16[4096,512]{1,0:T(8,128)(2,1)S(1)} copy-done((bf16[4096,512]{1,0:T(8,128)(2,1)S(1)}, bf16[4096,512]{1,0:T(8,128)(2,1)}, u32[]{:S(2)}) %copy-start.2) | copy-done | bytes 4194328
  19.7 1.7 copy-done.6
  21.4 4.3 %shard_map.92 = (bf16[128,2048]{1,0:T(8,128)(2,1)S(1)}, bf16[128,2048]{1,0:T(8,128)(2,1)S(1)}) custom-call(s32[10]{0:T(128)S(1)} %stack.43.refs_0_, bf16[8,32,512]{2,1,0:T(8,128)(2,1)S(1)} %all_to_all.20.refs_1_.refs_6_, bf16[8,32,512]{2,1,0:T(8,128)(2,1)S(1)} %collective-permute-done.refs_2_, bf16[4096,512]{1,0:T(8,128)(2,1)S(1)} %copy-done.2, ...), custom_call_target="tpu_custom_call" | custom-call | flops 1073741824 | bytes 5767168 | tf_op jit(solution)/shard_map/pallas_call | solution.py:113
  25.7 4.1 %collective-permute-done.3.refs_1_ = bf16[8,32,512]{2,1,0:T(8,128)(2,1)S(1)} collective-permute-done((bf16[8,32,512]{2,1,0:T(8,128)(2,1)S(1)}, bf16[8,32,512]{2,1,0:T(8,128)(2,1)S(1)}, u32[]{:S(2)}, u32[]{:S(2)}) %collective-permute-start.3) | collective-permute-done | bytes 262176 | tf_op jit(solution)/shard_map/ppermute | solution.py:83
  29.8 0.6 shard_map.93.refs_5_.refs_1_
  30.4 1.8 %shard_map.94 = (bf16[2,512,2048]{2,1,0:T(8,128)(2,1)S(1)}, bf16[2,128,2048]{2,1,0:T(8,128)(2,1)S(1)}) custom-call(s32[10]{0:T(128)S(1)} %stack.43.refs_0_, bf16[512,4096]{1,0:T(8,128)(2,1)S(1)} %copy-done, bf16[512,4096]{1,0:T(8,128)(2,1)S(1)} %copy-done.1, bf16[1,128,4096]{2,1,0:T(8,128)(2,1)S(1)} %copy-done.4, bf16[1,128,4096]{2,1,0:T(8,128)(2,1)S(1)} %copy-done.5, ...), custom_call_target="tpu_custom_call" | custom-call | bytes 10485760 | tf_op jit(solution)/shard_map/pallas_call | solution.py:113
  32.9 0.6 collective-permute-start.2
  33.4 3.5 %collective-permute-start.6 = (bf16[8,32,512]{2,1,0:T(8,128)(2,1)S(1)}, bf16[8,32,512]{2,1,0:T(8,128)(2,1)S(1)}, u32[]{:S(2)}, u32[]{:S(2)}) collective-permute-start(bf16[8,32,512]{2,1,0:T(8,128)(2,1)S(1)} %all_to_all.20.refs_1_.refs_6_), channel_id=1, source_target_pairs={{0,3},{1,2},{2,1},{3,0},{4,7},{5,6},{6,5},{7,4},{8,11},{9,10},{10,... | collective-permute-start | bytes 786440 | tf_op jit(solution)/shard_map/ppermute | solution.py:83
  36.9 5.1 %collective-permute-done.2.refs_2_ = bf16[128,2048]{1,0:T(8,128)(2,1)S(1)} collective-permute-done((bf16[128,2048]{1,0:T(8,128)(2,1)S(1)}, bf16[128,2048]{1,0:T(8,128)(2,1)S(1)}, u32[]{:S(2)}, u32[]{:S(2)}) %collective-permute-start.2) | collective-permute-done | bytes 524320 | tf_op jit(solution)/shard_map/ppermute | solution.py:88
  42.0 0.6 shard_map.95.refs_5_
  42.6 0.6 collective-permute-start.4
  43.3 4.3 %shard_map.96 = (bf16[128,2048]{1,0:T(8,128)(2,1)S(1)}, bf16[128,2048]{1,0:T(8,128)(2,1)S(1)}) custom-call(s32[10]{0:T(128)S(1)} %stack.43.refs_0_, bf16[8,32,512]{2,1,0:T(8,128)(2,1)S(1)} %shard_map.93.refs_5_.refs_1_, bf16[8,32,512]{2,1,0:T(8,128)(2,1)S(1)} %collective-permute-done.7.refs_2_, bf16[4096,512]{1,0:T(8,128)(2,1)S(1)} %copy-done.3, ...), custom_call_target="tpu_custom_call" | custom-call | flops 1073741824 | bytes 5767168 | tf_op jit(solution)/shard_map/pallas_call | solution.py:113
  47.5 0.6 collective-permute-start.13
  48.2 0.6 shard_map.97.refs_8_.refs_1_
  49.1 0.9 shard_map.98.refs_5_.refs_1_
  50.0 1.2 collective-permute-start.9
  51.2 1.5 collective-permute-done.14.refs_2_
  52.7 4.3 %shard_map.99 = (bf16[128,2048]{1,0:T(8,128)(2,1)S(1)}, bf16[128,2048]{1,0:T(8,128)(2,1)S(1)}) custom-call(s32[10]{0:T(128)S(1)} %stack.43.refs_0_, bf16[8,32,512]{2,1,0:T(8,128)(2,1)S(1)} %shard_map.97.refs_8_.refs_1_, bf16[8,32,512]{2,1,0:T(8,128)(2,1)S(1)} %collective-permute-done.14.refs_2_, bf16[4096,512]{1,0:T(8,128)(2,1)S(1)} %copy-done.3, ...), custom_call_target="tpu_custom_call" | custom-call | flops 1073741824 | bytes 5767168 | tf_op jit(solution)/shard_map/pallas_call | solution.py:113
  57.0 1.5 collective-permute-start.16
  58.5 0.7 collective-permute-start.12
  59.2 3.0 %collective-permute-done.13.refs_2_ = bf16[128,2048]{1,0:T(8,128)(2,1)S(1)} collective-permute-done((bf16[128,2048]{1,0:T(8,128)(2,1)S(1)}, bf16[128,2048]{1,0:T(8,128)(2,1)S(1)}, u32[]{:S(2)}, u32[]{:S(2)}) %collective-permute-start.13) | collective-permute-done | bytes 524320 | tf_op jit(solution)/shard_map/ppermute | solution.py:88
  62.2 0.6 shard_map.100.refs_2_
  62.8 1.5 collective-permute-start.17
  64.5 1.5 collective-permute-done.12.refs_1_
  66.0 1.1 collective-permute-start.10
  67.7 4.2 %collective-permute-done.17.refs_3_ = bf16[64,2048]{1,0:T(8,128)(2,1)S(1)} collective-permute-done((bf16[64,2048]{1,0:T(8,128)(2,1)S(1)}, bf16[64,2048]{1,0:T(8,128)(2,1)S(1)}, u32[]{:S(2)}, u32[]{:S(2)}) %collective-permute-start.17) | collective-permute-done | bytes 262176 | tf_op jit(solution)/shard_map/ppermute | solution.py:88
  71.8 0.9 shard_map.102.refs_3_.refs_1_
  72.7 1.5 collective-permute-start.18
  74.2 0.6 shard_map.103.refs_5_
  74.8 0.9 collective-permute-done.15.refs_2_
  75.7 0.6 collective-permute-start.21
  76.4 4.2 %shard_map.104 = (bf16[128,2048]{1,0:T(8,128)(2,1)S(1)}, bf16[128,2048]{1,0:T(8,128)(2,1)S(1)}) custom-call(s32[10]{0:T(128)S(1)} %stack.43.refs_0_, bf16[8,32,512]{2,1,0:T(8,128)(2,1)S(1)} %shard_map.101.refs_8_.refs_1_, bf16[8,32,512]{2,1,0:T(8,128)(2,1)S(1)} %collective-permute-done.15.refs_2_, bf16[4096,512]{1,0:T(8,128)(2,1)S(1)} %copy-done.3, ...), custom_call_target="tpu_custom_call" | custom-call | flops 1073741824 | bytes 5767168 | tf_op jit(solution)/shard_map/pallas_call | solution.py:113
  81.2 7.8 %collective-permute-done.10.refs_4_ = bf16[64,4096]{1,0:T(8,128)(2,1)S(1)} collective-permute-done((bf16[64,4096]{1,0:T(8,128)(2,1)S(1)}, bf16[64,4096]{1,0:T(8,128)(2,1)S(1)}, u32[]{:S(2)}, u32[]{:S(2)}) %collective-permute-start.10) | collective-permute-done | bytes 524320 | tf_op jit(solution)/shard_map/ppermute | solution.py:88
  89.0 4.2 %shard_map.105 = (f32[1,8,32,512]{3,2,1,0:T(8,128)S(1)}, bf16[1,8,32,512]{3,2,1,0:T(8,128)(2,1)S(1)}) custom-call(s32[10]{0:T(128)S(1)} %stack.43.refs_0_, bf16[64,4096]{1,0:T(8,128)(2,1)S(1)} %shard_map.98.refs_5_.refs_1_, bf16[64,4096]{1,0:T(8,128)(2,1)S(1)} %collective-permute-done.8.refs_2_, bf16[64,4096]{1,0:T(8,128)(2,1)S(1)} %collective-permute-done.9.refs_4_.refs_3_, ...), custom_call_target="tpu_custom_call" | custom-call | flops 2147483648 | bytes 11272192 | tf_op jit(solution)/shard_map/pallas_call | solution.py:113
  93.3 0.9 shard_map.106.refs_3_.refs_1_
  94.2 1.5 collective-permute-start.25
  95.6 2.0 %collective-permute-start.23 = (bf16[64,4096]{1,0:T(8,128)(2,1)S(1)}, bf16[64,4096]{1,0:T(8,128)(2,1)S(1)}, u32[]{:S(2)}, u32[]{:S(2)}) collective-permute-start(bf16[64,4096]{1,0:T(8,128)(2,1)S(1)} %collective-permute-done.18.refs_10_.refs_3_), channel_id=1, source_target_pairs={{0,8},{4,20},{8,0},{12,28},{16,24},{20,4},{24,16},{28,12},{1,9},{5... | collective-permute-start | bytes 1572872 | tf_op jit(solution)/shard_map/ppermute | solution.py:88
  97.6 0.6 shard_map.107.refs_3_
  98.3 0.7 collective-permute-start.24
  99.2 0.6 shard_map.108.refs_8_.refs_10_
  99.8 14.9 %collective-permute-done.24.refs_3_ = bf16[64,2048]{1,0:T(8,128)(2,1)S(1)} collective-permute-done((bf16[64,2048]{1,0:T(8,128)(2,1)S(1)}, bf16[64,2048]{1,0:T(8,128)(2,1)S(1)}, u32[]{:S(2)}, u32[]{:S(2)}) %collective-permute-start.24) | collective-permute-done | bytes 262176 | tf_op jit(solution)/shard_map/ppermute | solution.py:88
  114.7 0.9 shard_map.109.refs_9_.refs_1_
  115.5 1.4 collective-permute-start.30
  117.0 2.0 %collective-permute-start.29 = (bf16[64,4096]{1,0:T(8,128)(2,1)S(1)}, bf16[64,4096]{1,0:T(8,128)(2,1)S(1)}, u32[]{:S(2)}, u32[]{:S(2)}) collective-permute-start(bf16[64,4096]{1,0:T(8,128)(2,1)S(1)} %collective-permute-done.25.refs_9_.refs_3_), channel_id=1, source_target_pairs={{0,8},{4,20},{8,0},{12,28},{16,24},{20,4},{24,16},{28,12},{1,9},{5... | collective-permute-start | bytes 1572872 | tf_op jit(solution)/shard_map/ppermute | solution.py:88
  119.0 4.2 %shard_map.110 = (f32[1,8,32,512]{3,2,1,0:T(8,128)S(1)}, bf16[1,8,32,512]{3,2,1,0:T(8,128)(2,1)S(1)}) custom-call(s32[10]{0:T(128)S(1)} %stack.43.refs_0_, bf16[64,4096]{1,0:T(8,128)(2,1)S(1)} %shard_map.102.refs_3_.refs_1_, bf16[64,4096]{1,0:T(8,128)(2,1)S(1)} %collective-permute-done.22.refs_2_, ...), custom_call_target="tpu_custom_call" | custom-call | flops 2147483648 | bytes 11272192 | tf_op jit(solution)/shard_map/pallas_call | solution.py:113
  123.4 7.0 %collective-permute-done.30.refs_10_.refs_3_ = bf16[64,4096]{1,0:T(8,128)(2,1)S(1)} collective-permute-done((bf16[64,4096]{1,0:T(8,128)(2,1)S(1)}, bf16[64,4096]{1,0:T(8,128)(2,1)S(1)}, u32[]{:S(2)}, u32[]{:S(2)}) %collective-permute-start.30) | collective-permute-done | bytes 524320 | tf_op jit(solution)/shard_map/ppermute | solution.py:88
  130.9 0.6 shard_map.111.refs_9_
  131.6 0.8 collective-permute-done.29.refs_4_
  132.5 4.2 %shard_map.112 = (f32[1,8,32,512]{3,2,1,0:T(8,128)S(1)}, bf16[1,8,32,512]{3,2,1,0:T(8,128)(2,1)S(1)}) custom-call(s32[10]{0:T(128)S(1)} %stack.43.refs_0_, bf16[64,4096]{1,0:T(8,128)(2,1)S(1)} %shard_map.106.refs_3_.refs_1_, bf16[64,4096]{1,0:T(8,128)(2,1)S(1)} %collective-permute-done.28.refs_2_, ...), custom_call_target="tpu_custom_call" | custom-call | flops 2147483648 | bytes 11272192 | tf_op jit(solution)/shard_map/pallas_call | solution.py:113
  136.7 0.9 collective-permute-start.31
  137.6 4.1 %collective-permute-done.27.refs_4_ = bf16[8,32,512]{2,1,0:T(8,128)(2,1)S(1)} collective-permute-done((bf16[8,32,512]{2,1,0:T(8,128)(2,1)S(1)}, bf16[8,32,512]{2,1,0:T(8,128)(2,1)S(1)}, u32[]{:S(2)}, u32[]{:S(2)}) %collective-permute-start.27) | collective-permute-done | bytes 262176 | tf_op jit(solution)/shard_map/ppermute | solution.py:83
  141.7 0.6 shard_map.113.refs_9_
  142.3 1.0 collective-permute-start.32
  143.7 4.2 %shard_map.114 = (f32[1,8,32,512]{3,2,1,0:T(8,128)S(1)}, bf16[1,8,32,512]{3,2,1,0:T(8,128)(2,1)S(1)}) custom-call(s32[10]{0:T(128)S(1)} %stack.43.refs_0_, bf16[64,4096]{1,0:T(8,128)(2,1)S(1)} %shard_map.109.refs_9_.refs_1_, bf16[64,4096]{1,0:T(8,128)(2,1)S(1)} %collective-permute-done.33.refs_2_, ...), custom_call_target="tpu_custom_call" | custom-call | flops 2147483648 | bytes 11272192 | tf_op jit(solution)/shard_map/pallas_call | solution.py:113
  147.9 0.6 collective-permute-start.35
  148.5 2.1 %collective-permute-done.32.refs_4_ = bf16[8,32,512]{2,1,0:T(8,128)(2,1)S(1)} collective-permute-done((bf16[8,32,512]{2,1,0:T(8,128)(2,1)S(1)}, bf16[8,32,512]{2,1,0:T(8,128)(2,1)S(1)}, u32[]{:S(2)}, u32[]{:S(2)}) %collective-permute-start.32) | collective-permute-done | bytes 262176 | tf_op jit(solution)/shard_map/ppermute | solution.py:83
  150.6 0.6 shard_map.115
  151.2 5.4 %collective-permute-start.36 = (bf16[8,32,512]{2,1,0:T(8,128)(2,1)S(1)}, bf16[8,32,512]{2,1,0:T(8,128)(2,1)S(1)}, u32[]{:S(2)}, u32[]{:S(2)}) collective-permute-start(bf16[8,32,512]{2,1,0:T(8,128)(2,1)S(1)} %shard_map.115), channel_id=1, source_target_pairs={{0,1},{1,0},{2,3},{3,2},{4,5},{5,4},{6,7},{7,6},{8,9},{9,8},{10,11... | collective-permute-start | bytes 786440 | tf_op jit(solution)/shard_map/ppermute | solution.py:83
  156.6 6.5 %collective-permute-done.36 = bf16[8,32,512]{2,1,0:T(8,128)(2,1)S(1)} collective-permute-done((bf16[8,32,512]{2,1,0:T(8,128)(2,1)S(1)}, bf16[8,32,512]{2,1,0:T(8,128)(2,1)S(1)}, u32[]{:S(2)}, u32[]{:S(2)}) %collective-permute-start.36) | collective-permute-done | bytes 262176 | tf_op jit(solution)/shard_map/ppermute | solution.py:83
  163.3 9.3 %all_to_all.21 = bf16[8,32,1,512]{3,1,2,0:T(8,128)(2,1)S(1)} all-to-all(bf16[8,32,1,512]{3,1,2,0:T(8,128)(2,1)S(1)} %fusion), channel_id=1, replica_groups=mesh['dp'=8,'et'=4] {'dp'}, dimensions={0} | all-to-all | bytes 524288 | tf_op jit(solution)/shard_map/all_to_all | solution.py:497
  172.6 1.4 convolution_convert_fusion
  (57 shorter events, 4.4 us)
Async XLA Ops:
  0.0 17.3 %collective-permute-start.1 = (bf16[4096,512]{1,0:T(8,128)(2,1)}, bf16[4096,512]{1,0:T(8,128)(2,1)}, u32[]{:S(2)}, u32[]{:S(2)}) collective-permute-start(bf16[4096,512]{1,0:T(8,128)(2,1)} %refs_3_.9), channel_id=1, source_target_pairs={{0,4},{4,0},{8,12},{12,8},{16,20},{20,16},{24,28},{28,24},{1,5},{5... | collective-permute-start | bytes 12582920 | tf_op jit(solution)/shard_map/ppermute | solution.py:83
  14.6 2.7 %collective-permute-start = (bf16[8,32,512]{2,1,0:T(8,128)(2,1)S(1)}, bf16[8,32,512]{2,1,0:T(8,128)(2,1)S(1)}, u32[]{:S(2)}, u32[]{:S(2)}) collective-permute-start(bf16[8,32,512]{2,1,0:T(8,128)(2,1)S(1)} %all_to_all.20.refs_1_.refs_6_), channel_id=1, source_target_pairs={{0,4},{4,0},{8,12},{12,8},{16,20},{20,16},{24,28},{28,24},{1,5},{5... | collective-permute-start | bytes 786440 | tf_op jit(solution)/shard_map/ppermute | solution.py:83
  14.6 15.2 %collective-permute-start.3 = (bf16[8,32,512]{2,1,0:T(8,128)(2,1)S(1)}, bf16[8,32,512]{2,1,0:T(8,128)(2,1)S(1)}, u32[]{:S(2)}, u32[]{:S(2)}) collective-permute-start(bf16[8,32,512]{2,1,0:T(8,128)(2,1)S(1)} %all_to_all.20.refs_1_.refs_6_), channel_id=1, source_target_pairs={{0,2},{1,3},{2,0},{3,1},{4,6},{5,7},{6,4},{7,5},{8,10},{9,11},{10,... | collective-permute-start | bytes 786440 | tf_op jit(solution)/shard_map/ppermute | solution.py:83
  17.3 13.1 %copy-start = (bf16[512,4096]{1,0:T(8,128)(2,1)S(1)}, bf16[512,4096]{1,0:T(8,128)(2,1)}, u32[]{:S(2)}) copy-start(bf16[512,4096]{1,0:T(8,128)(2,1)} %refs_5_.15) | copy-start | bytes 12582916
  17.3 13.1 %copy-start.1 = (bf16[512,4096]{1,0:T(8,128)(2,1)S(1)}, bf16[512,4096]{1,0:T(8,128)(2,1)}, u32[]{:S(2)}) copy-start(bf16[512,4096]{1,0:T(8,128)(2,1)} %refs_6_.7) | copy-start | bytes 12582916
  17.3 2.3 %copy-start.2 = (bf16[4096,512]{1,0:T(8,128)(2,1)S(1)}, bf16[4096,512]{1,0:T(8,128)(2,1)}, u32[]{:S(2)}) copy-start(bf16[4096,512]{1,0:T(8,128)(2,1)} %refs_3_.9) | copy-start | bytes 12582916
  19.6 1.7 copy-start.6
  21.4 9.0 %copy-start.4 = (bf16[1,128,4096]{2,1,0:T(8,128)(2,1)S(1)}, bf16[1,128,4096]{2,1,0:T(8,128)(2,1)}, u32[]{:S(2)}) copy-start(bf16[1,128,4096]{2,1,0:T(8,128)(2,1)} %refs_4_.11) | copy-start | bytes 3145732
  21.4 9.0 %copy-start.5 = (bf16[1,128,4096]{2,1,0:T(8,128)(2,1)S(1)}, bf16[1,128,4096]{2,1,0:T(8,128)(2,1)}, u32[]{:S(2)}) copy-start(bf16[1,128,4096]{2,1,0:T(8,128)(2,1)} %refs_5_.12) | copy-start | bytes 3145732
  32.3 11.0 %copy-start.3 = (bf16[4096,512]{1,0:T(8,128)(2,1)S(1)}, bf16[4096,512]{1,0:T(8,128)(2,1)}, u32[]{:S(2)}) copy-start(bf16[4096,512]{1,0:T(8,128)(2,1)} %refs_3_.9) | copy-start | bytes 12582916
  32.3 56.7 %collective-permute-start.11 = (bf16[2,512,2048]{2,1,0:T(8,128)(2,1)S(1)}, bf16[2,512,2048]{2,1,0:T(8,128)(2,1)S(1)}, u32[]{:S(2)}, u32[]{:S(2)}) collective-permute-start(bf16[2,512,2048]{2,1,0:T(8,128)(2,1)S(1)} %get-tuple-element.29.refs_3_), channel_id=1, source_target_pairs={{0,4},{4,0},{8,12},{12,8},{16,20},{20,16},{24,28},{28,24},{1,5},{5... | collective-permute-start | bytes 12582920 | tf_op jit(solution)/shard_map/ppermute | solution.py:83
  32.4 16.7 %collective-permute-start.5 = (bf16[2,128,2048]{2,1,0:T(8,128)(2,1)S(1)}, bf16[2,128,2048]{2,1,0:T(8,128)(2,1)S(1)}, u32[]{:S(2)}, u32[]{:S(2)}) collective-permute-start(bf16[2,128,2048]{2,1,0:T(8,128)(2,1)S(1)} %get-tuple-element.30), channel_id=1, source_target_pairs={{0,4},{4,0},{8,12},{12,8},{16,20},{20,16},{24,28},{28,24},{1,5},{5... | collective-permute-start | bytes 3145736 | tf_op jit(solution)/shard_map/ppermute | solution.py:83
  32.9 9.2 %collective-permute-start.2 = (bf16[128,2048]{1,0:T(8,128)(2,1)S(1)}, bf16[128,2048]{1,0:T(8,128)(2,1)S(1)}, u32[]{:S(2)}, u32[]{:S(2)}) collective-permute-start(bf16[128,2048]{1,0:T(8,128)(2,1)S(1)} %get-tuple-element.28.refs_2_), channel_id=1, source_target_pairs={{0,8},{4,20},{8,0},{12,28},{16,24},{20,4},{24,16},{28,12},{1,9},{5... | collective-permute-start | bytes 1572872 | tf_op jit(solution)/shard_map/ppermute | solution.py:88
  33.4 9.9 %collective-permute-start.7 = (bf16[8,32,512]{2,1,0:T(8,128)(2,1)S(1)}, bf16[8,32,512]{2,1,0:T(8,128)(2,1)S(1)}, u32[]{:S(2)}, u32[]{:S(2)}) collective-permute-start(bf16[8,32,512]{2,1,0:T(8,128)(2,1)S(1)} %shard_map.93.refs_5_.refs_1_), channel_id=1, source_target_pairs={{0,4},{4,0},{8,12},{12,8},{16,20},{20,16},{24,28},{28,24},{1,5},{5... | collective-permute-start | bytes 786440 | tf_op jit(solution)/shard_map/ppermute | solution.py:83
  33.4 14.7 %collective-permute-start.6 = (bf16[8,32,512]{2,1,0:T(8,128)(2,1)S(1)}, bf16[8,32,512]{2,1,0:T(8,128)(2,1)S(1)}, u32[]{:S(2)}, u32[]{:S(2)}) collective-permute-start(bf16[8,32,512]{2,1,0:T(8,128)(2,1)S(1)} %all_to_all.20.refs_1_.refs_6_), channel_id=1, source_target_pairs={{0,3},{1,2},{2,1},{3,0},{4,7},{5,6},{6,5},{7,4},{8,11},{9,10},{10,... | collective-permute-start | bytes 786440 | tf_op jit(solution)/shard_map/ppermute | solution.py:83
  42.6 6.4 %collective-permute-start.4 = (bf16[64,2048]{1,0:T(8,128)(2,1)S(1)}, bf16[64,2048]{1,0:T(8,128)(2,1)S(1)}, u32[]{:S(2)}, u32[]{:S(2)}) collective-permute-start(bf16[64,2048]{1,0:T(8,128)(2,1)S(1)} %shard_map.95.refs_5_), channel_id=1, source_target_pairs={{0,16},{4,12},{8,24},{12,4},{16,0},{20,28},{24,8},{28,20},{1,17},{... | collective-permute-start | bytes 786440 | tf_op jit(solution)/shard_map/ppermute | solution.py:88
  47.5 14.7 %collective-permute-start.13 = (bf16[128,2048]{1,0:T(8,128)(2,1)S(1)}, bf16[128,2048]{1,0:T(8,128)(2,1)S(1)}, u32[]{:S(2)}, u32[]{:S(2)}) collective-permute-start(bf16[128,2048]{1,0:T(8,128)(2,1)S(1)} %get-tuple-element.31.refs_2_), channel_id=1, source_target_pairs={{0,8},{4,20},{8,0},{12,28},{16,24},{20,4},{24,16},{28,12},{1,9},{5... | collective-permute-start | bytes 1572872 | tf_op jit(solution)/shard_map/ppermute | solution.py:88
  50.0 12.3 %collective-permute-start.9 = (bf16[64,4096]{1,0:T(8,128)(2,1)S(1)}, bf16[64,4096]{1,0:T(8,128)(2,1)S(1)}, u32[]{:S(2)}, u32[]{:S(2)}) collective-permute-start(bf16[64,4096]{1,0:T(8,128)(2,1)S(1)} %shard_map.98.refs_5_.refs_1_), channel_id=1, source_target_pairs={{0,16},{4,12},{8,24},{12,4},{16,0},{20,28},{24,8},{28,20},{1,17},{... | collective-permute-start | bytes 1572872 | tf_op jit(solution)/shard_map/ppermute | solution.py:88
  51.2 1.5 collective-permute-start.14
  57.0 17.2 %collective-permute-start.16 = (bf16[128,2048]{1,0:T(8,128)(2,1)S(1)}, bf16[128,2048]{1,0:T(8,128)(2,1)S(1)}, u32[]{:S(2)}, u32[]{:S(2)}) collective-permute-start(bf16[128,2048]{1,0:T(8,128)(2,1)S(1)} %get-tuple-element.33.refs_3_), channel_id=1, source_target_pairs={{0,8},{4,20},{8,0},{12,28},{16,24},{20,4},{24,16},{28,12},{1,9},{5... | collective-permute-start | bytes 1572872 | tf_op jit(solution)/shard_map/ppermute | solution.py:88
  58.5 7.5 %collective-permute-start.12 = (bf16[8,32,512]{2,1,0:T(8,128)(2,1)S(1)}, bf16[8,32,512]{2,1,0:T(8,128)(2,1)S(1)}, u32[]{:S(2)}, u32[]{:S(2)}) collective-permute-start(bf16[8,32,512]{2,1,0:T(8,128)(2,1)S(1)} %all_to_all.20.refs_1_.refs_6_), channel_id=1, source_target_pairs={{0,1},{1,0},{2,3},{3,2},{4,5},{5,4},{6,7},{7,6},{8,9},{9,8},{10,11... | collective-permute-start | bytes 786440 | tf_op jit(solution)/shard_map/ppermute | solution.py:83
  62.8 9.0 %collective-permute-start.17 = (bf16[64,2048]{1,0:T(8,128)(2,1)S(1)}, bf16[64,2048]{1,0:T(8,128)(2,1)S(1)}, u32[]{:S(2)}, u32[]{:S(2)}) collective-permute-start(bf16[64,2048]{1,0:T(8,128)(2,1)S(1)} %shard_map.100.refs_2_), channel_id=1, source_target_pairs={{0,16},{4,12},{8,24},{12,4},{16,0},{20,28},{24,8},{28,20},{1,17},{... | collective-permute-start | bytes 786440 | tf_op jit(solution)/shard_map/ppermute | solution.py:88
  64.3 16.3 %collective-permute-start.8 = (bf16[64,4096]{1,0:T(8,128)(2,1)S(1)}, bf16[64,4096]{1,0:T(8,128)(2,1)S(1)}, u32[]{:S(2)}, u32[]{:S(2)}) collective-permute-start(bf16[64,4096]{1,0:T(8,128)(2,1)S(1)} %shard_map.98.refs_5_.refs_1_), channel_id=1, source_target_pairs={{0,8},{4,20},{8,0},{12,28},{16,24},{20,4},{24,16},{28,12},{1,9},{5... | collective-permute-start | bytes 1572872 | tf_op jit(solution)/shard_map/ppermute | solution.py:88
  66.0 23.0 %collective-permute-start.10 = (bf16[64,4096]{1,0:T(8,128)(2,1)S(1)}, bf16[64,4096]{1,0:T(8,128)(2,1)S(1)}, u32[]{:S(2)}, u32[]{:S(2)}) collective-permute-start(bf16[64,4096]{1,0:T(8,128)(2,1)S(1)} %collective-permute-done.9.refs_4_.refs_3_), channel_id=1, source_target_pairs={{0,8},{4,20},{8,0},{12,28},{16,24},{20,4},{24,16},{28,12},{1,9},{5... | collective-permute-start | bytes 1572872 | tf_op jit(solution)/shard_map/ppermute | solution.py:88
  72.7 16.2 %collective-permute-start.18 = (bf16[64,4096]{1,0:T(8,128)(2,1)S(1)}, bf16[64,4096]{1,0:T(8,128)(2,1)S(1)}, u32[]{:S(2)}, u32[]{:S(2)}) collective-permute-start(bf16[64,4096]{1,0:T(8,128)(2,1)S(1)} %shard_map.102.refs_3_.refs_1_), channel_id=1, source_target_pairs={{0,16},{4,12},{8,24},{12,4},{16,0},{20,28},{24,8},{28,20},{1,17},{... | collective-permute-start | bytes 1572872 | tf_op jit(solution)/shard_map/ppermute | solution.py:88
  74.2 1.5 collective-permute-start.15
  75.7 17.5 %collective-permute-start.21 = (bf16[64,2048]{1,0:T(8,128)(2,1)S(1)}, bf16[64,2048]{1,0:T(8,128)(2,1)S(1)}, u32[]{:S(2)}, u32[]{:S(2)}) collective-permute-start(bf16[64,2048]{1,0:T(8,128)(2,1)S(1)} %shard_map.103.refs_5_), channel_id=1, source_target_pairs={{0,16},{4,12},{8,24},{12,4},{16,0},{20,28},{24,8},{28,20},{1,17},{... | collective-permute-start | bytes 786440 | tf_op jit(solution)/shard_map/ppermute | solution.py:88
  80.6 17.0 %collective-permute-start.20 = (bf16[128,2048]{1,0:T(8,128)(2,1)S(1)}, bf16[128,2048]{1,0:T(8,128)(2,1)S(1)}, u32[]{:S(2)}, u32[]{:S(2)}) collective-permute-start(bf16[128,2048]{1,0:T(8,128)(2,1)S(1)} %get-tuple-element.35.refs_9_), channel_id=1, source_target_pairs={{0,8},{4,20},{8,0},{12,28},{16,24},{20,4},{24,16},{28,12},{1,9},{5... | collective-permute-start | bytes 1572872 | tf_op jit(solution)/shard_map/ppermute | solution.py:88
  94.2 20.5 %collective-permute-start.25 = (bf16[64,4096]{1,0:T(8,128)(2,1)S(1)}, bf16[64,4096]{1,0:T(8,128)(2,1)S(1)}, u32[]{:S(2)}, u32[]{:S(2)}) collective-permute-start(bf16[64,4096]{1,0:T(8,128)(2,1)S(1)} %shard_map.106.refs_3_.refs_1_), channel_id=1, source_target_pairs={{0,16},{4,12},{8,24},{12,4},{16,0},{20,28},{24,8},{28,20},{1,17},{... | collective-permute-start | bytes 1572872 | tf_op jit(solution)/shard_map/ppermute | solution.py:88
  95.6 23.4 %collective-permute-start.22 = (bf16[64,4096]{1,0:T(8,128)(2,1)S(1)}, bf16[64,4096]{1,0:T(8,128)(2,1)S(1)}, u32[]{:S(2)}, u32[]{:S(2)}) collective-permute-start(bf16[64,4096]{1,0:T(8,128)(2,1)S(1)} %shard_map.102.refs_3_.refs_1_), channel_id=1, source_target_pairs={{0,8},{4,20},{8,0},{12,28},{16,24},{20,4},{24,16},{28,12},{1,9},{5... | collective-permute-start | bytes 1572872 | tf_op jit(solution)/shard_map/ppermute | solution.py:88
  95.6 23.4 %collective-permute-start.23 = (bf16[64,4096]{1,0:T(8,128)(2,1)S(1)}, bf16[64,4096]{1,0:T(8,128)(2,1)S(1)}, u32[]{:S(2)}, u32[]{:S(2)}) collective-permute-start(bf16[64,4096]{1,0:T(8,128)(2,1)S(1)} %collective-permute-done.18.refs_10_.refs_3_), channel_id=1, source_target_pairs={{0,8},{4,20},{8,0},{12,28},{16,24},{20,4},{24,16},{28,12},{1,9},{5... | collective-permute-start | bytes 1572872 | tf_op jit(solution)/shard_map/ppermute | solution.py:88
  97.6 1.5 collective-permute-start.19
  98.3 16.4 %collective-permute-start.24 = (bf16[64,2048]{1,0:T(8,128)(2,1)S(1)}, bf16[64,2048]{1,0:T(8,128)(2,1)S(1)}, u32[]{:S(2)}, u32[]{:S(2)}) collective-permute-start(bf16[64,2048]{1,0:T(8,128)(2,1)S(1)} %shard_map.107.refs_3_), channel_id=1, source_target_pairs={{0,16},{4,12},{8,24},{12,4},{16,0},{20,28},{24,8},{28,20},{1,17},{... | collective-permute-start | bytes 786440 | tf_op jit(solution)/shard_map/ppermute | solution.py:88
  115.5 14.9 %collective-permute-start.30 = (bf16[64,4096]{1,0:T(8,128)(2,1)S(1)}, bf16[64,4096]{1,0:T(8,128)(2,1)S(1)}, u32[]{:S(2)}, u32[]{:S(2)}) collective-permute-start(bf16[64,4096]{1,0:T(8,128)(2,1)S(1)} %shard_map.109.refs_9_.refs_1_), channel_id=1, source_target_pairs={{0,16},{4,12},{8,24},{12,4},{16,0},{20,28},{24,8},{28,20},{1,17},{... | collective-permute-start | bytes 1572872 | tf_op jit(solution)/shard_map/ppermute | solution.py:88
  117.0 14.6 %collective-permute-start.28 = (bf16[64,4096]{1,0:T(8,128)(2,1)S(1)}, bf16[64,4096]{1,0:T(8,128)(2,1)S(1)}, u32[]{:S(2)}, u32[]{:S(2)}) collective-permute-start(bf16[64,4096]{1,0:T(8,128)(2,1)S(1)} %shard_map.106.refs_3_.refs_1_), channel_id=1, source_target_pairs={{0,8},{4,20},{8,0},{12,28},{16,24},{20,4},{24,16},{28,12},{1,9},{5... | collective-permute-start | bytes 1572872 | tf_op jit(solution)/shard_map/ppermute | solution.py:88
  117.0 15.5 %collective-permute-start.29 = (bf16[64,4096]{1,0:T(8,128)(2,1)S(1)}, bf16[64,4096]{1,0:T(8,128)(2,1)S(1)}, u32[]{:S(2)}, u32[]{:S(2)}) collective-permute-start(bf16[64,4096]{1,0:T(8,128)(2,1)S(1)} %collective-permute-done.25.refs_9_.refs_3_), channel_id=1, source_target_pairs={{0,8},{4,20},{8,0},{12,28},{16,24},{20,4},{24,16},{28,12},{1,9},{5... | collective-permute-start | bytes 1572872 | tf_op jit(solution)/shard_map/ppermute | solution.py:88
  123.3 7.7 %collective-permute-start.26 = (bf16[1,8,32,512]{3,2,1,0:T(8,128)(2,1)S(1)}, bf16[1,8,32,512]{3,2,1,0:T(8,128)(2,1)S(1)}, u32[]{:S(2)}, u32[]{:S(2)}) collective-permute-start(bf16[1,8,32,512]{3,2,1,0:T(8,128)(2,1)S(1)} %get-tuple-element.40), channel_id=1, source_target_pairs={{0,4},{4,0},{8,12},{12,8},{16,20},{20,16},{24,28},{28,24},{1,5},{5... | collective-permute-start | bytes 786440 | tf_op jit(solution)/shard_map/ppermute | solution.py:83
  123.3 19.9 %collective-permute-start.33 = (bf16[64,4096]{1,0:T(8,128)(2,1)S(1)}, bf16[64,4096]{1,0:T(8,128)(2,1)S(1)}, u32[]{:S(2)}, u32[]{:S(2)}) collective-permute-start(bf16[64,4096]{1,0:T(8,128)(2,1)S(1)} %shard_map.109.refs_9_.refs_1_), channel_id=1, source_target_pairs={{0,8},{4,20},{8,0},{12,28},{16,24},{20,4},{24,16},{28,12},{1,9},{5... | collective-permute-start | bytes 1572872 | tf_op jit(solution)/shard_map/ppermute | solution.py:88
  130.5 13.2 %collective-permute-start.34 = (bf16[64,4096]{1,0:T(8,128)(2,1)S(1)}, bf16[64,4096]{1,0:T(8,128)(2,1)S(1)}, u32[]{:S(2)}, u32[]{:S(2)}) collective-permute-start(bf16[64,4096]{1,0:T(8,128)(2,1)S(1)} %collective-permute-done.30.refs_10_.refs_3_), channel_id=1, source_target_pairs={{0,8},{4,20},{8,0},{12,28},{16,24},{20,4},{24,16},{28,12},{1,9},{5... | collective-permute-start | bytes 1572872 | tf_op jit(solution)/shard_map/ppermute | solution.py:88
  131.5 10.1 %collective-permute-start.27 = (bf16[8,32,512]{2,1,0:T(8,128)(2,1)S(1)}, bf16[8,32,512]{2,1,0:T(8,128)(2,1)S(1)}, u32[]{:S(2)}, u32[]{:S(2)}) collective-permute-start(bf16[8,32,512]{2,1,0:T(8,128)(2,1)S(1)} %shard_map.111.refs_9_), channel_id=1, source_target_pairs={{0,2},{1,3},{2,0},{3,1},{4,6},{5,7},{6,4},{7,5},{8,10},{9,11},{10,... | collective-permute-start | bytes 786440 | tf_op jit(solution)/shard_map/ppermute | solution.py:83
  136.7 5.0 %collective-permute-start.31 = (bf16[1,8,32,512]{3,2,1,0:T(8,128)(2,1)S(1)}, bf16[1,8,32,512]{3,2,1,0:T(8,128)(2,1)S(1)}, u32[]{:S(2)}, u32[]{:S(2)}) collective-permute-start(bf16[1,8,32,512]{3,2,1,0:T(8,128)(2,1)S(1)} %get-tuple-element.42), channel_id=1, source_target_pairs={{0,4},{4,0},{8,12},{12,8},{16,20},{20,16},{24,28},{28,24},{1,5},{5... | collective-permute-start | bytes 786440 | tf_op jit(solution)/shard_map/ppermute | solution.py:83
  142.3 8.3 %collective-permute-start.32 = (bf16[8,32,512]{2,1,0:T(8,128)(2,1)S(1)}, bf16[8,32,512]{2,1,0:T(8,128)(2,1)S(1)}, u32[]{:S(2)}, u32[]{:S(2)}) collective-permute-start(bf16[8,32,512]{2,1,0:T(8,128)(2,1)S(1)} %shard_map.113.refs_9_), channel_id=1, source_target_pairs={{0,3},{1,2},{2,1},{3,0},{4,7},{5,6},{6,5},{7,4},{8,11},{9,10},{10,... | collective-permute-start | bytes 786440 | tf_op jit(solution)/shard_map/ppermute | solution.py:83
  147.9 24.7 %copy-start.7 = (bf16[32,128]{1,0:T(8,128)(2,1)S(1)}, bf16[32,128]{1,0:T(8,128)(2,1)}, u32[]{:S(2)}) copy-start(bf16[32,128]{1,0:T(8,128)(2,1)} %get-tuple-element.25) | copy-start | bytes 24580
  147.9 2.7 %collective-permute-start.35 = (bf16[1,8,32,512]{3,2,1,0:T(8,128)(2,1)S(1)}, bf16[1,8,32,512]{3,2,1,0:T(8,128)(2,1)S(1)}, u32[]{:S(2)}, u32[]{:S(2)}) collective-permute-start(bf16[1,8,32,512]{3,2,1,0:T(8,128)(2,1)S(1)} %get-tuple-element.44), channel_id=1, source_target_pairs={{0,4},{4,0},{8,12},{12,8},{16,20},{20,16},{24,28},{28,24},{1,5},{5... | collective-permute-start | bytes 786440 | tf_op jit(solution)/shard_map/ppermute | solution.py:83
  151.2 11.9 %collective-permute-start.36 = (bf16[8,32,512]{2,1,0:T(8,128)(2,1)S(1)}, bf16[8,32,512]{2,1,0:T(8,128)(2,1)S(1)}, u32[]{:S(2)}, u32[]{:S(2)}) collective-permute-start(bf16[8,32,512]{2,1,0:T(8,128)(2,1)S(1)} %shard_map.115), channel_id=1, source_target_pairs={{0,1},{1,0},{2,3},{3,2},{4,5},{5,4},{6,7},{7,6},{8,9},{9,8},{10,11... | collective-permute-start | bytes 786440 | tf_op jit(solution)/shard_map/ppermute | solution.py:83

commit v6 on v5

--- a/solution.py
+++ b/solution.py
@@ -9,8 +9,8 @@
 VMEM_LIMIT = 24 * 1024 * 1024
 PACK_LIMIT = 60 * 1024 * 1024
 CHUNKS = (((0,), 0, 32), ((2,), 0, 32), ((3,), 0, 32), ((1,), 0, 32))
-SUM_STEPS = 4
-ORDER = (0, 1, -1, 0, 1, 2, 0, 2, 0, 1, 3, 1, 2, 3, 1, 0, 2, 3, 0, 2, 3, 0, 1, 1, 3, 2, 1, 2, 3, 2, 3, 3)
+SUM_STEPS = 2
+ORDER = (0, 1, -1, 0, 1, 2, 0, 2, 0, 1, 3, 1, 2, 3, 1, 0, 2, 3, 0, 2, 3, 1, 0, 1, 3, 2, 1, 2, 3, 2, 3, 3)
 
 
 def swiglu_grads(upstream, gate_pre, up_pre):

time: 175 us -> 174 us (level)
  waiting for transfers between devices: 64.9 us -> 72.3 us
  starting transfers between devices: 33.9 us -> 29.1 us
  Pallas kernels: 48.1 us -> 44.7 us
    ppermute x20, waiting for transfers between devices: 43.8 us -> 49.5 us  [exchange(): lax.ppermute(values, 'dp', [(i, i ^ (2 if (i + turn) % 2 == 0 else 4)) fo...]
    ppermute x20, starting transfers between devices: 18.1 us -> 14.2 us  [exchange(): lax.ppermute(values, 'dp', [(i, i ^ (2 if (i + turn) % 2 == 0 else 4)) fo...]
    pallas_call x25, Pallas kernels: 48.1 us -> 44.7 us  [call(): pl.pallas_call(ordered, out_shape=out_shape, cost_estimate=pl.CostEstimat...]
  transfers between devices with their start and end apart: 37 -> 37, of which waited for: 18 -> 18; matrix products, arithmetic and copies ran while one was open for 0% -> 0% of each run, Pallas kernels for 26% -> 24%
where the time goes in v6:
time: 174 us; the launch traced here: 173 us
  waiting for transfers between devices  72.3 us (42%)
  Pallas kernels  44.7 us (26%)
  starting transfers between devices  29.1 us (17%)
  blocking collectives  21.2 us (12%)
  local copies, waits for them, and re-layouts  4.19 us (2%)
    ppermute x20, waiting for transfers between devices, exchange(): lax.ppermute(values, 'dp', [(i, i ^ (2 if (i + turn) % 2 == 0 else 4)) fo...  49.5 us
    pallas_call x25, Pallas kernels, call(): pl.pallas_call(ordered, out_shape=out_shape, cost_estimate=pl.CostEstimat...  44.7 us
    ppermute x17, waiting for transfers between devices, swap(): return lax.ppermute(values, axis, [(i, i ^ offset) for i in range(size)])  22.7 us
    ppermute x17, starting transfers between devices, swap(): return lax.ppermute(values, axis, [(i, i ^ offset) for i in range(size)])  14.9 us
    ppermute x20, starting transfers between devices, exchange(): lax.ppermute(values, 'dp', [(i, i ^ (2 if (i + turn) % 2 == 0 else 4)) fo...  14.2 us
    all_to_all x1, blocking collectives, per_device(): rows = lax.all_to_all(rows, 'dp', split_axis=0, concat_axis=0, tiled=True)  11.8 us
    all_to_all x1, blocking collectives, per_device(): summed = lax.all_to_all(summed, 'dp', split_axis=0, concat_axis=1)  9.45 us
    unnamed x17, local copies, waits for them, and re-layouts  4.11 us
  transfers between devices with their start and end apart: 37, of which 18 were waited for; matrix products, arithmetic and copies ran while one was open for 0% of the time, Pallas kernels for 24%

profile of v6, /device:TPU:0, one launch (start us, length us, event | category | flops | bytes accessed | tf_op | source)
XLA Modules:
  0.0 173.3 jit_solution(17369101518740141549)
XLA Ops:
  0.5 2.4 %shard_map.91 = (bf16[8,32,512]{2,1,0:T(8,128)(2,1)}, bf16[32,128]{1,0:T(8,128)(2,1)}) custom-call(s32[1]{0:T(128)} %constant.23.clone.1.refs_0_, bf16[128,4096]{1,0:T(8,128)(2,1)} %refs_1_.2, s32[2,128]{1,0:T(2,128)} %bitcast.29, f32[2,128]{1,0:T(2,128)} %bitcast.30, s32[1,8]{1,0:T(1,128)} %refs_4_.6), custom_call_target="tpu_custom_call" | custom-call | flops 33554432 | bytes 1310720 | tf_op jit(solution)/shard_map/pallas_call | solution.py:113
  2.8 11.8 %all_to_all.20.refs_1_.refs_6_ = bf16[8,32,512]{2,1,0:T(8,128)(2,1)S(1)} all-to-all(bf16[8,32,512]{2,1,0:T(8,128)(2,1)} %get-tuple-element.26.refs_5_), channel_id=1, replica_groups=mesh['dp'=8,'et'=4] {'dp'}, dimensions={0} | all-to-all | bytes 524288 | tf_op jit(solution)/shard_map/all_to_all | solution.py:476
  14.6 2.6 %collective-permute-start.3 = (bf16[8,32,512]{2,1,0:T(8,128)(2,1)S(1)}, bf16[8,32,512]{2,1,0:T(8,128)(2,1)S(1)}, u32[]{:S(2)}, u32[]{:S(2)}) collective-permute-start(bf16[8,32,512]{2,1,0:T(8,128)(2,1)S(1)} %all_to_all.20.refs_1_.refs_6_), channel_id=1, source_target_pairs={{0,2},{1,3},{2,0},{3,1},{4,6},{5,7},{6,4},{7,5},{8,10},{9,11},{10,... | collective-permute-start | bytes 786440 | tf_op jit(solution)/shard_map/ppermute | solution.py:83
  17.3 2.3 %copy-done.2 = bf16[4096,512]{1,0:T(8,128)(2,1)S(1)} copy-done((bf16[4096,512]{1,0:T(8,128)(2,1)S(1)}, bf16[4096,512]{1,0:T(8,128)(2,1)}, u32[]{:S(2)}) %copy-start.2) | copy-done | bytes 4194328
  19.7 1.7 copy-done.6
  21.4 3.5 %shard_map.92 = (bf16[128,2048]{1,0:T(8,128)(2,1)S(1)}, bf16[128,2048]{1,0:T(8,128)(2,1)S(1)}) custom-call(s32[10]{0:T(128)S(1)} %stack.43.refs_0_, bf16[8,32,512]{2,1,0:T(8,128)(2,1)S(1)} %all_to_all.20.refs_1_.refs_6_, bf16[8,32,512]{2,1,0:T(8,128)(2,1)S(1)} %collective-permute-done.refs_2_, bf16[4096,512]{1,0:T(8,128)(2,1)S(1)} %copy-done.2, ...), custom_call_target="tpu_custom_call" | custom-call | flops 1073741824 | bytes 5767168 | tf_op jit(solution)/shard_map/pallas_call | solution.py:113
  24.9 5.0 %collective-permute-done.3.refs_1_ = bf16[8,32,512]{2,1,0:T(8,128)(2,1)S(1)} collective-permute-done((bf16[8,32,512]{2,1,0:T(8,128)(2,1)S(1)}, bf16[8,32,512]{2,1,0:T(8,128)(2,1)S(1)}, u32[]{:S(2)}, u32[]{:S(2)}) %collective-permute-start.3) | collective-permute-done | bytes 262176 | tf_op jit(solution)/shard_map/ppermute | solution.py:83
  30.4 1.8 %shard_map.94 = (bf16[2,512,2048]{2,1,0:T(8,128)(2,1)S(1)}, bf16[2,128,2048]{2,1,0:T(8,128)(2,1)S(1)}) custom-call(s32[10]{0:T(128)S(1)} %stack.43.refs_0_, bf16[512,4096]{1,0:T(8,128)(2,1)S(1)} %copy-done, bf16[512,4096]{1,0:T(8,128)(2,1)S(1)} %copy-done.1, bf16[1,128,4096]{2,1,0:T(8,128)(2,1)S(1)} %copy-done.4, bf16[1,128,4096]{2,1,0:T(8,128)(2,1)S(1)} %copy-done.5, ...), custom_call_target="tpu_custom_call" | custom-call | bytes 10485760 | tf_op jit(solution)/shard_map/pallas_call | solution.py:113
  32.9 0.6 collective-permute-start.2
  33.4 3.5 %collective-permute-start.6 = (bf16[8,32,512]{2,1,0:T(8,128)(2,1)S(1)}, bf16[8,32,512]{2,1,0:T(8,128)(2,1)S(1)}, u32[]{:S(2)}, u32[]{:S(2)}) collective-permute-start(bf16[8,32,512]{2,1,0:T(8,128)(2,1)S(1)} %all_to_all.20.refs_1_.refs_6_), channel_id=1, source_target_pairs={{0,3},{1,2},{2,1},{3,0},{4,7},{5,6},{6,5},{7,4},{8,11},{9,10},{10,... | collective-permute-start | bytes 786440 | tf_op jit(solution)/shard_map/ppermute | solution.py:83
  36.9 5.1 %collective-permute-done.2.refs_2_ = bf16[128,2048]{1,0:T(8,128)(2,1)S(1)} collective-permute-done((bf16[128,2048]{1,0:T(8,128)(2,1)S(1)}, bf16[128,2048]{1,0:T(8,128)(2,1)S(1)}, u32[]{:S(2)}, u32[]{:S(2)}) %collective-permute-start.2) | collective-permute-done | bytes 524320 | tf_op jit(solution)/shard_map/ppermute | solution.py:88
  42.0 0.6 shard_map.95.refs_5_
  42.6 0.6 collective-permute-start.4
  43.3 3.4 %shard_map.96 = (bf16[128,2048]{1,0:T(8,128)(2,1)S(1)}, bf16[128,2048]{1,0:T(8,128)(2,1)S(1)}) custom-call(s32[10]{0:T(128)S(1)} %stack.43.refs_0_, bf16[8,32,512]{2,1,0:T(8,128)(2,1)S(1)} %shard_map.93.refs_5_.refs_1_, bf16[8,32,512]{2,1,0:T(8,128)(2,1)S(1)} %collective-permute-done.7.refs_2_, bf16[4096,512]{1,0:T(8,128)(2,1)S(1)} %copy-done.3, ...), custom_call_target="tpu_custom_call" | custom-call | flops 1073741824 | bytes 5767168 | tf_op jit(solution)/shard_map/pallas_call | solution.py:113
  46.7 0.6 collective-permute-start.13
  47.3 0.6 shard_map.97.refs_8_.refs_1_
  47.9 1.9 %collective-permute-done.4.refs_3_ = bf16[64,2048]{1,0:T(8,128)(2,1)S(1)} collective-permute-done((bf16[64,2048]{1,0:T(8,128)(2,1)S(1)}, bf16[64,2048]{1,0:T(8,128)(2,1)S(1)}, u32[]{:S(2)}, u32[]{:S(2)}) %collective-permute-start.4) | collective-permute-done | bytes 262176 | tf_op jit(solution)/shard_map/ppermute | solution.py:88
  49.8 0.9 shard_map.98.refs_5_.refs_1_
  50.7 0.6 collective-permute-start.9
  51.3 1.5 collective-permute-done.14.refs_2_
  52.9 3.4 %shard_map.99 = (bf16[128,2048]{1,0:T(8,128)(2,1)S(1)}, bf16[128,2048]{1,0:T(8,128)(2,1)S(1)}) custom-call(s32[10]{0:T(128)S(1)} %stack.43.refs_0_, bf16[8,32,512]{2,1,0:T(8,128)(2,1)S(1)} %shard_map.97.refs_8_.refs_1_, bf16[8,32,512]{2,1,0:T(8,128)(2,1)S(1)} %collective-permute-done.14.refs_2_, bf16[4096,512]{1,0:T(8,128)(2,1)S(1)} %copy-done.3, ...), custom_call_target="tpu_custom_call" | custom-call | flops 1073741824 | bytes 5767168 | tf_op jit(solution)/shard_map/pallas_call | solution.py:113
  56.8 0.7 collective-permute-start.12
  57.5 3.4 %collective-permute-done.13.refs_2_ = bf16[128,2048]{1,0:T(8,128)(2,1)S(1)} collective-permute-done((bf16[128,2048]{1,0:T(8,128)(2,1)S(1)}, bf16[128,2048]{1,0:T(8,128)(2,1)S(1)}, u32[]{:S(2)}, u32[]{:S(2)}) %collective-permute-start.13) | collective-permute-done | bytes 524320 | tf_op jit(solution)/shard_map/ppermute | solution.py:88
  60.9 0.6 collective-permute-done.9.refs_4_.refs_3_
  61.5 0.6 shard_map.100.refs_2_
  62.1 1.4 collective-permute-start.17
  63.6 2.3 %collective-permute-done.12.refs_1_ = bf16[8,32,512]{2,1,0:T(8,128)(2,1)S(1)} collective-permute-done((bf16[8,32,512]{2,1,0:T(8,128)(2,1)S(1)}, bf16[8,32,512]{2,1,0:T(8,128)(2,1)S(1)}, u32[]{:S(2)}, u32[]{:S(2)}) %collective-permute-start.12) | collective-permute-done | bytes 262176 | tf_op jit(solution)/shard_map/ppermute | solution.py:83
  65.9 0.6 shard_map.101.refs_8_.refs_1_
  66.4 5.0 %collective-permute-done.17.refs_3_ = bf16[64,2048]{1,0:T(8,128)(2,1)S(1)} collective-permute-done((bf16[64,2048]{1,0:T(8,128)(2,1)S(1)}, bf16[64,2048]{1,0:T(8,128)(2,1)S(1)}, u32[]{:S(2)}, u32[]{:S(2)}) %collective-permute-start.17) | collective-permute-done | bytes 262176 | tf_op jit(solution)/shard_map/ppermute | solution.py:88
  71.4 0.9 shard_map.102.refs_3_.refs_1_
  72.3 1.0 collective-permute-start.18
  73.4 0.6 shard_map.103.refs_5_
  74.0 0.9 collective-permute-done.15.refs_2_
  74.9 1.1 collective-permute-start.21
  76.0 3.4 %shard_map.104 = (bf16[128,2048]{1,0:T(8,128)(2,1)S(1)}, bf16[128,2048]{1,0:T(8,128)(2,1)S(1)}) custom-call(s32[10]{0:T(128)S(1)} %stack.43.refs_0_, bf16[8,32,512]{2,1,0:T(8,128)(2,1)S(1)} %shard_map.101.refs_8_.refs_1_, bf16[8,32,512]{2,1,0:T(8,128)(2,1)S(1)} %collective-permute-done.15.refs_2_, bf16[4096,512]{1,0:T(8,128)(2,1)S(1)} %copy-done.3, ...), custom_call_target="tpu_custom_call" | custom-call | flops 1073741824 | bytes 5767168 | tf_op jit(solution)/shard_map/pallas_call | solution.py:113
  79.6 7.8 %collective-permute-done.10.refs_4_ = bf16[64,4096]{1,0:T(8,128)(2,1)S(1)} collective-permute-done((bf16[64,4096]{1,0:T(8,128)(2,1)S(1)}, bf16[64,4096]{1,0:T(8,128)(2,1)S(1)}, u32[]{:S(2)}, u32[]{:S(2)}) %collective-permute-start.10) | collective-permute-done | bytes 524320 | tf_op jit(solution)/shard_map/ppermute | solution.py:88
  87.5 4.2 %shard_map.105 = (f32[1,8,32,512]{3,2,1,0:T(8,128)S(1)}, bf16[1,8,32,512]{3,2,1,0:T(8,128)(2,1)S(1)}) custom-call(s32[10]{0:T(128)S(1)} %stack.43.refs_0_, bf16[64,4096]{1,0:T(8,128)(2,1)S(1)} %shard_map.98.refs_5_.refs_1_, bf16[64,4096]{1,0:T(8,128)(2,1)S(1)} %collective-permute-done.8.refs_2_, bf16[64,4096]{1,0:T(8,128)(2,1)S(1)} %collective-permute-done.9.refs_4_.refs_3_, ...), custom_call_target="tpu_custom_call" | custom-call | flops 2147483648 | bytes 11272192 | tf_op jit(solution)/shard_map/pallas_call | solution.py:113
  91.7 1.2 collective-permute-done.21.refs_3_
  92.9 0.9 shard_map.106.refs_3_.refs_1_
  93.7 1.0 collective-permute-start.25
  94.8 2.0 %collective-permute-start.23 = (bf16[64,4096]{1,0:T(8,128)(2,1)S(1)}, bf16[64,4096]{1,0:T(8,128)(2,1)S(1)}, u32[]{:S(2)}, u32[]{:S(2)}) collective-permute-start(bf16[64,4096]{1,0:T(8,128)(2,1)S(1)} %collective-permute-done.18.refs_10_.refs_3_), channel_id=1, source_target_pairs={{0,8},{4,20},{8,0},{12,28},{16,24},{20,4},{24,16},{28,12},{1,9},{5... | collective-permute-start | bytes 1572872 | tf_op jit(solution)/shard_map/ppermute | solution.py:88
  96.8 0.6 shard_map.107.refs_3_
  97.4 1.1 collective-permute-start.24
  98.5 0.6 shard_map.108.refs_8_.refs_4_
  99.1 15.1 %collective-permute-done.24.refs_3_ = bf16[64,2048]{1,0:T(8,128)(2,1)S(1)} collective-permute-done((bf16[64,2048]{1,0:T(8,128)(2,1)S(1)}, bf16[64,2048]{1,0:T(8,128)(2,1)S(1)}, u32[]{:S(2)}, u32[]{:S(2)}) %collective-permute-start.24) | collective-permute-done | bytes 262176 | tf_op jit(solution)/shard_map/ppermute | solution.py:88
  114.3 0.9 shard_map.109.refs_9_.refs_1_
  115.2 1.0 collective-permute-start.30
  116.2 2.0 %collective-permute-start.29 = (bf16[64,4096]{1,0:T(8,128)(2,1)S(1)}, bf16[64,4096]{1,0:T(8,128)(2,1)S(1)}, u32[]{:S(2)}, u32[]{:S(2)}) collective-permute-start(bf16[64,4096]{1,0:T(8,128)(2,1)S(1)} %collective-permute-done.25.refs_9_.refs_3_), channel_id=1, source_target_pairs={{0,8},{4,20},{8,0},{12,28},{16,24},{20,4},{24,16},{28,12},{1,9},{5... | collective-permute-start | bytes 1572872 | tf_op jit(solution)/shard_map/ppermute | solution.py:88
  118.2 4.2 %shard_map.110 = (f32[1,8,32,512]{3,2,1,0:T(8,128)S(1)}, bf16[1,8,32,512]{3,2,1,0:T(8,128)(2,1)S(1)}) custom-call(s32[10]{0:T(128)S(1)} %stack.43.refs_0_, bf16[64,4096]{1,0:T(8,128)(2,1)S(1)} %shard_map.102.refs_3_.refs_1_, bf16[64,4096]{1,0:T(8,128)(2,1)S(1)} %collective-permute-done.22.refs_2_, ...), custom_call_target="tpu_custom_call" | custom-call | flops 2147483648 | bytes 11272192 | tf_op jit(solution)/shard_map/pallas_call | solution.py:113
  122.6 7.5 %collective-permute-done.30.refs_10_.refs_3_ = bf16[64,4096]{1,0:T(8,128)(2,1)S(1)} collective-permute-done((bf16[64,4096]{1,0:T(8,128)(2,1)S(1)}, bf16[64,4096]{1,0:T(8,128)(2,1)S(1)}, u32[]{:S(2)}, u32[]{:S(2)}) %collective-permute-start.30) | collective-permute-done | bytes 524320 | tf_op jit(solution)/shard_map/ppermute | solution.py:88
  130.2 0.6 shard_map.111.refs_9_
  130.9 1.1 collective-permute-done.29.refs_4_
  132.0 4.2 %shard_map.112 = (f32[1,8,32,512]{3,2,1,0:T(8,128)S(1)}, bf16[1,8,32,512]{3,2,1,0:T(8,128)(2,1)S(1)}) custom-call(s32[10]{0:T(128)S(1)} %stack.43.refs_0_, bf16[64,4096]{1,0:T(8,128)(2,1)S(1)} %shard_map.106.refs_3_.refs_1_, bf16[64,4096]{1,0:T(8,128)(2,1)S(1)} %collective-permute-done.28.refs_2_, ...), custom_call_target="tpu_custom_call" | custom-call | flops 2147483648 | bytes 11272192 | tf_op jit(solution)/shard_map/pallas_call | solution.py:113
  136.7 4.3 %collective-permute-done.27.refs_4_ = bf16[8,32,512]{2,1,0:T(8,128)(2,1)S(1)} collective-permute-done((bf16[8,32,512]{2,1,0:T(8,128)(2,1)S(1)}, bf16[8,32,512]{2,1,0:T(8,128)(2,1)S(1)}, u32[]{:S(2)}, u32[]{:S(2)}) %collective-permute-start.27) | collective-permute-done | bytes 262176 | tf_op jit(solution)/shard_map/ppermute | solution.py:83
  141.0 0.6 shard_map.113.refs_9_
  141.6 1.0 collective-permute-start.32
  142.5 0.7 collective-permute-done.34.refs_4_
  143.2 4.2 %shard_map.114 = (f32[1,8,32,512]{3,2,1,0:T(8,128)S(1)}, bf16[1,8,32,512]{3,2,1,0:T(8,128)(2,1)S(1)}) custom-call(s32[10]{0:T(128)S(1)} %stack.43.refs_0_, bf16[64,4096]{1,0:T(8,128)(2,1)S(1)} %shard_map.109.refs_9_.refs_1_, bf16[64,4096]{1,0:T(8,128)(2,1)S(1)} %collective-permute-done.33.refs_2_, ...), custom_call_target="tpu_custom_call" | custom-call | flops 2147483648 | bytes 11272192 | tf_op jit(solution)/shard_map/pallas_call | solution.py:113
  147.7 2.2 %collective-permute-done.32.refs_4_ = bf16[8,32,512]{2,1,0:T(8,128)(2,1)S(1)} collective-permute-done((bf16[8,32,512]{2,1,0:T(8,128)(2,1)S(1)}, bf16[8,32,512]{2,1,0:T(8,128)(2,1)S(1)}, u32[]{:S(2)}, u32[]{:S(2)}) %collective-permute-start.32) | collective-permute-done | bytes 262176 | tf_op jit(solution)/shard_map/ppermute | solution.py:83
  149.9 0.6 shard_map.115
  150.5 5.3 %collective-permute-start.36 = (bf16[8,32,512]{2,1,0:T(8,128)(2,1)S(1)}, bf16[8,32,512]{2,1,0:T(8,128)(2,1)S(1)}, u32[]{:S(2)}, u32[]{:S(2)}) collective-permute-start(bf16[8,32,512]{2,1,0:T(8,128)(2,1)S(1)} %shard_map.115), channel_id=1, source_target_pairs={{0,1},{1,0},{2,3},{3,2},{4,5},{5,4},{6,7},{7,6},{8,9},{9,8},{10,11... | collective-permute-start | bytes 786440 | tf_op jit(solution)/shard_map/ppermute | solution.py:83
  155.8 6.5 %collective-permute-done.36 = bf16[8,32,512]{2,1,0:T(8,128)(2,1)S(1)} collective-permute-done((bf16[8,32,512]{2,1,0:T(8,128)(2,1)S(1)}, bf16[8,32,512]{2,1,0:T(8,128)(2,1)S(1)}, u32[]{:S(2)}, u32[]{:S(2)}) %collective-permute-start.36) | collective-permute-done | bytes 262176 | tf_op jit(solution)/shard_map/ppermute | solution.py:83
  162.4 9.4 %all_to_all.21 = bf16[8,32,1,512]{3,1,2,0:T(8,128)(2,1)S(1)} all-to-all(bf16[8,32,1,512]{3,1,2,0:T(8,128)(2,1)S(1)} %fusion), channel_id=1, replica_groups=mesh['dp'=8,'et'=4] {'dp'}, dimensions={0} | all-to-all | bytes 524288 | tf_op jit(solution)/shard_map/all_to_all | solution.py:497
  171.9 1.4 convolution_convert_fusion
  (57 shorter events, 3.9 us)
Async XLA Ops:
  0.0 17.3 %collective-permute-start.1 = (bf16[4096,512]{1,0:T(8,128)(2,1)}, bf16[4096,512]{1,0:T(8,128)(2,1)}, u32[]{:S(2)}, u32[]{:S(2)}) collective-permute-start(bf16[4096,512]{1,0:T(8,128)(2,1)} %refs_3_.9), channel_id=1, source_target_pairs={{0,4},{4,0},{8,12},{12,8},{16,20},{20,16},{24,28},{28,24},{1,5},{5... | collective-permute-start | bytes 12582920 | tf_op jit(solution)/shard_map/ppermute | solution.py:83
  14.6 2.7 %collective-permute-start = (bf16[8,32,512]{2,1,0:T(8,128)(2,1)S(1)}, bf16[8,32,512]{2,1,0:T(8,128)(2,1)S(1)}, u32[]{:S(2)}, u32[]{:S(2)}) collective-permute-start(bf16[8,32,512]{2,1,0:T(8,128)(2,1)S(1)} %all_to_all.20.refs_1_.refs_6_), channel_id=1, source_target_pairs={{0,4},{4,0},{8,12},{12,8},{16,20},{20,16},{24,28},{28,24},{1,5},{5... | collective-permute-start | bytes 786440 | tf_op jit(solution)/shard_map/ppermute | solution.py:83
  14.6 15.2 %collective-permute-start.3 = (bf16[8,32,512]{2,1,0:T(8,128)(2,1)S(1)}, bf16[8,32,512]{2,1,0:T(8,128)(2,1)S(1)}, u32[]{:S(2)}, u32[]{:S(2)}) collective-permute-start(bf16[8,32,512]{2,1,0:T(8,128)(2,1)S(1)} %all_to_all.20.refs_1_.refs_6_), channel_id=1, source_target_pairs={{0,2},{1,3},{2,0},{3,1},{4,6},{5,7},{6,4},{7,5},{8,10},{9,11},{10,... | collective-permute-start | bytes 786440 | tf_op jit(solution)/shard_map/ppermute | solution.py:83
  17.3 13.1 %copy-start = (bf16[512,4096]{1,0:T(8,128)(2,1)S(1)}, bf16[512,4096]{1,0:T(8,128)(2,1)}, u32[]{:S(2)}) copy-start(bf16[512,4096]{1,0:T(8,128)(2,1)} %refs_5_.15) | copy-start | bytes 12582916
  17.3 13.1 %copy-start.1 = (bf16[512,4096]{1,0:T(8,128)(2,1)S(1)}, bf16[512,4096]{1,0:T(8,128)(2,1)}, u32[]{:S(2)}) copy-start(bf16[512,4096]{1,0:T(8,128)(2,1)} %refs_6_.7) | copy-start | bytes 12582916
  17.3 2.3 %copy-start.2 = (bf16[4096,512]{1,0:T(8,128)(2,1)S(1)}, bf16[4096,512]{1,0:T(8,128)(2,1)}, u32[]{:S(2)}) copy-start(bf16[4096,512]{1,0:T(8,128)(2,1)} %refs_3_.9) | copy-start | bytes 12582916
  19.6 1.7 copy-start.6
  21.4 9.0 %copy-start.4 = (bf16[1,128,4096]{2,1,0:T(8,128)(2,1)S(1)}, bf16[1,128,4096]{2,1,0:T(8,128)(2,1)}, u32[]{:S(2)}) copy-start(bf16[1,128,4096]{2,1,0:T(8,128)(2,1)} %refs_4_.11) | copy-start | bytes 3145732
  21.4 9.0 %copy-start.5 = (bf16[1,128,4096]{2,1,0:T(8,128)(2,1)S(1)}, bf16[1,128,4096]{2,1,0:T(8,128)(2,1)}, u32[]{:S(2)}) copy-start(bf16[1,128,4096]{2,1,0:T(8,128)(2,1)} %refs_5_.12) | copy-start | bytes 3145732
  32.3 11.0 %copy-start.3 = (bf16[4096,512]{1,0:T(8,128)(2,1)S(1)}, bf16[4096,512]{1,0:T(8,128)(2,1)}, u32[]{:S(2)}) copy-start(bf16[4096,512]{1,0:T(8,128)(2,1)} %refs_3_.9) | copy-start | bytes 12582916
  32.3 55.2 %collective-permute-start.11 = (bf16[2,512,2048]{2,1,0:T(8,128)(2,1)S(1)}, bf16[2,512,2048]{2,1,0:T(8,128)(2,1)S(1)}, u32[]{:S(2)}, u32[]{:S(2)}) collective-permute-start(bf16[2,512,2048]{2,1,0:T(8,128)(2,1)S(1)} %get-tuple-element.29.refs_3_), channel_id=1, source_target_pairs={{0,4},{4,0},{8,12},{12,8},{16,20},{20,16},{24,28},{28,24},{1,5},{5... | collective-permute-start | bytes 12582920 | tf_op jit(solution)/shard_map/ppermute | solution.py:83
  32.4 17.4 %collective-permute-start.5 = (bf16[2,128,2048]{2,1,0:T(8,128)(2,1)S(1)}, bf16[2,128,2048]{2,1,0:T(8,128)(2,1)S(1)}, u32[]{:S(2)}, u32[]{:S(2)}) collective-permute-start(bf16[2,128,2048]{2,1,0:T(8,128)(2,1)S(1)} %get-tuple-element.30), channel_id=1, source_target_pairs={{0,4},{4,0},{8,12},{12,8},{16,20},{20,16},{24,28},{28,24},{1,5},{5... | collective-permute-start | bytes 3145736 | tf_op jit(solution)/shard_map/ppermute | solution.py:83
  32.9 9.2 %collective-permute-start.2 = (bf16[128,2048]{1,0:T(8,128)(2,1)S(1)}, bf16[128,2048]{1,0:T(8,128)(2,1)S(1)}, u32[]{:S(2)}, u32[]{:S(2)}) collective-permute-start(bf16[128,2048]{1,0:T(8,128)(2,1)S(1)} %get-tuple-element.28.refs_2_), channel_id=1, source_target_pairs={{0,8},{4,20},{8,0},{12,28},{16,24},{20,4},{24,16},{28,12},{1,9},{5... | collective-permute-start | bytes 1572872 | tf_op jit(solution)/shard_map/ppermute | solution.py:88
  33.4 9.9 %collective-permute-start.7 = (bf16[8,32,512]{2,1,0:T(8,128)(2,1)S(1)}, bf16[8,32,512]{2,1,0:T(8,128)(2,1)S(1)}, u32[]{:S(2)}, u32[]{:S(2)}) collective-permute-start(bf16[8,32,512]{2,1,0:T(8,128)(2,1)S(1)} %shard_map.93.refs_5_.refs_1_), channel_id=1, source_target_pairs={{0,4},{4,0},{8,12},{12,8},{16,20},{20,16},{24,28},{28,24},{1,5},{5... | collective-permute-start | bytes 786440 | tf_op jit(solution)/shard_map/ppermute | solution.py:83
  33.4 13.9 %collective-permute-start.6 = (bf16[8,32,512]{2,1,0:T(8,128)(2,1)S(1)}, bf16[8,32,512]{2,1,0:T(8,128)(2,1)S(1)}, u32[]{:S(2)}, u32[]{:S(2)}) collective-permute-start(bf16[8,32,512]{2,1,0:T(8,128)(2,1)S(1)} %all_to_all.20.refs_1_.refs_6_), channel_id=1, source_target_pairs={{0,3},{1,2},{2,1},{3,0},{4,7},{5,6},{6,5},{7,4},{8,11},{9,10},{10,... | collective-permute-start | bytes 786440 | tf_op jit(solution)/shard_map/ppermute | solution.py:83
  42.6 7.2 %collective-permute-start.4 = (bf16[64,2048]{1,0:T(8,128)(2,1)S(1)}, bf16[64,2048]{1,0:T(8,128)(2,1)S(1)}, u32[]{:S(2)}, u32[]{:S(2)}) collective-permute-start(bf16[64,2048]{1,0:T(8,128)(2,1)S(1)} %shard_map.95.refs_5_), channel_id=1, source_target_pairs={{0,16},{4,12},{8,24},{12,4},{16,0},{20,28},{24,8},{28,20},{1,17},{... | collective-permute-start | bytes 786440 | tf_op jit(solution)/shard_map/ppermute | solution.py:88
  46.7 14.2 %collective-permute-start.13 = (bf16[128,2048]{1,0:T(8,128)(2,1)S(1)}, bf16[128,2048]{1,0:T(8,128)(2,1)S(1)}, u32[]{:S(2)}, u32[]{:S(2)}) collective-permute-start(bf16[128,2048]{1,0:T(8,128)(2,1)S(1)} %get-tuple-element.31.refs_2_), channel_id=1, source_target_pairs={{0,8},{4,20},{8,0},{12,28},{16,24},{20,4},{24,16},{28,12},{1,9},{5... | collective-permute-start | bytes 1572872 | tf_op jit(solution)/shard_map/ppermute | solution.py:88
  50.7 10.8 %collective-permute-start.9 = (bf16[64,4096]{1,0:T(8,128)(2,1)S(1)}, bf16[64,4096]{1,0:T(8,128)(2,1)S(1)}, u32[]{:S(2)}, u32[]{:S(2)}) collective-permute-start(bf16[64,4096]{1,0:T(8,128)(2,1)S(1)} %shard_map.98.refs_5_.refs_1_), channel_id=1, source_target_pairs={{0,16},{4,12},{8,24},{12,4},{16,0},{20,28},{24,8},{28,20},{1,17},{... | collective-permute-start | bytes 1572872 | tf_op jit(solution)/shard_map/ppermute | solution.py:88
  51.3 1.5 collective-permute-start.14
  56.3 17.1 %collective-permute-start.16 = (bf16[128,2048]{1,0:T(8,128)(2,1)S(1)}, bf16[128,2048]{1,0:T(8,128)(2,1)S(1)}, u32[]{:S(2)}, u32[]{:S(2)}) collective-permute-start(bf16[128,2048]{1,0:T(8,128)(2,1)S(1)} %get-tuple-element.33.refs_3_), channel_id=1, source_target_pairs={{0,8},{4,20},{8,0},{12,28},{16,24},{20,4},{24,16},{28,12},{1,9},{5... | collective-permute-start | bytes 1572872 | tf_op jit(solution)/shard_map/ppermute | solution.py:88
  56.8 9.1 %collective-permute-start.12 = (bf16[8,32,512]{2,1,0:T(8,128)(2,1)S(1)}, bf16[8,32,512]{2,1,0:T(8,128)(2,1)S(1)}, u32[]{:S(2)}, u32[]{:S(2)}) collective-permute-start(bf16[8,32,512]{2,1,0:T(8,128)(2,1)S(1)} %all_to_all.20.refs_1_.refs_6_), channel_id=1, source_target_pairs={{0,1},{1,0},{2,3},{3,2},{4,5},{5,4},{6,7},{7,6},{8,9},{9,8},{10,11... | collective-permute-start | bytes 786440 | tf_op jit(solution)/shard_map/ppermute | solution.py:83
  62.1 9.3 %collective-permute-start.17 = (bf16[64,2048]{1,0:T(8,128)(2,1)S(1)}, bf16[64,2048]{1,0:T(8,128)(2,1)S(1)}, u32[]{:S(2)}, u32[]{:S(2)}) collective-permute-start(bf16[64,2048]{1,0:T(8,128)(2,1)S(1)} %shard_map.100.refs_2_), channel_id=1, source_target_pairs={{0,16},{4,12},{8,24},{12,4},{16,0},{20,28},{24,8},{28,20},{1,17},{... | collective-permute-start | bytes 786440 | tf_op jit(solution)/shard_map/ppermute | solution.py:88
  63.5 15.9 %collective-permute-start.8 = (bf16[64,4096]{1,0:T(8,128)(2,1)S(1)}, bf16[64,4096]{1,0:T(8,128)(2,1)S(1)}, u32[]{:S(2)}, u32[]{:S(2)}) collective-permute-start(bf16[64,4096]{1,0:T(8,128)(2,1)S(1)} %shard_map.98.refs_5_.refs_1_), channel_id=1, source_target_pairs={{0,8},{4,20},{8,0},{12,28},{16,24},{20,4},{24,16},{28,12},{1,9},{5... | collective-permute-start | bytes 1572872 | tf_op jit(solution)/shard_map/ppermute | solution.py:88
  65.9 21.6 %collective-permute-start.10 = (bf16[64,4096]{1,0:T(8,128)(2,1)S(1)}, bf16[64,4096]{1,0:T(8,128)(2,1)S(1)}, u32[]{:S(2)}, u32[]{:S(2)}) collective-permute-start(bf16[64,4096]{1,0:T(8,128)(2,1)S(1)} %collective-permute-done.9.refs_4_.refs_3_), channel_id=1, source_target_pairs={{0,8},{4,20},{8,0},{12,28},{16,24},{20,4},{24,16},{28,12},{1,9},{5... | collective-permute-start | bytes 1572872 | tf_op jit(solution)/shard_map/ppermute | solution.py:88
  72.3 15.2 %collective-permute-start.18 = (bf16[64,4096]{1,0:T(8,128)(2,1)S(1)}, bf16[64,4096]{1,0:T(8,128)(2,1)S(1)}, u32[]{:S(2)}, u32[]{:S(2)}) collective-permute-start(bf16[64,4096]{1,0:T(8,128)(2,1)S(1)} %shard_map.102.refs_3_.refs_1_), channel_id=1, source_target_pairs={{0,16},{4,12},{8,24},{12,4},{16,0},{20,28},{24,8},{28,20},{1,17},{... | collective-permute-start | bytes 1572872 | tf_op jit(solution)/shard_map/ppermute | solution.py:88
  73.3 1.5 collective-permute-start.15
  74.9 18.0 %collective-permute-start.21 = (bf16[64,2048]{1,0:T(8,128)(2,1)S(1)}, bf16[64,2048]{1,0:T(8,128)(2,1)S(1)}, u32[]{:S(2)}, u32[]{:S(2)}) collective-permute-start(bf16[64,2048]{1,0:T(8,128)(2,1)S(1)} %shard_map.103.refs_5_), channel_id=1, source_target_pairs={{0,16},{4,12},{8,24},{12,4},{16,0},{20,28},{24,8},{28,20},{1,17},{... | collective-permute-start | bytes 786440 | tf_op jit(solution)/shard_map/ppermute | solution.py:88
  79.4 17.4 %collective-permute-start.20 = (bf16[128,2048]{1,0:T(8,128)(2,1)S(1)}, bf16[128,2048]{1,0:T(8,128)(2,1)S(1)}, u32[]{:S(2)}, u32[]{:S(2)}) collective-permute-start(bf16[128,2048]{1,0:T(8,128)(2,1)S(1)} %get-tuple-element.35.refs_9_), channel_id=1, source_target_pairs={{0,8},{4,20},{8,0},{12,28},{16,24},{20,4},{24,16},{28,12},{1,9},{5... | collective-permute-start | bytes 1572872 | tf_op jit(solution)/shard_map/ppermute | solution.py:88
  93.7 20.5 %collective-permute-start.25 = (bf16[64,4096]{1,0:T(8,128)(2,1)S(1)}, bf16[64,4096]{1,0:T(8,128)(2,1)S(1)}, u32[]{:S(2)}, u32[]{:S(2)}) collective-permute-start(bf16[64,4096]{1,0:T(8,128)(2,1)S(1)} %shard_map.106.refs_3_.refs_1_), channel_id=1, source_target_pairs={{0,16},{4,12},{8,24},{12,4},{16,0},{20,28},{24,8},{28,20},{1,17},{... | collective-permute-start | bytes 1572872 | tf_op jit(solution)/shard_map/ppermute | solution.py:88
  94.8 23.4 %collective-permute-start.22 = (bf16[64,4096]{1,0:T(8,128)(2,1)S(1)}, bf16[64,4096]{1,0:T(8,128)(2,1)S(1)}, u32[]{:S(2)}, u32[]{:S(2)}) collective-permute-start(bf16[64,4096]{1,0:T(8,128)(2,1)S(1)} %shard_map.102.refs_3_.refs_1_), channel_id=1, source_target_pairs={{0,8},{4,20},{8,0},{12,28},{16,24},{20,4},{24,16},{28,12},{1,9},{5... | collective-permute-start | bytes 1572872 | tf_op jit(solution)/shard_map/ppermute | solution.py:88
  94.8 23.4 %collective-permute-start.23 = (bf16[64,4096]{1,0:T(8,128)(2,1)S(1)}, bf16[64,4096]{1,0:T(8,128)(2,1)S(1)}, u32[]{:S(2)}, u32[]{:S(2)}) collective-permute-start(bf16[64,4096]{1,0:T(8,128)(2,1)S(1)} %collective-permute-done.18.refs_10_.refs_3_), channel_id=1, source_target_pairs={{0,8},{4,20},{8,0},{12,28},{16,24},{20,4},{24,16},{28,12},{1,9},{5... | collective-permute-start | bytes 1572872 | tf_op jit(solution)/shard_map/ppermute | solution.py:88
  96.8 1.7 %collective-permute-start.19 = (bf16[1,8,32,512]{3,2,1,0:T(8,128)(2,1)S(1)}, bf16[1,8,32,512]{3,2,1,0:T(8,128)(2,1)S(1)}, u32[]{:S(2)}, u32[]{:S(2)}) collective-permute-start(bf16[1,8,32,512]{3,2,1,0:T(8,128)(2,1)S(1)} %get-tuple-element.37), channel_id=1, source_target_pairs={{0,4},{4,0},{8,12},{12,8},{16,20},{20,16},{24,28},{28,24},{1,5},{5... | collective-permute-start | bytes 786440 | tf_op jit(solution)/shard_map/ppermute | solution.py:83
  97.4 16.9 %collective-permute-start.24 = (bf16[64,2048]{1,0:T(8,128)(2,1)S(1)}, bf16[64,2048]{1,0:T(8,128)(2,1)S(1)}, u32[]{:S(2)}, u32[]{:S(2)}) collective-permute-start(bf16[64,2048]{1,0:T(8,128)(2,1)S(1)} %shard_map.107.refs_3_), channel_id=1, source_target_pairs={{0,16},{4,12},{8,24},{12,4},{16,0},{20,28},{24,8},{28,20},{1,17},{... | collective-permute-start | bytes 786440 | tf_op jit(solution)/shard_map/ppermute | solution.py:88
  115.2 14.9 %collective-permute-start.30 = (bf16[64,4096]{1,0:T(8,128)(2,1)S(1)}, bf16[64,4096]{1,0:T(8,128)(2,1)S(1)}, u32[]{:S(2)}, u32[]{:S(2)}) collective-permute-start(bf16[64,4096]{1,0:T(8,128)(2,1)S(1)} %shard_map.109.refs_9_.refs_1_), channel_id=1, source_target_pairs={{0,16},{4,12},{8,24},{12,4},{16,0},{20,28},{24,8},{28,20},{1,17},{... | collective-permute-start | bytes 1572872 | tf_op jit(solution)/shard_map/ppermute | solution.py:88
  116.1 14.7 %collective-permute-start.28 = (bf16[64,4096]{1,0:T(8,128)(2,1)S(1)}, bf16[64,4096]{1,0:T(8,128)(2,1)S(1)}, u32[]{:S(2)}, u32[]{:S(2)}) collective-permute-start(bf16[64,4096]{1,0:T(8,128)(2,1)S(1)} %shard_map.106.refs_3_.refs_1_), channel_id=1, source_target_pairs={{0,8},{4,20},{8,0},{12,28},{16,24},{20,4},{24,16},{28,12},{1,9},{5... | collective-permute-start | bytes 1572872 | tf_op jit(solution)/shard_map/ppermute | solution.py:88
  116.2 15.8 %collective-permute-start.29 = (bf16[64,4096]{1,0:T(8,128)(2,1)S(1)}, bf16[64,4096]{1,0:T(8,128)(2,1)S(1)}, u32[]{:S(2)}, u32[]{:S(2)}) collective-permute-start(bf16[64,4096]{1,0:T(8,128)(2,1)S(1)} %collective-permute-done.25.refs_9_.refs_3_), channel_id=1, source_target_pairs={{0,8},{4,20},{8,0},{12,28},{16,24},{20,4},{24,16},{28,12},{1,9},{5... | collective-permute-start | bytes 1572872 | tf_op jit(solution)/shard_map/ppermute | solution.py:88
  122.4 7.8 %collective-permute-start.26 = (bf16[1,8,32,512]{3,2,1,0:T(8,128)(2,1)S(1)}, bf16[1,8,32,512]{3,2,1,0:T(8,128)(2,1)S(1)}, u32[]{:S(2)}, u32[]{:S(2)}) collective-permute-start(bf16[1,8,32,512]{3,2,1,0:T(8,128)(2,1)S(1)} %get-tuple-element.40), channel_id=1, source_target_pairs={{0,4},{4,0},{8,12},{12,8},{16,20},{20,16},{24,28},{28,24},{1,5},{5... | collective-permute-start | bytes 786440 | tf_op jit(solution)/shard_map/ppermute | solution.py:83
  122.5 20.0 %collective-permute-start.33 = (bf16[64,4096]{1,0:T(8,128)(2,1)S(1)}, bf16[64,4096]{1,0:T(8,128)(2,1)S(1)}, u32[]{:S(2)}, u32[]{:S(2)}) collective-permute-start(bf16[64,4096]{1,0:T(8,128)(2,1)S(1)} %shard_map.109.refs_9_.refs_1_), channel_id=1, source_target_pairs={{0,8},{4,20},{8,0},{12,28},{16,24},{20,4},{24,16},{28,12},{1,9},{5... | collective-permute-start | bytes 1572872 | tf_op jit(solution)/shard_map/ppermute | solution.py:88
  130.1 13.1 %collective-permute-start.34 = (bf16[64,4096]{1,0:T(8,128)(2,1)S(1)}, bf16[64,4096]{1,0:T(8,128)(2,1)S(1)}, u32[]{:S(2)}, u32[]{:S(2)}) collective-permute-start(bf16[64,4096]{1,0:T(8,128)(2,1)S(1)} %collective-permute-done.30.refs_10_.refs_3_), channel_id=1, source_target_pairs={{0,8},{4,20},{8,0},{12,28},{16,24},{20,4},{24,16},{28,12},{1,9},{5... | collective-permute-start | bytes 1572872 | tf_op jit(solution)/shard_map/ppermute | solution.py:88
  130.8 10.1 %collective-permute-start.27 = (bf16[8,32,512]{2,1,0:T(8,128)(2,1)S(1)}, bf16[8,32,512]{2,1,0:T(8,128)(2,1)S(1)}, u32[]{:S(2)}, u32[]{:S(2)}) collective-permute-start(bf16[8,32,512]{2,1,0:T(8,128)(2,1)S(1)} %shard_map.111.refs_9_), channel_id=1, source_target_pairs={{0,2},{1,3},{2,0},{3,1},{4,6},{5,7},{6,4},{7,5},{8,10},{9,11},{10,... | collective-permute-start | bytes 786440 | tf_op jit(solution)/shard_map/ppermute | solution.py:83
  136.2 4.7 %collective-permute-start.31 = (bf16[1,8,32,512]{3,2,1,0:T(8,128)(2,1)S(1)}, bf16[1,8,32,512]{3,2,1,0:T(8,128)(2,1)S(1)}, u32[]{:S(2)}, u32[]{:S(2)}) collective-permute-start(bf16[1,8,32,512]{3,2,1,0:T(8,128)(2,1)S(1)} %get-tuple-element.42), channel_id=1, source_target_pairs={{0,4},{4,0},{8,12},{12,8},{16,20},{20,16},{24,28},{28,24},{1,5},{5... | collective-permute-start | bytes 786440 | tf_op jit(solution)/shard_map/ppermute | solution.py:83
  141.6 8.3 %collective-permute-start.32 = (bf16[8,32,512]{2,1,0:T(8,128)(2,1)S(1)}, bf16[8,32,512]{2,1,0:T(8,128)(2,1)S(1)}, u32[]{:S(2)}, u32[]{:S(2)}) collective-permute-start(bf16[8,32,512]{2,1,0:T(8,128)(2,1)S(1)} %shard_map.113.refs_9_), channel_id=1, source_target_pairs={{0,3},{1,2},{2,1},{3,0},{4,7},{5,6},{6,5},{7,4},{8,11},{9,10},{10,... | collective-permute-start | bytes 786440 | tf_op jit(solution)/shard_map/ppermute | solution.py:83
  147.4 24.4 %copy-start.7 = (bf16[32,128]{1,0:T(8,128)(2,1)S(1)}, bf16[32,128]{1,0:T(8,128)(2,1)}, u32[]{:S(2)}) copy-start(bf16[32,128]{1,0:T(8,128)(2,1)} %get-tuple-element.25) | copy-start | bytes 24580
  147.5 2.4 %collective-permute-start.35 = (bf16[1,8,32,512]{3,2,1,0:T(8,128)(2,1)S(1)}, bf16[1,8,32,512]{3,2,1,0:T(8,128)(2,1)S(1)}, u32[]{:S(2)}, u32[]{:S(2)}) collective-permute-start(bf16[1,8,32,512]{3,2,1,0:T(8,128)(2,1)S(1)} %get-tuple-element.44), channel_id=1, source_target_pairs={{0,4},{4,0},{8,12},{12,8},{16,20},{20,16},{24,28},{28,24},{1,5},{5... | collective-permute-start | bytes 786440 | tf_op jit(solution)/shard_map/ppermute | solution.py:83
  150.5 11.8 %collective-permute-start.36 = (bf16[8,32,512]{2,1,0:T(8,128)(2,1)S(1)}, bf16[8,32,512]{2,1,0:T(8,128)(2,1)S(1)}, u32[]{:S(2)}, u32[]{:S(2)}) collective-permute-start(bf16[8,32,512]{2,1,0:T(8,128)(2,1)S(1)} %shard_map.115), channel_id=1, source_target_pairs={{0,1},{1,0},{2,3},{3,2},{4,5},{5,4},{6,7},{7,6},{8,9},{9,8},{10,11... | collective-permute-start | bytes 786440 | tf_op jit(solution)/shard_map/ppermute | solution.py:83

commit v7 on v6

--- a/solution.py
+++ b/solution.py
@@ -442,9 +442,9 @@
     last = exchange(second_terms(steps, keep, got), 1)
     yield
     own = hidden_grads(steps, chunk, keep, got, last, saved)
-    from_second, from_first = exchange(own, 1), exchange(own, 0)
+    from_second = exchange(own, 1)
     yield
-    far = exchange(from_second, 0)
+    far, from_first = exchange(from_second, 0), exchange(own, 0)
     steps.waits = steps.waits + [from_second]
     yield
     own_terms, other_terms = input_terms(steps, chunk, [own, from_first, from_second, far], weights)

time: 174 us -> 174 us (level)
  no operation moved by 1% of the time
where the time goes in v7:
time: 174 us; the launch traced here: 173 us
  waiting for transfers between devices  72.3 us (42%)
  Pallas kernels  44.7 us (26%)
  starting transfers between devices  29.1 us (17%)
  blocking collectives  21.2 us (12%)
  local copies, waits for them, and re-layouts  4.19 us (2%)
    ppermute x20, waiting for transfers between devices, exchange(): lax.ppermute(values, 'dp', [(i, i ^ (2 if (i + turn) % 2 == 0 else 4)) fo...  49.5 us
    pallas_call x25, Pallas kernels, call(): pl.pallas_call(ordered, out_shape=out_shape, cost_estimate=pl.CostEstimat...  44.7 us
    ppermute x17, waiting for transfers between devices, swap(): return lax.ppermute(values, axis, [(i, i ^ offset) for i in range(size)])  22.7 us
    ppermute x17, starting transfers between devices, swap(): return lax.ppermute(values, axis, [(i, i ^ offset) for i in range(size)])  14.9 us
    ppermute x20, starting transfers between devices, exchange(): lax.ppermute(values, 'dp', [(i, i ^ (2 if (i + turn) % 2 == 0 else 4)) fo...  14.2 us
    all_to_all x1, blocking collectives, per_device(): rows = lax.all_to_all(rows, 'dp', split_axis=0, concat_axis=0, tiled=True)  11.8 us
    all_to_all x1, blocking collectives, per_device(): summed = lax.all_to_all(summed, 'dp', split_axis=0, concat_axis=1)  9.45 us
    unnamed x17, local copies, waits for them, and re-layouts  4.11 us
  transfers between devices with their start and end apart: 37, of which 18 were waited for; matrix products, arithmetic and copies ran while one was open for 0% of the time, Pallas kernels for 24%

profile of v7, /device:TPU:0, one launch (start us, length us, event | category | flops | bytes accessed | tf_op | source)
XLA Modules:
  0.0 173.3 jit_solution(17369101518740141549)
XLA Ops:
  0.5 2.4 %shard_map.91 = (bf16[8,32,512]{2,1,0:T(8,128)(2,1)}, bf16[32,128]{1,0:T(8,128)(2,1)}) custom-call(s32[1]{0:T(128)} %constant.23.clone.1.refs_0_, bf16[128,4096]{1,0:T(8,128)(2,1)} %refs_1_.2, s32[2,128]{1,0:T(2,128)} %bitcast.29, f32[2,128]{1,0:T(2,128)} %bitcast.30, s32[1,8]{1,0:T(1,128)} %refs_4_.6), custom_call_target="tpu_custom_call" | custom-call | flops 33554432 | bytes 1310720 | tf_op jit(solution)/shard_map/pallas_call | solution.py:113
  2.8 11.8 %all_to_all.20.refs_1_.refs_6_ = bf16[8,32,512]{2,1,0:T(8,128)(2,1)S(1)} all-to-all(bf16[8,32,512]{2,1,0:T(8,128)(2,1)} %get-tuple-element.26.refs_5_), channel_id=1, replica_groups=mesh['dp'=8,'et'=4] {'dp'}, dimensions={0} | all-to-all | bytes 524288 | tf_op jit(solution)/shard_map/all_to_all | solution.py:476
  14.6 2.6 %collective-permute-start.3 = (bf16[8,32,512]{2,1,0:T(8,128)(2,1)S(1)}, bf16[8,32,512]{2,1,0:T(8,128)(2,1)S(1)}, u32[]{:S(2)}, u32[]{:S(2)}) collective-permute-start(bf16[8,32,512]{2,1,0:T(8,128)(2,1)S(1)} %all_to_all.20.refs_1_.refs_6_), channel_id=1, source_target_pairs={{0,2},{1,3},{2,0},{3,1},{4,6},{5,7},{6,4},{7,5},{8,10},{9,11},{10,... | collective-permute-start | bytes 786440 | tf_op jit(solution)/shard_map/ppermute | solution.py:83
  17.3 2.3 %copy-done.2 = bf16[4096,512]{1,0:T(8,128)(2,1)S(1)} copy-done((bf16[4096,512]{1,0:T(8,128)(2,1)S(1)}, bf16[4096,512]{1,0:T(8,128)(2,1)}, u32[]{:S(2)}) %copy-start.2) | copy-done | bytes 4194328
  19.7 1.7 copy-done.6
  21.4 3.5 %shard_map.92 = (bf16[128,2048]{1,0:T(8,128)(2,1)S(1)}, bf16[128,2048]{1,0:T(8,128)(2,1)S(1)}) custom-call(s32[10]{0:T(128)S(1)} %stack.43.refs_0_, bf16[8,32,512]{2,1,0:T(8,128)(2,1)S(1)} %all_to_all.20.refs_1_.refs_6_, bf16[8,32,512]{2,1,0:T(8,128)(2,1)S(1)} %collective-permute-done.refs_2_, bf16[4096,512]{1,0:T(8,128)(2,1)S(1)} %copy-done.2, ...), custom_call_target="tpu_custom_call" | custom-call | flops 1073741824 | bytes 5767168 | tf_op jit(solution)/shard_map/pallas_call | solution.py:113
  24.9 5.0 %collective-permute-done.3.refs_1_ = bf16[8,32,512]{2,1,0:T(8,128)(2,1)S(1)} collective-permute-done((bf16[8,32,512]{2,1,0:T(8,128)(2,1)S(1)}, bf16[8,32,512]{2,1,0:T(8,128)(2,1)S(1)}, u32[]{:S(2)}, u32[]{:S(2)}) %collective-permute-start.3) | collective-permute-done | bytes 262176 | tf_op jit(solution)/shard_map/ppermute | solution.py:83
  30.4 1.8 %shard_map.94 = (bf16[2,512,2048]{2,1,0:T(8,128)(2,1)S(1)}, bf16[2,128,2048]{2,1,0:T(8,128)(2,1)S(1)}) custom-call(s32[10]{0:T(128)S(1)} %stack.43.refs_0_, bf16[512,4096]{1,0:T(8,128)(2,1)S(1)} %copy-done, bf16[512,4096]{1,0:T(8,128)(2,1)S(1)} %copy-done.1, bf16[1,128,4096]{2,1,0:T(8,128)(2,1)S(1)} %copy-done.4, bf16[1,128,4096]{2,1,0:T(8,128)(2,1)S(1)} %copy-done.5, ...), custom_call_target="tpu_custom_call" | custom-call | bytes 10485760 | tf_op jit(solution)/shard_map/pallas_call | solution.py:113
  32.9 0.6 collective-permute-start.2
  33.4 3.5 %collective-permute-start.6 = (bf16[8,32,512]{2,1,0:T(8,128)(2,1)S(1)}, bf16[8,32,512]{2,1,0:T(8,128)(2,1)S(1)}, u32[]{:S(2)}, u32[]{:S(2)}) collective-permute-start(bf16[8,32,512]{2,1,0:T(8,128)(2,1)S(1)} %all_to_all.20.refs_1_.refs_6_), channel_id=1, source_target_pairs={{0,3},{1,2},{2,1},{3,0},{4,7},{5,6},{6,5},{7,4},{8,11},{9,10},{10,... | collective-permute-start | bytes 786440 | tf_op jit(solution)/shard_map/ppermute | solution.py:83
  36.9 5.1 %collective-permute-done.2.refs_2_ = bf16[128,2048]{1,0:T(8,128)(2,1)S(1)} collective-permute-done((bf16[128,2048]{1,0:T(8,128)(2,1)S(1)}, bf16[128,2048]{1,0:T(8,128)(2,1)S(1)}, u32[]{:S(2)}, u32[]{:S(2)}) %collective-permute-start.2) | collective-permute-done | bytes 524320 | tf_op jit(solution)/shard_map/ppermute | solution.py:88
  42.0 0.6 shard_map.95.refs_5_
  42.6 0.6 collective-permute-start.4
  43.3 3.4 %shard_map.96 = (bf16[128,2048]{1,0:T(8,128)(2,1)S(1)}, bf16[128,2048]{1,0:T(8,128)(2,1)S(1)}) custom-call(s32[10]{0:T(128)S(1)} %stack.43.refs_0_, bf16[8,32,512]{2,1,0:T(8,128)(2,1)S(1)} %shard_map.93.refs_5_.refs_1_, bf16[8,32,512]{2,1,0:T(8,128)(2,1)S(1)} %collective-permute-done.7.refs_2_, bf16[4096,512]{1,0:T(8,128)(2,1)S(1)} %copy-done.3, ...), custom_call_target="tpu_custom_call" | custom-call | flops 1073741824 | bytes 5767168 | tf_op jit(solution)/shard_map/pallas_call | solution.py:113
  46.7 0.6 collective-permute-start.13
  47.3 0.6 shard_map.97.refs_8_.refs_1_
  47.9 1.9 %collective-permute-done.4.refs_3_ = bf16[64,2048]{1,0:T(8,128)(2,1)S(1)} collective-permute-done((bf16[64,2048]{1,0:T(8,128)(2,1)S(1)}, bf16[64,2048]{1,0:T(8,128)(2,1)S(1)}, u32[]{:S(2)}, u32[]{:S(2)}) %collective-permute-start.4) | collective-permute-done | bytes 262176 | tf_op jit(solution)/shard_map/ppermute | solution.py:88
  49.8 0.9 shard_map.98.refs_5_.refs_1_
  50.7 0.6 collective-permute-start.9
  51.3 1.5 collective-permute-done.14.refs_2_
  52.9 3.4 %shard_map.99 = (bf16[128,2048]{1,0:T(8,128)(2,1)S(1)}, bf16[128,2048]{1,0:T(8,128)(2,1)S(1)}) custom-call(s32[10]{0:T(128)S(1)} %stack.43.refs_0_, bf16[8,32,512]{2,1,0:T(8,128)(2,1)S(1)} %shard_map.97.refs_8_.refs_1_, bf16[8,32,512]{2,1,0:T(8,128)(2,1)S(1)} %collective-permute-done.14.refs_2_, bf16[4096,512]{1,0:T(8,128)(2,1)S(1)} %copy-done.3, ...), custom_call_target="tpu_custom_call" | custom-call | flops 1073741824 | bytes 5767168 | tf_op jit(solution)/shard_map/pallas_call | solution.py:113
  56.8 0.7 collective-permute-start.12
  57.5 3.4 %collective-permute-done.13.refs_2_ = bf16[128,2048]{1,0:T(8,128)(2,1)S(1)} collective-permute-done((bf16[128,2048]{1,0:T(8,128)(2,1)S(1)}, bf16[128,2048]{1,0:T(8,128)(2,1)S(1)}, u32[]{:S(2)}, u32[]{:S(2)}) %collective-permute-start.13) | collective-permute-done | bytes 524320 | tf_op jit(solution)/shard_map/ppermute | solution.py:88
  60.9 0.6 collective-permute-done.9.refs_4_.refs_3_
  61.5 0.6 shard_map.100.refs_2_
  62.1 1.4 collective-permute-start.17
  63.6 2.3 %collective-permute-done.12.refs_1_ = bf16[8,32,512]{2,1,0:T(8,128)(2,1)S(1)} collective-permute-done((bf16[8,32,512]{2,1,0:T(8,128)(2,1)S(1)}, bf16[8,32,512]{2,1,0:T(8,128)(2,1)S(1)}, u32[]{:S(2)}, u32[]{:S(2)}) %collective-permute-start.12) | collective-permute-done | bytes 262176 | tf_op jit(solution)/shard_map/ppermute | solution.py:83
  65.9 0.6 shard_map.101.refs_8_.refs_1_
  66.4 5.0 %collective-permute-done.17.refs_3_ = bf16[64,2048]{1,0:T(8,128)(2,1)S(1)} collective-permute-done((bf16[64,2048]{1,0:T(8,128)(2,1)S(1)}, bf16[64,2048]{1,0:T(8,128)(2,1)S(1)}, u32[]{:S(2)}, u32[]{:S(2)}) %collective-permute-start.17) | collective-permute-done | bytes 262176 | tf_op jit(solution)/shard_map/ppermute | solution.py:88
  71.4 0.9 shard_map.102.refs_3_.refs_1_
  72.3 1.0 collective-permute-start.18
  73.4 0.6 shard_map.103.refs_5_
  74.0 0.9 collective-permute-done.15.refs_2_
  74.9 1.1 collective-permute-start.21
  76.0 3.4 %shard_map.104 = (bf16[128,2048]{1,0:T(8,128)(2,1)S(1)}, bf16[128,2048]{1,0:T(8,128)(2,1)S(1)}) custom-call(s32[10]{0:T(128)S(1)} %stack.43.refs_0_, bf16[8,32,512]{2,1,0:T(8,128)(2,1)S(1)} %shard_map.101.refs_8_.refs_1_, bf16[8,32,512]{2,1,0:T(8,128)(2,1)S(1)} %collective-permute-done.15.refs_2_, bf16[4096,512]{1,0:T(8,128)(2,1)S(1)} %copy-done.3, ...), custom_call_target="tpu_custom_call" | custom-call | flops 1073741824 | bytes 5767168 | tf_op jit(solution)/shard_map/pallas_call | solution.py:113
  79.6 7.8 %collective-permute-done.10.refs_4_ = bf16[64,4096]{1,0:T(8,128)(2,1)S(1)} collective-permute-done((bf16[64,4096]{1,0:T(8,128)(2,1)S(1)}, bf16[64,4096]{1,0:T(8,128)(2,1)S(1)}, u32[]{:S(2)}, u32[]{:S(2)}) %collective-permute-start.10) | collective-permute-done | bytes 524320 | tf_op jit(solution)/shard_map/ppermute | solution.py:88
  87.5 4.2 %shard_map.105 = (f32[1,8,32,512]{3,2,1,0:T(8,128)S(1)}, bf16[1,8,32,512]{3,2,1,0:T(8,128)(2,1)S(1)}) custom-call(s32[10]{0:T(128)S(1)} %stack.43.refs_0_, bf16[64,4096]{1,0:T(8,128)(2,1)S(1)} %shard_map.98.refs_5_.refs_1_, bf16[64,4096]{1,0:T(8,128)(2,1)S(1)} %collective-permute-done.8.refs_2_, bf16[64,4096]{1,0:T(8,128)(2,1)S(1)} %collective-permute-done.9.refs_4_.refs_3_, ...), custom_call_target="tpu_custom_call" | custom-call | flops 2147483648 | bytes 11272192 | tf_op jit(solution)/shard_map/pallas_call | solution.py:113
  91.7 1.2 collective-permute-done.21.refs_3_
  92.9 0.9 shard_map.106.refs_3_.refs_1_
  93.7 1.0 collective-permute-start.25
  94.8 2.0 %collective-permute-start.23 = (bf16[64,4096]{1,0:T(8,128)(2,1)S(1)}, bf16[64,4096]{1,0:T(8,128)(2,1)S(1)}, u32[]{:S(2)}, u32[]{:S(2)}) collective-permute-start(bf16[64,4096]{1,0:T(8,128)(2,1)S(1)} %collective-permute-done.18.refs_10_.refs_3_), channel_id=1, source_target_pairs={{0,8},{4,20},{8,0},{12,28},{16,24},{20,4},{24,16},{28,12},{1,9},{5... | collective-permute-start | bytes 1572872 | tf_op jit(solution)/shard_map/ppermute | solution.py:88
  96.8 0.6 shard_map.107.refs_3_
  97.4 1.1 collective-permute-start.24
  98.5 0.6 shard_map.108.refs_8_.refs_4_
  99.1 15.1 %collective-permute-done.24.refs_3_ = bf16[64,2048]{1,0:T(8,128)(2,1)S(1)} collective-permute-done((bf16[64,2048]{1,0:T(8,128)(2,1)S(1)}, bf16[64,2048]{1,0:T(8,128)(2,1)S(1)}, u32[]{:S(2)}, u32[]{:S(2)}) %collective-permute-start.24) | collective-permute-done | bytes 262176 | tf_op jit(solution)/shard_map/ppermute | solution.py:88
  114.3 0.9 shard_map.109.refs_9_.refs_1_
  115.2 1.0 collective-permute-start.30
  116.2 2.0 %collective-permute-start.29 = (bf16[64,4096]{1,0:T(8,128)(2,1)S(1)}, bf16[64,4096]{1,0:T(8,128)(2,1)S(1)}, u32[]{:S(2)}, u32[]{:S(2)}) collective-permute-start(bf16[64,4096]{1,0:T(8,128)(2,1)S(1)} %collective-permute-done.25.refs_9_.refs_3_), channel_id=1, source_target_pairs={{0,8},{4,20},{8,0},{12,28},{16,24},{20,4},{24,16},{28,12},{1,9},{5... | collective-permute-start | bytes 1572872 | tf_op jit(solution)/shard_map/ppermute | solution.py:88
  118.2 4.2 %shard_map.110 = (f32[1,8,32,512]{3,2,1,0:T(8,128)S(1)}, bf16[1,8,32,512]{3,2,1,0:T(8,128)(2,1)S(1)}) custom-call(s32[10]{0:T(128)S(1)} %stack.43.refs_0_, bf16[64,4096]{1,0:T(8,128)(2,1)S(1)} %shard_map.102.refs_3_.refs_1_, bf16[64,4096]{1,0:T(8,128)(2,1)S(1)} %collective-permute-done.22.refs_2_, ...), custom_call_target="tpu_custom_call" | custom-call | flops 2147483648 | bytes 11272192 | tf_op jit(solution)/shard_map/pallas_call | solution.py:113
  122.6 7.5 %collective-permute-done.30.refs_10_.refs_3_ = bf16[64,4096]{1,0:T(8,128)(2,1)S(1)} collective-permute-done((bf16[64,4096]{1,0:T(8,128)(2,1)S(1)}, bf16[64,4096]{1,0:T(8,128)(2,1)S(1)}, u32[]{:S(2)}, u32[]{:S(2)}) %collective-permute-start.30) | collective-permute-done | bytes 524320 | tf_op jit(solution)/shard_map/ppermute | solution.py:88
  130.2 0.6 shard_map.111.refs_9_
  130.9 1.1 collective-permute-done.29.refs_4_
  132.0 4.2 %shard_map.112 = (f32[1,8,32,512]{3,2,1,0:T(8,128)S(1)}, bf16[1,8,32,512]{3,2,1,0:T(8,128)(2,1)S(1)}) custom-call(s32[10]{0:T(128)S(1)} %stack.43.refs_0_, bf16[64,4096]{1,0:T(8,128)(2,1)S(1)} %shard_map.106.refs_3_.refs_1_, bf16[64,4096]{1,0:T(8,128)(2,1)S(1)} %collective-permute-done.28.refs_2_, ...), custom_call_target="tpu_custom_call" | custom-call | flops 2147483648 | bytes 11272192 | tf_op jit(solution)/shard_map/pallas_call | solution.py:113
  136.7 4.3 %collective-permute-done.27.refs_4_ = bf16[8,32,512]{2,1,0:T(8,128)(2,1)S(1)} collective-permute-done((bf16[8,32,512]{2,1,0:T(8,128)(2,1)S(1)}, bf16[8,32,512]{2,1,0:T(8,128)(2,1)S(1)}, u32[]{:S(2)}, u32[]{:S(2)}) %collective-permute-start.27) | collective-permute-done | bytes 262176 | tf_op jit(solution)/shard_map/ppermute | solution.py:83
  141.0 0.6 shard_map.113.refs_9_
  141.6 1.0 collective-permute-start.32
  142.5 0.7 collective-permute-done.34.refs_4_
  143.2 4.2 %shard_map.114 = (f32[1,8,32,512]{3,2,1,0:T(8,128)S(1)}, bf16[1,8,32,512]{3,2,1,0:T(8,128)(2,1)S(1)}) custom-call(s32[10]{0:T(128)S(1)} %stack.43.refs_0_, bf16[64,4096]{1,0:T(8,128)(2,1)S(1)} %shard_map.109.refs_9_.refs_1_, bf16[64,4096]{1,0:T(8,128)(2,1)S(1)} %collective-permute-done.33.refs_2_, ...), custom_call_target="tpu_custom_call" | custom-call | flops 2147483648 | bytes 11272192 | tf_op jit(solution)/shard_map/pallas_call | solution.py:113
  147.7 2.2 %collective-permute-done.32.refs_4_ = bf16[8,32,512]{2,1,0:T(8,128)(2,1)S(1)} collective-permute-done((bf16[8,32,512]{2,1,0:T(8,128)(2,1)S(1)}, bf16[8,32,512]{2,1,0:T(8,128)(2,1)S(1)}, u32[]{:S(2)}, u32[]{:S(2)}) %collective-permute-start.32) | collective-permute-done | bytes 262176 | tf_op jit(solution)/shard_map/ppermute | solution.py:83
  149.9 0.6 shard_map.115
  150.5 5.3 %collective-permute-start.36 = (bf16[8,32,512]{2,1,0:T(8,128)(2,1)S(1)}, bf16[8,32,512]{2,1,0:T(8,128)(2,1)S(1)}, u32[]{:S(2)}, u32[]{:S(2)}) collective-permute-start(bf16[8,32,512]{2,1,0:T(8,128)(2,1)S(1)} %shard_map.115), channel_id=1, source_target_pairs={{0,1},{1,0},{2,3},{3,2},{4,5},{5,4},{6,7},{7,6},{8,9},{9,8},{10,11... | collective-permute-start | bytes 786440 | tf_op jit(solution)/shard_map/ppermute | solution.py:83
  155.8 6.5 %collective-permute-done.36 = bf16[8,32,512]{2,1,0:T(8,128)(2,1)S(1)} collective-permute-done((bf16[8,32,512]{2,1,0:T(8,128)(2,1)S(1)}, bf16[8,32,512]{2,1,0:T(8,128)(2,1)S(1)}, u32[]{:S(2)}, u32[]{:S(2)}) %collective-permute-start.36) | collective-permute-done | bytes 262176 | tf_op jit(solution)/shard_map/ppermute | solution.py:83
  162.4 9.4 %all_to_all.21 = bf16[8,32,1,512]{3,1,2,0:T(8,128)(2,1)S(1)} all-to-all(bf16[8,32,1,512]{3,1,2,0:T(8,128)(2,1)S(1)} %fusion), channel_id=1, replica_groups=mesh['dp'=8,'et'=4] {'dp'}, dimensions={0} | all-to-all | bytes 524288 | tf_op jit(solution)/shard_map/all_to_all | solution.py:497
  171.9 1.4 convolution_convert_fusion
  (57 shorter events, 3.9 us)
Async XLA Ops:
  0.0 17.3 %collective-permute-start.1 = (bf16[4096,512]{1,0:T(8,128)(2,1)}, bf16[4096,512]{1,0:T(8,128)(2,1)}, u32[]{:S(2)}, u32[]{:S(2)}) collective-permute-start(bf16[4096,512]{1,0:T(8,128)(2,1)} %refs_3_.9), channel_id=1, source_target_pairs={{0,4},{4,0},{8,12},{12,8},{16,20},{20,16},{24,28},{28,24},{1,5},{5... | collective-permute-start | bytes 12582920 | tf_op jit(solution)/shard_map/ppermute | solution.py:83
  14.6 2.7 %collective-permute-start = (bf16[8,32,512]{2,1,0:T(8,128)(2,1)S(1)}, bf16[8,32,512]{2,1,0:T(8,128)(2,1)S(1)}, u32[]{:S(2)}, u32[]{:S(2)}) collective-permute-start(bf16[8,32,512]{2,1,0:T(8,128)(2,1)S(1)} %all_to_all.20.refs_1_.refs_6_), channel_id=1, source_target_pairs={{0,4},{4,0},{8,12},{12,8},{16,20},{20,16},{24,28},{28,24},{1,5},{5... | collective-permute-start | bytes 786440 | tf_op jit(solution)/shard_map/ppermute | solution.py:83
  14.6 15.2 %collective-permute-start.3 = (bf16[8,32,512]{2,1,0:T(8,128)(2,1)S(1)}, bf16[8,32,512]{2,1,0:T(8,128)(2,1)S(1)}, u32[]{:S(2)}, u32[]{:S(2)}) collective-permute-start(bf16[8,32,512]{2,1,0:T(8,128)(2,1)S(1)} %all_to_all.20.refs_1_.refs_6_), channel_id=1, source_target_pairs={{0,2},{1,3},{2,0},{3,1},{4,6},{5,7},{6,4},{7,5},{8,10},{9,11},{10,... | collective-permute-start | bytes 786440 | tf_op jit(solution)/shard_map/ppermute | solution.py:83
  17.3 13.1 %copy-start = (bf16[512,4096]{1,0:T(8,128)(2,1)S(1)}, bf16[512,4096]{1,0:T(8,128)(2,1)}, u32[]{:S(2)}) copy-start(bf16[512,4096]{1,0:T(8,128)(2,1)} %refs_5_.15) | copy-start | bytes 12582916
  17.3 13.1 %copy-start.1 = (bf16[512,4096]{1,0:T(8,128)(2,1)S(1)}, bf16[512,4096]{1,0:T(8,128)(2,1)}, u32[]{:S(2)}) copy-start(bf16[512,4096]{1,0:T(8,128)(2,1)} %refs_6_.7) | copy-start | bytes 12582916
  17.3 2.3 %copy-start.2 = (bf16[4096,512]{1,0:T(8,128)(2,1)S(1)}, bf16[4096,512]{1,0:T(8,128)(2,1)}, u32[]{:S(2)}) copy-start(bf16[4096,512]{1,0:T(8,128)(2,1)} %refs_3_.9) | copy-start | bytes 12582916
  19.6 1.7 copy-start.6
  21.4 9.0 %copy-start.4 = (bf16[1,128,4096]{2,1,0:T(8,128)(2,1)S(1)}, bf16[1,128,4096]{2,1,0:T(8,128)(2,1)}, u32[]{:S(2)}) copy-start(bf16[1,128,4096]{2,1,0:T(8,128)(2,1)} %refs_4_.11) | copy-start | bytes 3145732
  21.4 9.0 %copy-start.5 = (bf16[1,128,4096]{2,1,0:T(8,128)(2,1)S(1)}, bf16[1,128,4096]{2,1,0:T(8,128)(2,1)}, u32[]{:S(2)}) copy-start(bf16[1,128,4096]{2,1,0:T(8,128)(2,1)} %refs_5_.12) | copy-start | bytes 3145732
  32.3 11.0 %copy-start.3 = (bf16[4096,512]{1,0:T(8,128)(2,1)S(1)}, bf16[4096,512]{1,0:T(8,128)(2,1)}, u32[]{:S(2)}) copy-start(bf16[4096,512]{1,0:T(8,128)(2,1)} %refs_3_.9) | copy-start | bytes 12582916
  32.3 55.2 %collective-permute-start.11 = (bf16[2,512,2048]{2,1,0:T(8,128)(2,1)S(1)}, bf16[2,512,2048]{2,1,0:T(8,128)(2,1)S(1)}, u32[]{:S(2)}, u32[]{:S(2)}) collective-permute-start(bf16[2,512,2048]{2,1,0:T(8,128)(2,1)S(1)} %get-tuple-element.29.refs_3_), channel_id=1, source_target_pairs={{0,4},{4,0},{8,12},{12,8},{16,20},{20,16},{24,28},{28,24},{1,5},{5... | collective-permute-start | bytes 12582920 | tf_op jit(solution)/shard_map/ppermute | solution.py:83
  32.4 17.4 %collective-permute-start.5 = (bf16[2,128,2048]{2,1,0:T(8,128)(2,1)S(1)}, bf16[2,128,2048]{2,1,0:T(8,128)(2,1)S(1)}, u32[]{:S(2)}, u32[]{:S(2)}) collective-permute-start(bf16[2,128,2048]{2,1,0:T(8,128)(2,1)S(1)} %get-tuple-element.30), channel_id=1, source_target_pairs={{0,4},{4,0},{8,12},{12,8},{16,20},{20,16},{24,28},{28,24},{1,5},{5... | collective-permute-start | bytes 3145736 | tf_op jit(solution)/shard_map/ppermute | solution.py:83
  32.9 9.2 %collective-permute-start.2 = (bf16[128,2048]{1,0:T(8,128)(2,1)S(1)}, bf16[128,2048]{1,0:T(8,128)(2,1)S(1)}, u32[]{:S(2)}, u32[]{:S(2)}) collective-permute-start(bf16[128,2048]{1,0:T(8,128)(2,1)S(1)} %get-tuple-element.28.refs_2_), channel_id=1, source_target_pairs={{0,8},{4,20},{8,0},{12,28},{16,24},{20,4},{24,16},{28,12},{1,9},{5... | collective-permute-start | bytes 1572872 | tf_op jit(solution)/shard_map/ppermute | solution.py:88
  33.4 9.9 %collective-permute-start.7 = (bf16[8,32,512]{2,1,0:T(8,128)(2,1)S(1)}, bf16[8,32,512]{2,1,0:T(8,128)(2,1)S(1)}, u32[]{:S(2)}, u32[]{:S(2)}) collective-permute-start(bf16[8,32,512]{2,1,0:T(8,128)(2,1)S(1)} %shard_map.93.refs_5_.refs_1_), channel_id=1, source_target_pairs={{0,4},{4,0},{8,12},{12,8},{16,20},{20,16},{24,28},{28,24},{1,5},{5... | collective-permute-start | bytes 786440 | tf_op jit(solution)/shard_map/ppermute | solution.py:83
  33.4 13.9 %collective-permute-start.6 = (bf16[8,32,512]{2,1,0:T(8,128)(2,1)S(1)}, bf16[8,32,512]{2,1,0:T(8,128)(2,1)S(1)}, u32[]{:S(2)}, u32[]{:S(2)}) collective-permute-start(bf16[8,32,512]{2,1,0:T(8,128)(2,1)S(1)} %all_to_all.20.refs_1_.refs_6_), channel_id=1, source_target_pairs={{0,3},{1,2},{2,1},{3,0},{4,7},{5,6},{6,5},{7,4},{8,11},{9,10},{10,... | collective-permute-start | bytes 786440 | tf_op jit(solution)/shard_map/ppermute | solution.py:83
  42.6 7.2 %collective-permute-start.4 = (bf16[64,2048]{1,0:T(8,128)(2,1)S(1)}, bf16[64,2048]{1,0:T(8,128)(2,1)S(1)}, u32[]{:S(2)}, u32[]{:S(2)}) collective-permute-start(bf16[64,2048]{1,0:T(8,128)(2,1)S(1)} %shard_map.95.refs_5_), channel_id=1, source_target_pairs={{0,16},{4,12},{8,24},{12,4},{16,0},{20,28},{24,8},{28,20},{1,17},{... | collective-permute-start | bytes 786440 | tf_op jit(solution)/shard_map/ppermute | solution.py:88
  46.7 14.2 %collective-permute-start.13 = (bf16[128,2048]{1,0:T(8,128)(2,1)S(1)}, bf16[128,2048]{1,0:T(8,128)(2,1)S(1)}, u32[]{:S(2)}, u32[]{:S(2)}) collective-permute-start(bf16[128,2048]{1,0:T(8,128)(2,1)S(1)} %get-tuple-element.31.refs_2_), channel_id=1, source_target_pairs={{0,8},{4,20},{8,0},{12,28},{16,24},{20,4},{24,16},{28,12},{1,9},{5... | collective-permute-start | bytes 1572872 | tf_op jit(solution)/shard_map/ppermute | solution.py:88
  50.7 10.8 %collective-permute-start.9 = (bf16[64,4096]{1,0:T(8,128)(2,1)S(1)}, bf16[64,4096]{1,0:T(8,128)(2,1)S(1)}, u32[]{:S(2)}, u32[]{:S(2)}) collective-permute-start(bf16[64,4096]{1,0:T(8,128)(2,1)S(1)} %shard_map.98.refs_5_.refs_1_), channel_id=1, source_target_pairs={{0,16},{4,12},{8,24},{12,4},{16,0},{20,28},{24,8},{28,20},{1,17},{... | collective-permute-start | bytes 1572872 | tf_op jit(solution)/shard_map/ppermute | solution.py:88
  51.3 1.5 collective-permute-start.14
  56.3 17.1 %collective-permute-start.16 = (bf16[128,2048]{1,0:T(8,128)(2,1)S(1)}, bf16[128,2048]{1,0:T(8,128)(2,1)S(1)}, u32[]{:S(2)}, u32[]{:S(2)}) collective-permute-start(bf16[128,2048]{1,0:T(8,128)(2,1)S(1)} %get-tuple-element.33.refs_3_), channel_id=1, source_target_pairs={{0,8},{4,20},{8,0},{12,28},{16,24},{20,4},{24,16},{28,12},{1,9},{5... | collective-permute-start | bytes 1572872 | tf_op jit(solution)/shard_map/ppermute | solution.py:88
  56.8 9.1 %collective-permute-start.12 = (bf16[8,32,512]{2,1,0:T(8,128)(2,1)S(1)}, bf16[8,32,512]{2,1,0:T(8,128)(2,1)S(1)}, u32[]{:S(2)}, u32[]{:S(2)}) collective-permute-start(bf16[8,32,512]{2,1,0:T(8,128)(2,1)S(1)} %all_to_all.20.refs_1_.refs_6_), channel_id=1, source_target_pairs={{0,1},{1,0},{2,3},{3,2},{4,5},{5,4},{6,7},{7,6},{8,9},{9,8},{10,11... | collective-permute-start | bytes 786440 | tf_op jit(solution)/shard_map/ppermute | solution.py:83
  62.1 9.3 %collective-permute-start.17 = (bf16[64,2048]{1,0:T(8,128)(2,1)S(1)}, bf16[64,2048]{1,0:T(8,128)(2,1)S(1)}, u32[]{:S(2)}, u32[]{:S(2)}) collective-permute-start(bf16[64,2048]{1,0:T(8,128)(2,1)S(1)} %shard_map.100.refs_2_), channel_id=1, source_target_pairs={{0,16},{4,12},{8,24},{12,4},{16,0},{20,28},{24,8},{28,20},{1,17},{... | collective-permute-start | bytes 786440 | tf_op jit(solution)/shard_map/ppermute | solution.py:88
  63.5 15.9 %collective-permute-start.8 = (bf16[64,4096]{1,0:T(8,128)(2,1)S(1)}, bf16[64,4096]{1,0:T(8,128)(2,1)S(1)}, u32[]{:S(2)}, u32[]{:S(2)}) collective-permute-start(bf16[64,4096]{1,0:T(8,128)(2,1)S(1)} %shard_map.98.refs_5_.refs_1_), channel_id=1, source_target_pairs={{0,8},{4,20},{8,0},{12,28},{16,24},{20,4},{24,16},{28,12},{1,9},{5... | collective-permute-start | bytes 1572872 | tf_op jit(solution)/shard_map/ppermute | solution.py:88
  65.9 21.6 %collective-permute-start.10 = (bf16[64,4096]{1,0:T(8,128)(2,1)S(1)}, bf16[64,4096]{1,0:T(8,128)(2,1)S(1)}, u32[]{:S(2)}, u32[]{:S(2)}) collective-permute-start(bf16[64,4096]{1,0:T(8,128)(2,1)S(1)} %collective-permute-done.9.refs_4_.refs_3_), channel_id=1, source_target_pairs={{0,8},{4,20},{8,0},{12,28},{16,24},{20,4},{24,16},{28,12},{1,9},{5... | collective-permute-start | bytes 1572872 | tf_op jit(solution)/shard_map/ppermute | solution.py:88
  72.3 15.2 %collective-permute-start.18 = (bf16[64,4096]{1,0:T(8,128)(2,1)S(1)}, bf16[64,4096]{1,0:T(8,128)(2,1)S(1)}, u32[]{:S(2)}, u32[]{:S(2)}) collective-permute-start(bf16[64,4096]{1,0:T(8,128)(2,1)S(1)} %shard_map.102.refs_3_.refs_1_), channel_id=1, source_target_pairs={{0,16},{4,12},{8,24},{12,4},{16,0},{20,28},{24,8},{28,20},{1,17},{... | collective-permute-start | bytes 1572872 | tf_op jit(solution)/shard_map/ppermute | solution.py:88
  73.3 1.5 collective-permute-start.15
  74.9 18.0 %collective-permute-start.21 = (bf16[64,2048]{1,0:T(8,128)(2,1)S(1)}, bf16[64,2048]{1,0:T(8,128)(2,1)S(1)}, u32[]{:S(2)}, u32[]{:S(2)}) collective-permute-start(bf16[64,2048]{1,0:T(8,128)(2,1)S(1)} %shard_map.103.refs_5_), channel_id=1, source_target_pairs={{0,16},{4,12},{8,24},{12,4},{16,0},{20,28},{24,8},{28,20},{1,17},{... | collective-permute-start | bytes 786440 | tf_op jit(solution)/shard_map/ppermute | solution.py:88
  79.4 17.4 %collective-permute-start.20 = (bf16[128,2048]{1,0:T(8,128)(2,1)S(1)}, bf16[128,2048]{1,0:T(8,128)(2,1)S(1)}, u32[]{:S(2)}, u32[]{:S(2)}) collective-permute-start(bf16[128,2048]{1,0:T(8,128)(2,1)S(1)} %get-tuple-element.35.refs_9_), channel_id=1, source_target_pairs={{0,8},{4,20},{8,0},{12,28},{16,24},{20,4},{24,16},{28,12},{1,9},{5... | collective-permute-start | bytes 1572872 | tf_op jit(solution)/shard_map/ppermute | solution.py:88
  93.7 20.5 %collective-permute-start.25 = (bf16[64,4096]{1,0:T(8,128)(2,1)S(1)}, bf16[64,4096]{1,0:T(8,128)(2,1)S(1)}, u32[]{:S(2)}, u32[]{:S(2)}) collective-permute-start(bf16[64,4096]{1,0:T(8,128)(2,1)S(1)} %shard_map.106.refs_3_.refs_1_), channel_id=1, source_target_pairs={{0,16},{4,12},{8,24},{12,4},{16,0},{20,28},{24,8},{28,20},{1,17},{... | collective-permute-start | bytes 1572872 | tf_op jit(solution)/shard_map/ppermute | solution.py:88
  94.8 23.4 %collective-permute-start.22 = (bf16[64,4096]{1,0:T(8,128)(2,1)S(1)}, bf16[64,4096]{1,0:T(8,128)(2,1)S(1)}, u32[]{:S(2)}, u32[]{:S(2)}) collective-permute-start(bf16[64,4096]{1,0:T(8,128)(2,1)S(1)} %shard_map.102.refs_3_.refs_1_), channel_id=1, source_target_pairs={{0,8},{4,20},{8,0},{12,28},{16,24},{20,4},{24,16},{28,12},{1,9},{5... | collective-permute-start | bytes 1572872 | tf_op jit(solution)/shard_map/ppermute | solution.py:88
  94.8 23.4 %collective-permute-start.23 = (bf16[64,4096]{1,0:T(8,128)(2,1)S(1)}, bf16[64,4096]{1,0:T(8,128)(2,1)S(1)}, u32[]{:S(2)}, u32[]{:S(2)}) collective-permute-start(bf16[64,4096]{1,0:T(8,128)(2,1)S(1)} %collective-permute-done.18.refs_10_.refs_3_), channel_id=1, source_target_pairs={{0,8},{4,20},{8,0},{12,28},{16,24},{20,4},{24,16},{28,12},{1,9},{5... | collective-permute-start | bytes 1572872 | tf_op jit(solution)/shard_map/ppermute | solution.py:88
  96.8 1.7 %collective-permute-start.19 = (bf16[1,8,32,512]{3,2,1,0:T(8,128)(2,1)S(1)}, bf16[1,8,32,512]{3,2,1,0:T(8,128)(2,1)S(1)}, u32[]{:S(2)}, u32[]{:S(2)}) collective-permute-start(bf16[1,8,32,512]{3,2,1,0:T(8,128)(2,1)S(1)} %get-tuple-element.37), channel_id=1, source_target_pairs={{0,4},{4,0},{8,12},{12,8},{16,20},{20,16},{24,28},{28,24},{1,5},{5... | collective-permute-start | bytes 786440 | tf_op jit(solution)/shard_map/ppermute | solution.py:83
  97.4 16.9 %collective-permute-start.24 = (bf16[64,2048]{1,0:T(8,128)(2,1)S(1)}, bf16[64,2048]{1,0:T(8,128)(2,1)S(1)}, u32[]{:S(2)}, u32[]{:S(2)}) collective-permute-start(bf16[64,2048]{1,0:T(8,128)(2,1)S(1)} %shard_map.107.refs_3_), channel_id=1, source_target_pairs={{0,16},{4,12},{8,24},{12,4},{16,0},{20,28},{24,8},{28,20},{1,17},{... | collective-permute-start | bytes 786440 | tf_op jit(solution)/shard_map/ppermute | solution.py:88
  115.2 14.9 %collective-permute-start.30 = (bf16[64,4096]{1,0:T(8,128)(2,1)S(1)}, bf16[64,4096]{1,0:T(8,128)(2,1)S(1)}, u32[]{:S(2)}, u32[]{:S(2)}) collective-permute-start(bf16[64,4096]{1,0:T(8,128)(2,1)S(1)} %shard_map.109.refs_9_.refs_1_), channel_id=1, source_target_pairs={{0,16},{4,12},{8,24},{12,4},{16,0},{20,28},{24,8},{28,20},{1,17},{... | collective-permute-start | bytes 1572872 | tf_op jit(solution)/shard_map/ppermute | solution.py:88
  116.1 14.7 %collective-permute-start.28 = (bf16[64,4096]{1,0:T(8,128)(2,1)S(1)}, bf16[64,4096]{1,0:T(8,128)(2,1)S(1)}, u32[]{:S(2)}, u32[]{:S(2)}) collective-permute-start(bf16[64,4096]{1,0:T(8,128)(2,1)S(1)} %shard_map.106.refs_3_.refs_1_), channel_id=1, source_target_pairs={{0,8},{4,20},{8,0},{12,28},{16,24},{20,4},{24,16},{28,12},{1,9},{5... | collective-permute-start | bytes 1572872 | tf_op jit(solution)/shard_map/ppermute | solution.py:88
  116.2 15.8 %collective-permute-start.29 = (bf16[64,4096]{1,0:T(8,128)(2,1)S(1)}, bf16[64,4096]{1,0:T(8,128)(2,1)S(1)}, u32[]{:S(2)}, u32[]{:S(2)}) collective-permute-start(bf16[64,4096]{1,0:T(8,128)(2,1)S(1)} %collective-permute-done.25.refs_9_.refs_3_), channel_id=1, source_target_pairs={{0,8},{4,20},{8,0},{12,28},{16,24},{20,4},{24,16},{28,12},{1,9},{5... | collective-permute-start | bytes 1572872 | tf_op jit(solution)/shard_map/ppermute | solution.py:88
  122.4 7.8 %collective-permute-start.26 = (bf16[1,8,32,512]{3,2,1,0:T(8,128)(2,1)S(1)}, bf16[1,8,32,512]{3,2,1,0:T(8,128)(2,1)S(1)}, u32[]{:S(2)}, u32[]{:S(2)}) collective-permute-start(bf16[1,8,32,512]{3,2,1,0:T(8,128)(2,1)S(1)} %get-tuple-element.40), channel_id=1, source_target_pairs={{0,4},{4,0},{8,12},{12,8},{16,20},{20,16},{24,28},{28,24},{1,5},{5... | collective-permute-start | bytes 786440 | tf_op jit(solution)/shard_map/ppermute | solution.py:83
  122.5 20.0 %collective-permute-start.33 = (bf16[64,4096]{1,0:T(8,128)(2,1)S(1)}, bf16[64,4096]{1,0:T(8,128)(2,1)S(1)}, u32[]{:S(2)}, u32[]{:S(2)}) collective-permute-start(bf16[64,4096]{1,0:T(8,128)(2,1)S(1)} %shard_map.109.refs_9_.refs_1_), channel_id=1, source_target_pairs={{0,8},{4,20},{8,0},{12,28},{16,24},{20,4},{24,16},{28,12},{1,9},{5... | collective-permute-start | bytes 1572872 | tf_op jit(solution)/shard_map/ppermute | solution.py:88
  130.1 13.1 %collective-permute-start.34 = (bf16[64,4096]{1,0:T(8,128)(2,1)S(1)}, bf16[64,4096]{1,0:T(8,128)(2,1)S(1)}, u32[]{:S(2)}, u32[]{:S(2)}) collective-permute-start(bf16[64,4096]{1,0:T(8,128)(2,1)S(1)} %collective-permute-done.30.refs_10_.refs_3_), channel_id=1, source_target_pairs={{0,8},{4,20},{8,0},{12,28},{16,24},{20,4},{24,16},{28,12},{1,9},{5... | collective-permute-start | bytes 1572872 | tf_op jit(solution)/shard_map/ppermute | solution.py:88
  130.8 10.1 %collective-permute-start.27 = (bf16[8,32,512]{2,1,0:T(8,128)(2,1)S(1)}, bf16[8,32,512]{2,1,0:T(8,128)(2,1)S(1)}, u32[]{:S(2)}, u32[]{:S(2)}) collective-permute-start(bf16[8,32,512]{2,1,0:T(8,128)(2,1)S(1)} %shard_map.111.refs_9_), channel_id=1, source_target_pairs={{0,2},{1,3},{2,0},{3,1},{4,6},{5,7},{6,4},{7,5},{8,10},{9,11},{10,... | collective-permute-start | bytes 786440 | tf_op jit(solution)/shard_map/ppermute | solution.py:83
  136.2 4.7 %collective-permute-start.31 = (bf16[1,8,32,512]{3,2,1,0:T(8,128)(2,1)S(1)}, bf16[1,8,32,512]{3,2,1,0:T(8,128)(2,1)S(1)}, u32[]{:S(2)}, u32[]{:S(2)}) collective-permute-start(bf16[1,8,32,512]{3,2,1,0:T(8,128)(2,1)S(1)} %get-tuple-element.42), channel_id=1, source_target_pairs={{0,4},{4,0},{8,12},{12,8},{16,20},{20,16},{24,28},{28,24},{1,5},{5... | collective-permute-start | bytes 786440 | tf_op jit(solution)/shard_map/ppermute | solution.py:83
  141.6 8.3 %collective-permute-start.32 = (bf16[8,32,512]{2,1,0:T(8,128)(2,1)S(1)}, bf16[8,32,512]{2,1,0:T(8,128)(2,1)S(1)}, u32[]{:S(2)}, u32[]{:S(2)}) collective-permute-start(bf16[8,32,512]{2,1,0:T(8,128)(2,1)S(1)} %shard_map.113.refs_9_), channel_id=1, source_target_pairs={{0,3},{1,2},{2,1},{3,0},{4,7},{5,6},{6,5},{7,4},{8,11},{9,10},{10,... | collective-permute-start | bytes 786440 | tf_op jit(solution)/shard_map/ppermute | solution.py:83
  147.4 24.4 %copy-start.7 = (bf16[32,128]{1,0:T(8,128)(2,1)S(1)}, bf16[32,128]{1,0:T(8,128)(2,1)}, u32[]{:S(2)}) copy-start(bf16[32,128]{1,0:T(8,128)(2,1)} %get-tuple-element.25) | copy-start | bytes 24580
  147.5 2.4 %collective-permute-start.35 = (bf16[1,8,32,512]{3,2,1,0:T(8,128)(2,1)S(1)}, bf16[1,8,32,512]{3,2,1,0:T(8,128)(2,1)S(1)}, u32[]{:S(2)}, u32[]{:S(2)}) collective-permute-start(bf16[1,8,32,512]{3,2,1,0:T(8,128)(2,1)S(1)} %get-tuple-element.44), channel_id=1, source_target_pairs={{0,4},{4,0},{8,12},{12,8},{16,20},{20,16},{24,28},{28,24},{1,5},{5... | collective-permute-start | bytes 786440 | tf_op jit(solution)/shard_map/ppermute | solution.py:83
  150.5 11.8 %collective-permute-start.36 = (bf16[8,32,512]{2,1,0:T(8,128)(2,1)S(1)}, bf16[8,32,512]{2,1,0:T(8,128)(2,1)S(1)}, u32[]{:S(2)}, u32[]{:S(2)}) collective-permute-start(bf16[8,32,512]{2,1,0:T(8,128)(2,1)S(1)} %shard_map.115), channel_id=1, source_target_pairs={{0,1},{1,0},{2,3},{3,2},{4,5},{5,4},{6,7},{7,6},{8,9},{9,8},{10,11... | collective-permute-start | bytes 786440 | tf_op jit(solution)/shard_map/ppermute | solution.py:83
